TPU v7x, 256 devices: a whole 4x4x8 slice. The times are simulated.
256 devices in a mesh: replica: 4 (over y_lo, core), fsdp: 64 (over z, y_hi, x).
Axes of the slice: x: 4, y: 4 (y_hi: 2, y_lo: 2; y = y_hi * 2 + y_lo), z: 8, core: 2. Of those that a mesh axis runs over, the one named last changes fastest.
Arguments:
- local_weights: bfloat16 [4, 8192, 8192], P('replica', 'fsdp'), may hold values from -6 to 6
- anchor: bfloat16 [8192, 8192], P('fsdp'), may hold values from -6 to 6
- momentum: float32 [8192, 8192], P('replica', 'fsdp'), may hold values from -4 to 4
Outputs:
- new_momentum: float32 [8192, 8192], P('replica', 'fsdp')
- new_anchor: bfloat16 [8192, 8192], P('fsdp')
- mixed: bfloat16 [4, 8192, 8192], P('replica', 'fsdp')
All inputs are finite; a program needn't handle non-finite values.
Results may differ from a plain program's by a relative error of at most 0.03.
Values may be sent and summed in bfloat16 or wider, within the bound.
No kernel may reach another device: no remote copies, remote signals or barrier semaphores. Data moves between devices by JAX's collectives and lax.ppermute only.
A program may use at most 64 MiB of HBM per device.

v0:
```python
import jax
import jax.numpy as jnp
from jax import lax
from jax.sharding import PartitionSpec as P

outer_rate = 0.7
outer_beta = 0.9
mix_weight = 0.5


def local(local_weights, anchor, momentum):
    anchor_wide = anchor.astype(jnp.float32)
    local_wide = local_weights[0].astype(jnp.float32)
    delta = (anchor_wide - local_wide).astype(jnp.bfloat16)
    delta_cols = lax.all_to_all(delta, "fsdp", split_axis=1, concat_axis=0, tiled=True)
    replicas = lax.axis_size("replica")
    total = lax.psum_scatter(
        delta_cols.astype(jnp.float32).astype(jnp.bfloat16),
        "replica",
        scatter_dimension=0,
        tiled=True,
    ).astype(jnp.float32)
    average = total / replicas
    new_momentum = outer_beta * momentum + average
    change = (outer_rate * (average + outer_beta * new_momentum)).astype(jnp.bfloat16)
    rows_all = lax.all_gather(change, "replica", axis=0, tiled=True)
    own_change = lax.all_to_all(rows_all, "fsdp", split_axis=0, concat_axis=1, tiled=True)
    global_new = anchor_wide - own_change.astype(jnp.float32)
    new_anchor = global_new.astype(jnp.bfloat16)
    mixed = (mix_weight * local_wide + (1.0 - mix_weight) * global_new).astype(jnp.bfloat16)
    return (new_momentum, new_anchor, mixed[None])


def solution(mesh):
    return jax.shard_map(
        local,
        mesh=mesh,
        in_specs=(P("replica", "fsdp", None), P("fsdp", None), P("replica", "fsdp")),
        out_specs=(P("replica", "fsdp"), P("fsdp", None), P("replica", "fsdp", None)),
        check_vma=False,
    )
```

profile of v0, /device:TPU:8, one launch (start us, length us, event | category | flops | bytes accessed | tf_op | source)
XLA Modules:
  0.0 235.9 jit_solution(16071346583465763247)
XLA Ops:
  7.2 0.0 reduce-scatter.2.cloned.1.call-start
  7.2 3.2 %copy.9 = bf16[1,128,8192]{1,2,0:T(8,128)(2,1)S(1)} copy(bf16[1,128,8192]{2,1,0:T(8,128)(2,1)} %param.3) | data formatting | bytes 4194304 | tf_op args[0]
  10.4 4.1 %copy.8 = bf16[128,8192]{0,1:T(8,128)(2,1)} copy(bf16[128,8192]{1,0:T(8,128)(2,1)} %param.4) | data formatting | bytes 4194304 | tf_op args[1]
  14.5 3.5 %fusion = bf16[128,8192]{0,1:T(8,128)(2,1)} fusion(bf16[128,8192]{0,1:T(8,128)(2,1)} %copy.8, bf16[1,128,8192]{1,2,0:T(8,128)(2,1)S(1)} %copy.9), kind=kLoop, calls=%fused_computation.3 | loop fusion | flops 4194304 | bytes 6291456 | tf_op jit(solution)/shard_map/convert_element_type | solution.py:14
  18.0 4.1 %copy.10 = bf16[128,64,128]{2,0,1:T(8,128)(2,1)} copy(bf16[128,64,128]{0,2,1:T(8,128)(2,1)} %bitcast.19) | data formatting | bytes 4194304 | tf_op jit(solution)/shard_map/all_to_all | solution.py:15
  22.0 64.9 %all_to_all.32 = bf16[128,64,128]{2,0,1:T(8,128)(2,1)} all-to-all(bf16[128,64,128]{2,0,1:T(8,128)(2,1)} %copy.10), channel_id=1, replica_groups=mesh['replica'=4,'fsdp'=64] {'fsdp'}, dimensions={1} | all-to-all | bytes 4194304 | tf_op jit(solution)/shard_map/all_to_all | solution.py:15
  87.0 0.0 copy-start.1
  87.0 0.0 reduce-scatter.2.cloned.1.call-update
  87.0 0.0 all-gather.2.cloned.1.call-start
  87.0 26.1 %reduce-scatter.2.cloned.1.call-done = bf16[2048,128]{1,0:T(8,128)(2,1)} async-done(((bf16[8192,128]{1,0:T(8,128)(2,1)}), bf16[2048,128]{1,0:T(8,128)(2,1)}) %reduce-scatter.2.cloned.1.call-update) | async-done | bytes 524304 | tf_op jit(solution)/shard_map/reduce_scatter | solution.py:17
  113.1 0.0 copy-done.1
  113.1 2.5 %multiply_convert_fusion = (bf16[2048,128]{1,0:T(8,128)(2,1)}, f32[2048,128]{1,0:T(8,128)}) fusion(bf16[2048,128]{1,0:T(8,128)(2,1)} %reduce-scatter.2.cloned.1.call-done, f32[2048,128]{1,0:T(8,128)S(1)} %copy-done.1), kind=kLoop, calls=%fused_computation.7 | loop fusion | flops 2097152 | bytes 3145728 | tf_op jit(solution)/shard_map/convert_element_type | solution.py:25
  115.6 0.0 all-gather.2.cloned.1.call-update
  115.6 32.8 %all-gather.2.cloned.1.call-done = bf16[8192,128]{1,0:T(8,128)(2,1)} async-done(((bf16[2048,128]{1,0:T(8,128)(2,1)}), bf16[8192,128]{1,0:T(8,128)(2,1)}) %all-gather.2.cloned.1.call-update) | async-done | bytes 2097168 | tf_op jit(solution)/shard_map/all_gather | solution.py:26
  148.4 64.2 %all_to_all.33 = bf16[64,128,128]{2,1,0:T(8,128)(2,1)} all-to-all(bf16[64,128,128]{2,1,0:T(8,128)(2,1)} %bitcast.21), channel_id=1, replica_groups=mesh['replica'=4,'fsdp'=64] {'fsdp'}, dimensions={0} | all-to-all | bytes 4194304 | tf_op jit(solution)/shard_map/all_to_all | solution.py:27
  212.6 4.1 %copy.11 = bf16[64,128,128]{1,2,0:T(8,128)(2,1)} copy(bf16[64,128,128]{2,1,0:T(8,128)(2,1)} %all_to_all.33) | data formatting | bytes 4194304 | tf_op jit(solution)/shard_map/all_to_all | solution.py:27
  216.6 5.3 %fusion.2 = (bf16[128,8192]{0,1:T(8,128)(2,1)}, bf16[128,8192]{0,1:T(8,128)(2,1)}) fusion(bf16[128,8192]{0,1:T(8,128)(2,1)} %copy.8, bf16[64,128,128]{1,2,0:T(8,128)(2,1)} %copy.11, bf16[1,128,8192]{1,2,0:T(8,128)(2,1)S(1)} %copy.9), kind=kLoop, calls=%fused_computation.5 | loop fusion | flops 8388608 | bytes 10485760 | tf_op jit(solution)/shard_map/convert_element_type | solution.py:30
  221.9 0.0 copy-start
  221.9 4.2 %copy.13 = bf16[1,128,8192]{2,1,0:T(8,128)(2,1)} copy(bf16[1,128,8192]{1,2,0:T(8,128)(2,1)} %bitcast.18) | data formatting | bytes 4194304
  226.1 0.0 copy-done
  226.1 2.9 %copy.12 = bf16[128,8192]{1,0:T(8,128)(2,1)} copy(bf16[128,8192]{0,1:T(8,128)(2,1)S(1)} %copy-done) | data formatting | bytes 4194304
Async XLA Ops:
  7.2 106.0 %reduce-scatter.2.cloned.1.call-start = ((), (), s32[]{:S(2)}) async-start(), calls=%async_computation.3 | async-start | bytes 2621440 | tf_op jit(solution)/shard_map/reduce_scatter | solution.py:17
  87.0 26.2 %copy-start.1 = (f32[2048,128]{1,0:T(8,128)S(1)}, f32[2048,128]{1,0:T(8,128)}, u32[]{:S(2)}) copy-start(f32[2048,128]{1,0:T(8,128)} %param.5) | copy-start | bytes 3145732
  87.0 61.4 %all-gather.2.cloned.1.call-start = ((), (), s32[]{:S(2)}) async-start(), calls=%async_computation.4 | async-start | bytes 2621440 | tf_op jit(solution)/shard_map/all_gather | solution.py:26
  221.9 4.2 %copy-start = (bf16[128,8192]{0,1:T(8,128)(2,1)S(1)}, bf16[128,8192]{0,1:T(8,128)(2,1)}, u32[]{:S(2)}) copy-start(bf16[128,8192]{0,1:T(8,128)(2,1)} %get-tuple-element.9) | copy-start | bytes 6291460
Sparse Core Ops, SparseCore 0:
  87.1 25.9 reduce-scatter.1
  115.7 32.6 all-gather.1
where the time goes:
time: 238 us; the launch traced here: 236 us
  blocking collectives  129 us (54%)
  waiting for transfers between devices  58.9 us (25%)
  local copies, waits for them, and re-layouts  22.5 us (9%)
  between operations  14 us (6%)
  other arithmetic  11.2 us (5%)
    all_to_all x1, blocking collectives, local(): lax.all_to_all(delta, 'fsdp', split_axis=1, concat_axis=0, tiled=True)  64.9 us
    all_to_all x1, blocking collectives, local(): lax.all_to_all(rows_all, 'fsdp', split_axis=0, concat_axis=1, tiled=True)  64.2 us
    all_gather x1, waiting for transfers between devices, local(): rows_all = lax.all_gather(change, 'replica', axis=0, tiled=True)  32.8 us
    reduce_scatter x1, waiting for transfers between devices, local(): lax.psum_scatter(delta_cols.astype(jnp.float32).astype(jnp.bfloat16), 're...  26.1 us
    unnamed x8, local copies, waits for them, and re-layouts  14.4 us
    convert_element_type x1, other arithmetic, local(): (mix_weight * local_wide + (1.0 - mix_weight) * global_new).astype(jnp.bf...  5.28 us
  transfers between devices with their start and end apart: 2, of which 2 were waited for; matrix products, arithmetic and copies ran while one was open for 0% of the time, Pallas kernels for 0%

commit v1 on v0

v1 whole, which is shorter than its diff:
```python
import functools

import jax
import jax.numpy as jnp
from jax import lax
from jax.experimental import pallas as pl
from jax.experimental.pallas import tpu as pltpu
from jax.sharding import PartitionSpec as P

outer_rate = 0.7
outer_beta = 0.9
mix_weight = 0.5

BF = jnp.bfloat16
F32 = jnp.float32


def seg_of(r):
    return 2 * (r % 2) + r // 2


def params(mib=48):
    return pltpu.CompilerParams(vmem_limit_bytes=mib * 2**20)


def cost(n):
    return pl.CostEstimate(flops=n // 2, bytes_accessed=n, transcendentals=0)


def swap(x, k):
    return lax.ppermute(x, "replica", [(i, i ^ k) for i in range(4)])


def split_momentum(r, momentum):
    def body(r_ref, m_ref, *outs):
        for k in range(4):
            seg = seg_of(jnp.bitwise_xor(r_ref[0], k))
            for j in range(16):
                at = pl.multiple_of(j * 128 + seg * 32, 32)
                outs[k][j] = m_ref[pl.ds(at, 32), :].astype(BF)

    return pl.pallas_call(
        body,
        out_shape=[jax.ShapeDtypeStruct((16, 32, 128), BF)] * 4,
        in_specs=[pl.BlockSpec(memory_space=pltpu.SMEM), pl.BlockSpec(memory_space=pltpu.VMEM)],
        out_specs=[pl.BlockSpec(memory_space=pltpu.VMEM)] * 4,
        compiler_params=params(),
        cost_estimate=cost(3 << 19),
        name="split_momentum",
    )(r, momentum)


def in_order(r, pieces):
    def body(r_ref, *refs):
        for k in range(4):
            refs[4][jnp.bitwise_xor(r_ref[0], k)] = refs[k][...]

    return pl.pallas_call(
        body,
        out_shape=jax.ShapeDtypeStruct((4, 16, 32, 128), BF),
        in_specs=[pl.BlockSpec(memory_space=pltpu.SMEM)] + [pl.BlockSpec(memory_space=pltpu.VMEM)] * 4,
        out_specs=pl.BlockSpec(memory_space=pltpu.VMEM),
        compiler_params=params(),
        cost_estimate=cost(1 << 20),
        name="in_order",
    )(r, *pieces)


def out_of_order(r, whole):
    def body(r_ref, x_ref, *outs):
        for k in range(4):
            outs[k][...] = x_ref[jnp.bitwise_xor(r_ref[0], k)]

    return pl.pallas_call(
        body,
        out_shape=[jax.ShapeDtypeStruct((16, 32, 128), BF)] * 4,
        in_specs=[pl.BlockSpec(memory_space=pltpu.SMEM), pl.BlockSpec(memory_space=pltpu.VMEM)],
        out_specs=[pl.BlockSpec(memory_space=pltpu.VMEM)] * 4,
        compiler_params=params(),
        cost_estimate=cost(1 << 20),
        name="out_of_order",
    )(r, whole)


WIDTH = 2048


def spec(row):
    return pl.BlockSpec((32, WIDTH), lambda i, s: (row(s[0]), i))


def partial_for_other(r, local, theirs, anchor):
    def body(s_ref, l_ref, t_ref, a_ref, o_ref):
        a = a_ref[...].astype(F32)
        o_ref[...] = ((a - l_ref[...].astype(F32)) + (a - t_ref[...].astype(F32))).astype(BF)

    other = lambda r: seg_of(jnp.bitwise_xor(r, 2))
    return pl.pallas_call(
        body,
        out_shape=jax.ShapeDtypeStruct((32, 8192), BF),
        grid_spec=pltpu.PrefetchScalarGridSpec(
            num_scalar_prefetch=1,
            grid=(8192 // WIDTH,),
            in_specs=[spec(other), spec(lambda r: 1 - r // 2), spec(other)],
            out_specs=pl.BlockSpec((32, WIDTH), lambda i, s: (0, i)),
        ),
        compiler_params=params(),
        cost_estimate=cost(1 << 21),
        name="partial_for_other",
    )(r, local, theirs, anchor)


def average_rows(r, local, theirs, anchor, partial):
    def body(s_ref, l_ref, t_ref, a_ref, p_ref, avg_ref, cut_ref):
        a = a_ref[...].astype(F32)
        own = (a - l_ref[...].astype(F32)) + (a - t_ref[...].astype(F32))
        avg = (own + p_ref[...].astype(F32)) * 0.25
        avg_ref[...] = avg
        narrow = avg.astype(BF)
        for i in range(WIDTH // 128):
            cut_ref[i] = narrow[:, i * 128 : (i + 1) * 128]

    return pl.pallas_call(
        body,
        out_shape=[
            jax.ShapeDtypeStruct((32, 8192), F32),
            jax.ShapeDtypeStruct((64, 32, 128), BF),
        ],
        grid_spec=pltpu.PrefetchScalarGridSpec(
            num_scalar_prefetch=1,
            grid=(8192 // WIDTH,),
            in_specs=[
                spec(seg_of),
                spec(lambda r: r // 2),
                spec(seg_of),
                pl.BlockSpec((32, WIDTH), lambda i, s: (0, i)),
            ],
            out_specs=[
                pl.BlockSpec((32, WIDTH), lambda i, s: (0, i)),
                pl.BlockSpec((WIDTH // 128, 32, 128), lambda i, s: (i, 0, 0)),
            ],
        ),
        compiler_params=params(),
        cost_estimate=cost(4 << 20),
        name="average_rows",
    )(r, local, theirs, anchor, partial)


def change_rows(avg, m):
    def body(avg_ref, m_ref, o_ref):
        for i in range(WIDTH // 128):
            at = slice(i * 128, (i + 1) * 128)
            average = avg_ref[:, at]
            momentum = outer_beta * m_ref[i].astype(F32) + average
            o_ref[:, at] = (outer_rate * (average + outer_beta * momentum)).astype(BF)

    return pl.pallas_call(
        body,
        out_shape=jax.ShapeDtypeStruct((32, 8192), BF),
        grid=(8192 // WIDTH,),
        in_specs=[
            pl.BlockSpec((32, WIDTH), lambda i: (0, i)),
            pl.BlockSpec((WIDTH // 128, 32, 128), lambda i: (i, 0, 0)),
        ],
        out_specs=pl.BlockSpec((32, WIDTH), lambda i: (0, i)),
        compiler_params=params(),
        cost_estimate=cost(2 << 20),
        name="change_rows",
    )(avg, m)


def new_momentum_of(r, momentum, pieces):
    def body(r_ref, m_ref, *refs):
        for k in range(4):
            seg = seg_of(jnp.bitwise_xor(r_ref[0], k))
            for j in range(16):
                at = pl.ds(pl.multiple_of(j * 128 + seg * 32, 32), 32)
                refs[4][at, :] = outer_beta * m_ref[at, :] + refs[k][j].astype(F32)

    return pl.pallas_call(
        body,
        out_shape=jax.ShapeDtypeStruct((2048, 128), F32),
        in_specs=[pl.BlockSpec(memory_space=pltpu.SMEM)] + [pl.BlockSpec(memory_space=pltpu.VMEM)] * 5,
        out_specs=pl.BlockSpec(memory_space=pltpu.VMEM),
        compiler_params=params(),
        cost_estimate=cost(5 << 19),
        name="new_momentum_of",
    )(r, momentum, *pieces)


def outputs_of(r, local, anchor, changes):
    width = 1024

    def body(r_ref, l_ref, a_ref, *refs):
        new_ref, mixed_ref = refs[4:]
        for k in range(4):
            seg = seg_of(jnp.bitwise_xor(r_ref[0], k))
            at = pl.ds(pl.multiple_of(seg * 32, 32), 32)
            global_new = a_ref[at, :].astype(F32) - refs[k][...].astype(F32)
            new_ref[at, :] = global_new.astype(BF)
            mixed_ref[at, :] = (
                mix_weight * l_ref[at, :].astype(F32) + (1.0 - mix_weight) * global_new
            ).astype(BF)

    tall = pl.BlockSpec((128, width), lambda i, s: (0, i))
    flat = pl.BlockSpec((32, width), lambda i, s: (0, i))
    return pl.pallas_call(
        body,
        out_shape=[jax.ShapeDtypeStruct((128, 8192), BF)] * 2,
        grid_spec=pltpu.PrefetchScalarGridSpec(
            num_scalar_prefetch=1,
            grid=(8192 // width,),
            in_specs=[tall, tall] + [flat] * 4,
            out_specs=[tall, tall],
        ),
        compiler_params=params(),
        cost_estimate=cost(10 << 20),
        name="outputs_of",
    )(r, local, anchor, *changes)


def local(local_weights, anchor, momentum):
    own = local_weights[0]
    me = lax.axis_index("replica")
    r = me[None].astype(jnp.int32)
    core = me % 2

    theirs = swap(lax.dynamic_slice_in_dim(own, (1 - core) * 64, 64, 0), 1)

    pieces = split_momentum(r, momentum)
    pieces = [pieces[0]] + [swap(pieces[k], k) for k in (1, 2, 3)]
    by_row = in_order(r, pieces).reshape(64, 32, 128)
    m_rows = lax.all_to_all(by_row, "fsdp", 0, 0, tiled=True)

    partial = swap(partial_for_other(r, own, theirs, anchor), 2)
    avg, cut = average_rows(r, own, theirs, anchor, partial)

    cut = lax.all_to_all(cut, "fsdp", 0, 0, tiled=True).reshape(4, 16, 32, 128)
    cut = out_of_order(r, cut)
    cut = [cut[0]] + [swap(cut[k], k) for k in (1, 2, 3)]
    new_momentum = new_momentum_of(r, momentum, cut)

    change = change_rows(avg, m_rows)
    change2 = swap(change, 2)
    change1 = swap(change, 1)
    change3 = swap(change2, 1)
    new_anchor, mixed = outputs_of(r, own, anchor, [change, change1, change2, change3])
    return new_momentum, new_anchor, mixed[None]


def solution(mesh):
    return jax.shard_map(
        local,
        mesh=mesh,
        in_specs=(P("replica", "fsdp", None), P("fsdp", None), P("replica", "fsdp")),
        out_specs=(P("replica", "fsdp"), P("fsdp", None), P("replica", "fsdp", None)),
        check_vma=False,
    )
```

time: 238 us -> 100 us (0.42)
  the two profiles are of different devices: /device:TPU:8 before, /device:TPU:1 now
where the time goes in v1:
time: 100 us; the launch traced here: 99.3 us
  waiting for transfers between devices  38.6 us (39%)
  starting transfers between devices  35.1 us (35%)
  Pallas kernels  17.1 us (17%)
  local copies, waits for them, and re-layouts  7.71 us (8%)
    ppermute x11, waiting for transfers between devices, swap(): return lax.ppermute(x, 'replica', [(i, i ^ k) for i in range(4)])  38.6 us
    all_to_all x1, starting transfers between devices, local(): m_rows = lax.all_to_all(by_row, 'fsdp', 0, 0, tiled=True)  12.8 us
    all_to_all x1, starting transfers between devices, local(): cut = lax.all_to_all(cut, 'fsdp', 0, 0, tiled=True).reshape(4, 16, 32, 128)  11.9 us
    ppermute x11, starting transfers between devices, swap(): return lax.ppermute(x, 'replica', [(i, i ^ k) for i in range(4)])  10.4 us
    pallas_call x1, Pallas kernels, outputs_of(): pl.pallas_call(body, out_shape=[jax.ShapeDtypeStruct((128, 8192), BF)] *...  6.9 us
    unnamed x14, local copies, waits for them, and re-layouts  5.36 us
    pallas_call x1, Pallas kernels, change_rows(): pl.pallas_call(body, out_shape=jax.ShapeDtypeStruct((32, 8192), BF), grid...  3.29 us
    pallas_call x1, Pallas kernels, average_rows(): pl.pallas_call(body, out_shape=[jax.ShapeDtypeStruct((32, 8192), F32), ja...  2.46 us
  transfers between devices with their start and end apart: 13, of which 5 were waited for; matrix products, arithmetic and copies ran while one was open for 0% of the time, Pallas kernels for 16%

profile of v1, /device:TPU:1, one launch (start us, length us, event | category | flops | bytes accessed | tf_op | source)
XLA Modules:
  0.0 99.3 jit_solution(16923099805108165630)
XLA Ops:
  0.6 0.0 copy-start.2
  0.7 2.4 %dynamic-slice_bitcast_fusion = bf16[64,8192]{1,0:T(8,128)(2,1)} fusion(bf16[1,128,8192]{2,1,0:T(8,128)(2,1)} %param.3, s32[]{:T(128)S(6)} %select_n.11), kind=kLoop, calls=%fused_computation | loop fusion | bytes 2097156 | tf_op jit(solution)/shard_map/dynamic_slice | solution.py:228
  3.0 0.0 copy-start
  3.0 3.2 %collective-permute-start = (bf16[64,8192]{1,0:T(8,128)(2,1)}, bf16[64,8192]{1,0:T(8,128)(2,1)}, u32[]{:S(2)}, u32[]{:S(2)}) collective-permute-start(bf16[64,8192]{1,0:T(8,128)(2,1)} %dynamic-slice_bitcast_fusion), channel_id=1, source_target_pairs={{0,64},{64,0},{128,192},{192,128},{1,65},{65,1},{129,193},{193,129... | collective-permute-start | bytes 3145736 | tf_op jit(solution)/shard_map/ppermute | solution.py:31
  6.2 0.0 copy-done.2
  6.3 0.1 split_momentum.1
  6.3 0.1 collective-permute-start.5
  6.4 0.1 collective-permute-start.6
  6.5 2.0 %collective-permute-start.7 = (bf16[16,32,128]{2,1,0:T(8,128)(2,1)S(1)}, bf16[16,32,128]{2,1,0:T(8,128)(2,1)S(1)}, u32[]{:S(2)}, u32[]{:S(2)}) collective-permute-start(bf16[16,32,128]{2,1,0:T(8,128)(2,1)S(1)} %get-tuple-element.24), channel_id=1, source_target_pairs={{0,192},{64,128},{128,64},{192,0},{1,193},{65,129},{129,65},{193,1... | collective-permute-start | bytes 393224 | tf_op jit(solution)/shard_map/ppermute | solution.py:31
  8.5 0.2 collective-permute-done.5.refs_1_
  8.7 2.4 %collective-permute-done.6.refs_2_ = bf16[16,32,128]{2,1,0:T(8,128)(2,1)S(1)} collective-permute-done((bf16[16,32,128]{2,1,0:T(8,128)(2,1)S(1)}, bf16[16,32,128]{2,1,0:T(8,128)(2,1)S(1)}, u32[]{:S(2)}, u32[]{:S(2)}) %collective-permute-start.6) | collective-permute-done | bytes 131104 | tf_op jit(solution)/shard_map/ppermute | solution.py:31
  11.2 3.4 %collective-permute-done.7.refs_3_ = bf16[16,32,128]{2,1,0:T(8,128)(2,1)S(1)} collective-permute-done((bf16[16,32,128]{2,1,0:T(8,128)(2,1)S(1)}, bf16[16,32,128]{2,1,0:T(8,128)(2,1)S(1)}, u32[]{:S(2)}, u32[]{:S(2)}) %collective-permute-start.7) | collective-permute-done | bytes 131104 | tf_op jit(solution)/shard_map/ppermute | solution.py:31
  14.6 0.0 copy-start.3
  14.6 0.8 copy-done.3
  15.4 12.8 %all-to-all-start.1 = ((bf16[64,32,128]{2,1,0:T(8,128)(2,1)}), bf16[64,32,128]{2,1,0:T(8,128)(2,1)}, u32[]{:S(2)}, u32[]{:S(2)}) async-start(bf16[64,32,128]{2,1,0:T(8,128)(2,1)} %bitcast.10), calls=%async_computation.1 | async-start | bytes 1048576 | tf_op jit(solution)/shard_map/all_to_all | solution.py:233
  28.2 0.0 collective-permute-done.t_ref
  28.2 0.0 copy-done
  28.2 0.0 copy-start.1
  28.2 1.6 %copy-done.1 = bf16[128,8192]{1,0:T(8,128)(2,1)S(1)} copy-done((bf16[128,8192]{1,0:T(8,128)(2,1)S(1)}, bf16[128,8192]{1,0:T(8,128)(2,1)}, u32[]{:S(2)}) %copy-start.1) | copy-done | bytes 2097176
  29.8 2.2 %partial_for_other.1 = bf16[32,8192]{1,0:T(8,128)(2,1)S(1)} custom-call(s32[1]{0:T(128)} %bitcast.s_ref.r_ref, bf16[128,8192]{1,0:T(8,128)(2,1)S(1)} %bitcast.7, bf16[64,8192]{1,0:T(8,128)(2,1)} %collective-permute-done.t_ref, bf16[128,8192]{1,0:T(8,128)(2,1)S(1)} %copy-done.1), custom_call_target="tpu_custom_call" | custom-call | flops 1048576 | bytes 2097152 | tf_op jit(solution)/shard_map/partial_for_other/pallas_call | solution.py:98
  32.0 0.5 collective-permute-start.1
  32.5 16.8 %collective-permute-done.1.p_ref = bf16[32,8192]{1,0:T(8,128)(2,1)S(1)} collective-permute-done((bf16[32,8192]{1,0:T(8,128)(2,1)S(1)}, bf16[32,8192]{1,0:T(8,128)(2,1)S(1)}, u32[]{:S(2)}, u32[]{:S(2)}) %collective-permute-start.1) | collective-permute-done | bytes 524320 | tf_op jit(solution)/shard_map/ppermute | solution.py:31
  49.2 2.5 %average_rows.1 = (f32[32,8192]{1,0:T(8,128)S(1)}, bf16[64,32,128]{2,1,0:T(8,128)(2,1)S(1)}) custom-call(s32[1]{0:T(128)} %bitcast.s_ref.r_ref, bf16[128,8192]{1,0:T(8,128)(2,1)S(1)} %bitcast.8, bf16[64,8192]{1,0:T(8,128)(2,1)} %collective-permute-done.t_ref, bf16[128,8192]{1,0:T(8,128)(2,1)} %a_ref.5, bf16[32,8192]{1,0:T(8,128)(2,1)S(1)} %collective-permute-done.1.p_ref), custom_call_target="tpu_custom_call" | custom-call | flops 2097152 | bytes 4194304 | tf_op jit(solution)/shard_map/average_rows/pallas_call | solution.py:123
  51.7 0.0 copy-start.4
  51.7 1.0 copy-done.4
  52.7 0.0 copy-start.6
  52.7 0.8 copy-done.6
  53.5 0.0 all-to-all-done.1.m_ref
  53.5 11.9 %all-to-all-start = ((bf16[64,32,128]{2,1,0:T(8,128)(2,1)}), bf16[64,32,128]{2,1,0:T(8,128)(2,1)}, u32[]{:S(2)}, u32[]{:S(2)}) async-start(bf16[64,32,128]{2,1,0:T(8,128)(2,1)} %copy-done.6), calls=%async_computation | async-start | bytes 1048576 | tf_op jit(solution)/shard_map/all_to_all | solution.py:238
  65.4 0.0 copy-start.5
  65.4 1.2 %copy-done.5 = f32[32,8192]{1,0:T(8,128)S(1)} copy-done((f32[32,8192]{1,0:T(8,128)S(1)}, f32[32,8192]{1,0:T(8,128)}, u32[]{:S(2)}) %copy-start.5) | copy-done | bytes 1048600
  66.6 3.3 %change_rows.1.refs_0_ = bf16[32,8192]{1,0:T(8,128)(2,1)} custom-call(f32[32,8192]{1,0:T(8,128)S(1)} %copy-done.5, bf16[64,32,128]{2,1,0:T(8,128)(2,1)} %all-to-all-done.1.m_ref), custom_call_target="tpu_custom_call" | custom-call | flops 1048576 | bytes 2097152 | tf_op jit(solution)/shard_map/change_rows/pallas_call | solution.py:157
  69.9 0.0 collective-permute-start.9
  69.9 1.2 %collective-permute-start.8 = (bf16[32,8192]{1,0:T(8,128)(2,1)}, bf16[32,8192]{1,0:T(8,128)(2,1)}, u32[]{:S(2)}, u32[]{:S(2)}) collective-permute-start(bf16[32,8192]{1,0:T(8,128)(2,1)} %change_rows.1.refs_0_), channel_id=1, source_target_pairs={{0,64},{64,0},{128,192},{192,128},{1,65},{65,1},{129,193},{193,129... | collective-permute-start | bytes 1572872 | tf_op jit(solution)/shard_map/ppermute | solution.py:31
  71.1 15.8 %collective-permute-done.9.refs_2_ = bf16[32,8192]{1,0:T(8,128)(2,1)} collective-permute-done((bf16[32,8192]{1,0:T(8,128)(2,1)}, bf16[32,8192]{1,0:T(8,128)(2,1)}, u32[]{:S(2)}, u32[]{:S(2)}) %collective-permute-start.9) | collective-permute-done | bytes 524320 | tf_op jit(solution)/shard_map/ppermute | solution.py:31
  86.9 1.0 %collective-permute-start.10 = (bf16[32,8192]{1,0:T(8,128)(2,1)}, bf16[32,8192]{1,0:T(8,128)(2,1)}, u32[]{:S(2)}, u32[]{:S(2)}) collective-permute-start(bf16[32,8192]{1,0:T(8,128)(2,1)} %collective-permute-done.9.refs_2_), channel_id=1, source_target_pairs={{0,64},{64,0},{128,192},{192,128},{1,65},{65,1},{129,193},{193,129... | collective-permute-start | bytes 1572872 | tf_op jit(solution)/shard_map/ppermute | solution.py:31
  88.0 0.0 all-to-all-done
  88.0 1.1 %out_of_order.1 = (bf16[16,32,128]{2,1,0:T(8,128)(2,1)S(1)}, bf16[16,32,128]{2,1,0:T(8,128)(2,1)S(1)}, bf16[16,32,128]{2,1,0:T(8,128)(2,1)S(1)}, bf16[16,32,128]{2,1,0:T(8,128)(2,1)S(1)}) custom-call(s32[1]{0:T(128)} %bitcast.s_ref.r_ref, bf16[4,16,32,128]{3,2,1,0:T(8,128)(2,1)} %bitcast.3.x_ref), custom_call_target="tpu_custom_call" | custom-call | flops 524288 | bytes 1048576 | tf_op jit(solution)/shard_map/out_of_order/pallas_call | solution.py:74
  89.0 0.1 collective-permute-start.2
  89.1 0.5 collective-permute-start.3
  89.7 1.6 %collective-permute-start.4 = (bf16[16,32,128]{2,1,0:T(8,128)(2,1)S(1)}, bf16[16,32,128]{2,1,0:T(8,128)(2,1)S(1)}, u32[]{:S(2)}, u32[]{:S(2)}) collective-permute-start(bf16[16,32,128]{2,1,0:T(8,128)(2,1)S(1)} %get-tuple-element.19), channel_id=1, source_target_pairs={{0,192},{64,128},{128,64},{192,0},{1,193},{65,129},{129,65},{193,1... | collective-permute-start | bytes 393224 | tf_op jit(solution)/shard_map/ppermute | solution.py:31
  91.3 0.0 collective-permute-done.8.refs_1_
  91.3 0.0 collective-permute-done.10.refs_3_
  91.3 6.9 %outputs_of.1 = (bf16[128,8192]{1,0:T(8,128)(2,1)}, bf16[128,8192]{1,0:T(8,128)(2,1)}) custom-call(s32[1]{0:T(128)} %bitcast.s_ref.r_ref, bf16[128,8192]{1,0:T(8,128)(2,1)S(1)} %bitcast.9, bf16[128,8192]{1,0:T(8,128)(2,1)} %a_ref.5, bf16[32,8192]{1,0:T(8,128)(2,1)} %change_rows.1.refs_0_, bf16[32,8192]{1,0:T(8,128)(2,1)} %collective-permute-done.8.refs_1_, ...), custom_call_target="tpu_custom_call" | custom-call | flops 5242880 | bytes 10485760 | tf_op jit(solution)/shard_map/outputs_of/pallas_call | solution.py:207
  98.2 0.0 collective-permute-done.2.refs_1_
  98.2 0.0 collective-permute-done.3.refs_2_
  98.2 0.0 collective-permute-done.4.refs_3_
  98.2 1.1 %new_momentum_of.1 = f32[2048,128]{1,0:T(8,128)} custom-call(s32[1]{0:T(128)} %bitcast.s_ref.r_ref, f32[2048,128]{1,0:T(8,128)S(1)} %copy-done.2, bf16[16,32,128]{2,1,0:T(8,128)(2,1)S(1)} %get-tuple-element.16.refs_0_, bf16[16,32,128]{2,1,0:T(8,128)(2,1)S(1)} %collective-permute-done.2.refs_1_, bf16[16,32,128]{2,1,0:T(8,128)(2,1)S(1)} %collective-permute-done.3.refs_2_, ...), custom_call_target="tpu_custom_call" | custom-call | flops 1310720 | bytes 2621440 | tf_op jit(solution)/shard_map/new_momentum_of/pallas_call | solution.py:180
  (1 shorter events, 0.0 us)
Async XLA Ops:
  0.6 5.6 %copy-start.2 = (f32[2048,128]{1,0:T(8,128)S(1)}, f32[2048,128]{1,0:T(8,128)}, u32[]{:S(2)}) copy-start(f32[2048,128]{1,0:T(8,128)} %m_ref.3) | copy-start | bytes 3145732
  3.0 25.2 %copy-start = (bf16[1,128,8192]{2,1,0:T(8,128)(2,1)S(1)}, bf16[1,128,8192]{2,1,0:T(8,128)(2,1)}, u32[]{:S(2)}) copy-start(bf16[1,128,8192]{2,1,0:T(8,128)(2,1)} %param.3) | copy-start | bytes 6291460
  3.0 25.2 %collective-permute-start = (bf16[64,8192]{1,0:T(8,128)(2,1)}, bf16[64,8192]{1,0:T(8,128)(2,1)}, u32[]{:S(2)}, u32[]{:S(2)}) collective-permute-start(bf16[64,8192]{1,0:T(8,128)(2,1)} %dynamic-slice_bitcast_fusion), channel_id=1, source_target_pairs={{0,64},{64,0},{128,192},{192,128},{1,65},{65,1},{129,193},{193,129... | collective-permute-start | bytes 3145736 | tf_op jit(solution)/shard_map/ppermute | solution.py:31
  6.3 2.4 %collective-permute-start.5 = (bf16[16,32,128]{2,1,0:T(8,128)(2,1)S(1)}, bf16[16,32,128]{2,1,0:T(8,128)(2,1)S(1)}, u32[]{:S(2)}, u32[]{:S(2)}) collective-permute-start(bf16[16,32,128]{2,1,0:T(8,128)(2,1)S(1)} %get-tuple-element.22), channel_id=1, source_target_pairs={{0,64},{64,0},{128,192},{192,128},{1,65},{65,1},{129,193},{193,129... | collective-permute-start | bytes 393224 | tf_op jit(solution)/shard_map/ppermute | solution.py:31
  6.4 4.7 %collective-permute-start.6 = (bf16[16,32,128]{2,1,0:T(8,128)(2,1)S(1)}, bf16[16,32,128]{2,1,0:T(8,128)(2,1)S(1)}, u32[]{:S(2)}, u32[]{:S(2)}) collective-permute-start(bf16[16,32,128]{2,1,0:T(8,128)(2,1)S(1)} %get-tuple-element.23), channel_id=1, source_target_pairs={{0,128},{64,192},{128,0},{192,64},{1,129},{65,193},{129,1},{193,65... | collective-permute-start | bytes 393224 | tf_op jit(solution)/shard_map/ppermute | solution.py:31
  6.5 8.0 %collective-permute-start.7 = (bf16[16,32,128]{2,1,0:T(8,128)(2,1)S(1)}, bf16[16,32,128]{2,1,0:T(8,128)(2,1)S(1)}, u32[]{:S(2)}, u32[]{:S(2)}) collective-permute-start(bf16[16,32,128]{2,1,0:T(8,128)(2,1)S(1)} %get-tuple-element.24), channel_id=1, source_target_pairs={{0,192},{64,128},{128,64},{192,0},{1,193},{65,129},{129,65},{193,1... | collective-permute-start | bytes 393224 | tf_op jit(solution)/shard_map/ppermute | solution.py:31
  14.6 0.8 copy-start.3
  15.4 38.1 %all-to-all-start.1 = ((bf16[64,32,128]{2,1,0:T(8,128)(2,1)}), bf16[64,32,128]{2,1,0:T(8,128)(2,1)}, u32[]{:S(2)}, u32[]{:S(2)}) async-start(bf16[64,32,128]{2,1,0:T(8,128)(2,1)} %bitcast.10), calls=%async_computation.1 | async-start | bytes 1048576 | tf_op jit(solution)/shard_map/all_to_all | solution.py:233
  28.2 1.6 %copy-start.1 = (bf16[128,8192]{1,0:T(8,128)(2,1)S(1)}, bf16[128,8192]{1,0:T(8,128)(2,1)}, u32[]{:S(2)}) copy-start(bf16[128,8192]{1,0:T(8,128)(2,1)} %a_ref.5) | copy-start | bytes 6291460
  32.0 17.2 %collective-permute-start.1 = (bf16[32,8192]{1,0:T(8,128)(2,1)S(1)}, bf16[32,8192]{1,0:T(8,128)(2,1)S(1)}, u32[]{:S(2)}, u32[]{:S(2)}) collective-permute-start(bf16[32,8192]{1,0:T(8,128)(2,1)S(1)} %partial_for_other.1), channel_id=1, source_target_pairs={{0,128},{64,192},{128,0},{192,64},{1,129},{65,193},{129,1},{193,65... | collective-permute-start | bytes 1572872 | tf_op jit(solution)/shard_map/ppermute | solution.py:31
  51.7 1.0 copy-start.4
  52.7 0.8 copy-start.6
  53.5 34.5 %all-to-all-start = ((bf16[64,32,128]{2,1,0:T(8,128)(2,1)}), bf16[64,32,128]{2,1,0:T(8,128)(2,1)}, u32[]{:S(2)}, u32[]{:S(2)}) async-start(bf16[64,32,128]{2,1,0:T(8,128)(2,1)} %copy-done.6), calls=%async_computation | async-start | bytes 1048576 | tf_op jit(solution)/shard_map/all_to_all | solution.py:238
  65.4 1.2 %copy-start.5 = (f32[32,8192]{1,0:T(8,128)S(1)}, f32[32,8192]{1,0:T(8,128)}, u32[]{:S(2)}) copy-start(f32[32,8192]{1,0:T(8,128)} %copy-done.4) | copy-start | bytes 3145732
  69.9 17.0 %collective-permute-start.9 = (bf16[32,8192]{1,0:T(8,128)(2,1)}, bf16[32,8192]{1,0:T(8,128)(2,1)}, u32[]{:S(2)}, u32[]{:S(2)}) collective-permute-start(bf16[32,8192]{1,0:T(8,128)(2,1)} %change_rows.1.refs_0_), channel_id=1, source_target_pairs={{0,128},{64,192},{128,0},{192,64},{1,129},{65,193},{129,1},{193,65... | collective-permute-start | bytes 1572872 | tf_op jit(solution)/shard_map/ppermute | solution.py:31
  69.9 21.4 %collective-permute-start.8 = (bf16[32,8192]{1,0:T(8,128)(2,1)}, bf16[32,8192]{1,0:T(8,128)(2,1)}, u32[]{:S(2)}, u32[]{:S(2)}) collective-permute-start(bf16[32,8192]{1,0:T(8,128)(2,1)} %change_rows.1.refs_0_), channel_id=1, source_target_pairs={{0,64},{64,0},{128,192},{192,128},{1,65},{65,1},{129,193},{193,129... | collective-permute-start | bytes 1572872 | tf_op jit(solution)/shard_map/ppermute | solution.py:31
  86.9 4.4 %collective-permute-start.10 = (bf16[32,8192]{1,0:T(8,128)(2,1)}, bf16[32,8192]{1,0:T(8,128)(2,1)}, u32[]{:S(2)}, u32[]{:S(2)}) collective-permute-start(bf16[32,8192]{1,0:T(8,128)(2,1)} %collective-permute-done.9.refs_2_), channel_id=1, source_target_pairs={{0,64},{64,0},{128,192},{192,128},{1,65},{65,1},{129,193},{193,129... | collective-permute-start | bytes 1572872 | tf_op jit(solution)/shard_map/ppermute | solution.py:31
  89.0 9.1 %collective-permute-start.2 = (bf16[16,32,128]{2,1,0:T(8,128)(2,1)S(1)}, bf16[16,32,128]{2,1,0:T(8,128)(2,1)S(1)}, u32[]{:S(2)}, u32[]{:S(2)}) collective-permute-start(bf16[16,32,128]{2,1,0:T(8,128)(2,1)S(1)} %get-tuple-element.17), channel_id=1, source_target_pairs={{0,64},{64,0},{128,192},{192,128},{1,65},{65,1},{129,193},{193,129... | collective-permute-start | bytes 393224 | tf_op jit(solution)/shard_map/ppermute | solution.py:31
  89.1 9.0 %collective-permute-start.3 = (bf16[16,32,128]{2,1,0:T(8,128)(2,1)S(1)}, bf16[16,32,128]{2,1,0:T(8,128)(2,1)S(1)}, u32[]{:S(2)}, u32[]{:S(2)}) collective-permute-start(bf16[16,32,128]{2,1,0:T(8,128)(2,1)S(1)} %get-tuple-element.18), channel_id=1, source_target_pairs={{0,128},{64,192},{128,0},{192,64},{1,129},{65,193},{129,1},{193,65... | collective-permute-start | bytes 393224 | tf_op jit(solution)/shard_map/ppermute | solution.py:31
  89.7 8.5 %collective-permute-start.4 = (bf16[16,32,128]{2,1,0:T(8,128)(2,1)S(1)}, bf16[16,32,128]{2,1,0:T(8,128)(2,1)S(1)}, u32[]{:S(2)}, u32[]{:S(2)}) collective-permute-start(bf16[16,32,128]{2,1,0:T(8,128)(2,1)S(1)} %get-tuple-element.19), channel_id=1, source_target_pairs={{0,192},{64,128},{128,64},{192,0},{1,193},{65,129},{129,65},{193,1... | collective-permute-start | bytes 393224 | tf_op jit(solution)/shard_map/ppermute | solution.py:31

commit v2 on v0

v2 whole, which is shorter than its diff:
```python
import jax
import jax.numpy as jnp
from jax import lax
from jax.experimental import pallas as pl
from jax.experimental.pallas import tpu as pltpu
from jax.sharding import PartitionSpec as P

outer_rate = 0.7
outer_beta = 0.9
mix_weight = 0.5

BF = jnp.bfloat16
F32 = jnp.float32
VM = pl.BlockSpec(memory_space=pltpu.VMEM)
SM = pl.BlockSpec(memory_space=pltpu.SMEM)
HBM = pl.BlockSpec(memory_space=pltpu.HBM)
ANY = pl.BlockSpec(memory_space=pl.ANY)
STEP = 1024
ORDER = 1 << 34
AVERAGE = 1 << 34
OUTPUTS = 2 << 20


def seg_of(r):
    return 2 * (r % 2) + r // 2


def peer(r, k):
    return jnp.bitwise_xor(r, k)


def shape(*dims, dtype=BF):
    return jax.ShapeDtypeStruct(dims, dtype)


def rows(start, count):
    return pl.ds(pl.multiple_of(start, count), count)


def call(body, name, nbytes, out_shape, in_specs, out_specs, **more):
    return pl.pallas_call(
        body,
        out_shape=out_shape,
        in_specs=in_specs,
        out_specs=out_specs,
        compiler_params=pltpu.CompilerParams(vmem_limit_bytes=12 * 2**20),
        cost_estimate=pl.CostEstimate(flops=nbytes, bytes_accessed=nbytes, transcendentals=0),
        name=name,
        **more,
    )


def swap(x, k):
    return lax.ppermute(x, "replica", [(i, i ^ k) for i in range(4)])


def half_for_core(r, local):
    def body(r_ref, l_ref, o_ref, sem):
        at = rows((1 - r_ref[0] % 2) * 64, 64)
        copy = pltpu.make_async_copy(l_ref.at[at, :], o_ref, sem)
        copy.start()
        copy.wait()

    return call(
        body, "half_for_core", 2 << 20, shape(64, 8192), [SM, HBM], VM,
        scratch_shapes=[pltpu.SemaphoreType.DMA],
    )(r, local)


def split_momentum(r, momentum):
    def body(r_ref, m_ref, *outs):
        for k in range(4):
            seg = seg_of(peer(r_ref[0], k))
            for j in range(16):
                outs[k][j] = m_ref[rows(j * 128 + seg * 32, 32), :].astype(BF)

    return call(
        body, "split_momentum", 3 << 19, [shape(16, 32, 128)] * 4, [SM, VM], [VM] * 4
    )(r, momentum)


def in_order(r, pieces, after):
    def body(r_ref, *refs):
        for k in range(4):
            refs[5][peer(r_ref[0], k)] = refs[k][...]

    return call(
        body, "in_order", ORDER, shape(4, 16, 32, 128), [SM] + [VM] * 4 + [ANY], VM
    )(r, *pieces, after)


def partial_for_other(r, local, theirs, anchor, after):
    def body(r_ref, l_ref, t_ref, a_ref, after_ref, o_ref):
        at = rows(seg_of(peer(r_ref[0], 2)) * 32, 32)
        half = rows((1 - r_ref[0] // 2) * 32, 32)

        def step(i, carry):
            cols = rows(i * STEP, STEP)
            a = a_ref[at, cols].astype(F32)
            mine = a - l_ref[at, cols].astype(F32)
            o_ref[:, cols] = (mine + (a - t_ref[half, cols].astype(F32))).astype(BF)
            return carry

        lax.fori_loop(0, 8192 // STEP, step, 0)

    return call(
        body, "partial_for_other", 2 << 20, shape(32, 8192), [SM, VM, VM, VM, ANY], VM
    )(r, local, theirs, anchor, after)


def average_rows(r, local, theirs, anchor, partial):
    def body(r_ref, l_ref, t_ref, a_ref, p_ref, avg_ref):
        at = rows(seg_of(r_ref[0]) * 32, 32)
        half = rows((r_ref[0] // 2) * 32, 32)

        def step(i, carry):
            cols = rows(i * STEP, STEP)
            a = a_ref[at, cols].astype(F32)
            own = (a - l_ref[at, cols].astype(F32)) + (a - t_ref[half, cols].astype(F32))
            avg_ref[:, cols] = (own + p_ref[:, cols].astype(F32)) * 0.25
            return carry

        lax.fori_loop(0, 8192 // STEP, step, 0)

    return call(
        body, "average_rows", AVERAGE, shape(32, 8192, dtype=F32), [SM] + [VM] * 4, VM
    )(r, local, theirs, anchor, partial)


def cut_columns(r, avg):
    def body(r_ref, avg_ref, *outs):
        for k in range(4):
            start = peer(r_ref[0], k) * 2048

            def step(n, carry):
                outs[k][n] = avg_ref[:, rows(start + n * 128, 128)].astype(BF)
                return carry

            lax.fori_loop(0, 16, step, 0, unroll=8)

    return call(
        body, "cut_columns", 3 << 19, [shape(16, 32, 128)] * 4, [SM, VM], [VM] * 4
    )(r, avg)


def stack_pieces(pieces):
    def body(*refs):
        for k in range(4):
            refs[4][:, k] = refs[k][...]

    return call(body, "stack_pieces", 1 << 20, shape(16, 4, 32, 128), [VM] * 4, VM)(*pieces)


def change_rows(avg, m):
    def body(avg_ref, m_ref, o_ref):
        def step(n, carry):
            cols = rows(n * 128, 128)
            average = avg_ref[:, cols]
            momentum = outer_beta * m_ref[n].astype(F32) + average
            o_ref[:, cols] = (outer_rate * (average + outer_beta * momentum)).astype(BF)
            return carry

        lax.fori_loop(0, 64, step, 0, unroll=8)

    return call(body, "change_rows", 2 << 20, shape(32, 8192), [VM, VM], VM)(avg, m)


def new_momentum_of(g, momentum, pieces):
    def body(g_ref, m_ref, p_ref, o_ref):
        for k in range(4):
            seg = seg_of(peer(g_ref[0], k))
            for j in range(16):
                at = rows(j * 128 + seg * 32, 32)
                o_ref[at, :] = outer_beta * m_ref[at, :] + p_ref[j, k].astype(F32)

    return call(
        body, "new_momentum_of", 5 << 19, shape(2048, 128, dtype=F32), [SM, VM, VM], VM
    )(g, momentum, pieces)


def outputs_of(r, local, anchor, changes, before):
    ks = sorted(changes)
    n = len(ks)
    parts, width = 4, 2048

    def body(r_ref, l_ref, a_ref, *refs):
        news, mixes, sems = refs[-3:]
        new_ref, mixed_ref = refs[-5:-3]
        copies = []
        for m, k in enumerate(ks):
            at = rows(seg_of(peer(r_ref[0], k)) * 32, 32)
            for p in range(parts):

                def step(i, carry, m=m, p=p, at=at):
                    cols = rows(p * width + i * 512, 512)
                    global_new = a_ref[at, cols].astype(F32) - refs[m][:, cols].astype(F32)
                    news[m, :, cols] = global_new.astype(BF)
                    mixes[m, :, cols] = (
                        mix_weight * l_ref[at, cols].astype(F32) + (1.0 - mix_weight) * global_new
                    ).astype(BF)
                    return carry

                lax.fori_loop(0, width // 512, step, 0)
                cols = pl.ds(p * width, width)
                for o, (src, dst) in enumerate(((news, new_ref), (mixes, mixed_ref))):
                    sem = sems.at[(m * parts + p) * 2 + o]
                    copy = pltpu.make_async_copy(src.at[m, :, cols], dst.at[at, cols], sem)
                    copy.start()
                    copies.append(copy)
        for copy in copies:
            copy.wait()

    return call(
        body, "outputs_of", OUTPUTS, [shape(128, 8192)] * 2,
        [SM] + [VM] * (2 + n) + [HBM] * len(before), [HBM, HBM],
        scratch_shapes=[
            pltpu.VMEM((n, 32, 8192), BF),
            pltpu.VMEM((n, 32, 8192), BF),
            pltpu.SemaphoreType.DMA((n * parts * 2,)),
        ],
        input_output_aliases={3 + n + b: b for b in range(len(before))},
    )(r, local, anchor, *[changes[k] for k in ks], *before)


def across(x, k):
    pairs = [
        (64 * r + 16 * g + q, 64 * g + 16 * (r ^ k) + q)
        for r in range(4)
        for g in range(4)
        for q in range(16)
    ]
    return lax.ppermute(x, ("replica", "fsdp"), pairs)


def local(local_weights, anchor, momentum):
    own = local_weights[0]
    r = lax.axis_index("replica")[None].astype(jnp.int32)
    g = (lax.axis_index("fsdp") // 16)[None].astype(jnp.int32)

    theirs = swap(half_for_core(r, own), 1)

    pieces = split_momentum(r, momentum)
    head = pieces[0]
    pieces = [head] + [swap(pieces[k], k) for k in (1, 2, 3)]
    for_other = partial_for_other(r, own, theirs, anchor, head)
    partial = swap(for_other, 2)
    by_row = in_order(r, pieces, for_other).reshape(64, 32, 128)
    m_rows = lax.all_to_all(by_row, "fsdp", 0, 0, tiled=True)

    avg = average_rows(r, own, theirs, anchor, partial)
    cut = stack_pieces([across(x, k) for k, x in enumerate(cut_columns(r, avg))])
    groups = [[16 * i + q for q in range(16)] for i in range(4)]
    cut = lax.all_to_all(cut, "fsdp", 0, 0, axis_index_groups=groups, tiled=True)
    new_momentum = new_momentum_of(g, momentum, cut)

    change = change_rows(avg, m_rows)
    change2 = swap(change, 2)
    change1 = swap(change, 1)
    change3 = swap(change2, 1)
    outs = outputs_of(r, own, anchor, {0: change, 1: change1}, ())
    outs = outputs_of(r, own, anchor, {2: change2}, outs)
    new_anchor, mixed = outputs_of(r, own, anchor, {3: change3}, outs)
    return new_momentum, new_anchor, mixed[None]


def solution(mesh):
    return jax.shard_map(
        local,
        mesh=mesh,
        in_specs=(P("replica", "fsdp", None), P("fsdp", None), P("replica", "fsdp")),
        out_specs=(P("replica", "fsdp"), P("fsdp", None), P("replica", "fsdp", None)),
        check_vma=False,
    )
```

time: 238 us -> 85.5 us (0.36)
  blocking collectives: 129 us -> 0 us
  waiting for transfers between devices: 58.9 us -> 11 us
  starting transfers between devices: 0.08 us -> 47.3 us
  Pallas kernels: 0 us -> 15.8 us
  between operations: 14 us -> 0.82 us
  local copies, waits for them, and re-layouts: 22.5 us -> 9.85 us
  other arithmetic: 11.2 us -> 0 us
    all_to_all x2 -> x0, blocking collectives: 129 us -> none  [the longest x1 64.9 us: local(): lax.all_to_all(delta, 'fsdp', split_axis=1, concat_axis=0, tiled=True)]
    all_gather x1 -> x0, waiting for transfers between devices: 32.8 us -> none  [local(): rows_all = lax.all_gather(change, 'replica', axis=0, tiled=True)]
    all_to_all x0 -> x2, starting transfers between devices: none -> 26.6 us  [the longest x1 13.7 us: local(): lax.all_to_all(cut, 'fsdp', 0, 0, axis_index_groups=groups, tiled=True)]
    reduce_scatter x1 -> x0, waiting for transfers between devices: 26.1 us -> none  [local(): lax.psum_scatter(delta_cols.astype(jnp.float32).astype(jnp.bfloat16), 're...]
    ppermute x0 -> x12, starting transfers between devices: none -> 20.7 us  [the longest x4 15.9 us: across(): return lax.ppermute(x, ('replica', 'fsdp'), pairs)]
    pallas_call x0 -> x12, Pallas kernels: none -> 15.8 us  [the longest x3 7.06 us: outputs_of(): call(body, 'outputs_of', OUTPUTS, [shape(128, 8192)] * 2, [SM] + [VM] * (...]
    convert_element_type x3 -> x0, other arithmetic: 11.2 us -> none  [the longest x1 5.28 us: local(): (mix_weight * local_wide + (1.0 - mix_weight) * global_new).astype(jnp.bf...]
    all_to_all x2 -> x0, local copies, waits for them, and re-layouts: 8.12 us -> none  [the longest x1 4.06 us: local(): lax.all_to_all(rows_all, 'fsdp', split_axis=0, concat_axis=1, tiled=True)]
  transfers between devices with their start and end apart: 2 -> 14, of which waited for: 2 -> 6; matrix products, arithmetic and copies ran while one was open for 0% -> 0% of each run, Pallas kernels for 0% -> 16%
where the time goes in v2:
time: 85.5 us; the launch traced here: 84.8 us
  starting transfers between devices  47.3 us (55%)
  Pallas kernels  15.8 us (18%)
  waiting for transfers between devices  11 us (13%)
  local copies, waits for them, and re-layouts  9.85 us (12%)
    ppermute x4, starting transfers between devices, across(): return lax.ppermute(x, ('replica', 'fsdp'), pairs)  15.9 us
    all_to_all x1, starting transfers between devices, local(): lax.all_to_all(cut, 'fsdp', 0, 0, axis_index_groups=groups, tiled=True)  13.7 us
    all_to_all x1, starting transfers between devices, local(): m_rows = lax.all_to_all(by_row, 'fsdp', 0, 0, tiled=True)  12.9 us
    unnamed x24, local copies, waits for them, and re-layouts  9.85 us
    pallas_call x3, Pallas kernels, outputs_of(): call(body, 'outputs_of', OUTPUTS, [shape(128, 8192)] * 2, [SM] + [VM] * (...  7.06 us
    ppermute x8, waiting for transfers between devices, swap(): return lax.ppermute(x, 'replica', [(i, i ^ k) for i in range(4)])  5.79 us
    ppermute x8, starting transfers between devices, swap(): return lax.ppermute(x, 'replica', [(i, i ^ k) for i in range(4)])  4.81 us
    all_to_all x1, waiting for transfers between devices, local(): lax.all_to_all(cut, 'fsdp', 0, 0, axis_index_groups=groups, tiled=True)  3.64 us
  transfers between devices with their start and end apart: 14, of which 6 were waited for; matrix products, arithmetic and copies ran while one was open for 0% of the time, Pallas kernels for 16%

profile of v2, /device:TPU:8, one launch (start us, length us, event | category | flops | bytes accessed | tf_op | source)
XLA Modules:
  0.0 84.8 jit_solution(8672525670928527861)
XLA Ops:
  0.6 1.6 %copy-done = bf16[1,128,8192]{2,1,0:T(8,128)(2,1)S(1)} copy-done((bf16[1,128,8192]{2,1,0:T(8,128)(2,1)S(1)}, bf16[1,128,8192]{2,1,0:T(8,128)(2,1)}, u32[]{:S(2)}) %copy-start) | copy-done | bytes 2097176
  2.2 0.1 half_for_core.1
  2.3 0.1 collective-permute-start
  2.4 0.0 copy-start.6
  2.4 1.4 %copy-done.6 = f32[2048,128]{1,0:T(8,128)S(1)} copy-done((f32[2048,128]{1,0:T(8,128)S(1)}, f32[2048,128]{1,0:T(8,128)}, u32[]{:S(2)}) %copy-start.6) | copy-done | bytes 1048600
  3.8 0.1 split_momentum.1
  3.9 0.8 collective-permute-start.6
  4.7 1.8 %collective-permute-start.7 = (bf16[16,32,128]{2,1,0:T(8,128)(2,1)S(1)}, bf16[16,32,128]{2,1,0:T(8,128)(2,1)S(1)}, u32[]{:S(2)}, u32[]{:S(2)}) collective-permute-start(bf16[16,32,128]{2,1,0:T(8,128)(2,1)S(1)} %get-tuple-element.23), channel_id=1, source_target_pairs={{0,128},{64,192},{128,0},{192,64},{1,129},{65,193},{129,1},{193,65... | collective-permute-start | bytes 393224 | tf_op jit(solution)/shard_map/ppermute | solution.py:54
  6.5 0.0 collective-permute-start.8
  6.5 0.0 collective-permute-done.t_ref
  6.5 0.3 partial_for_other.1.refs_4_
  6.8 0.6 copy-done.8
  7.4 1.5 %collective-permute-start.1 = (bf16[32,8192]{1,0:T(8,128)(2,1)S(1)}, bf16[32,8192]{1,0:T(8,128)(2,1)S(1)}, u32[]{:S(2)}, u32[]{:S(2)}) collective-permute-start(bf16[32,8192]{1,0:T(8,128)(2,1)S(1)} %partial_for_other.1.refs_4_), channel_id=1, source_target_pairs={{0,128},{64,192},{128,0},{192,64},{1,129},{65,193},{129,1},{193,65... | collective-permute-start | bytes 1572872 | tf_op jit(solution)/shard_map/ppermute | solution.py:54
  9.0 0.0 collective-permute-done.6.refs_1_
  9.0 2.1 %collective-permute-done.7.refs_2_ = bf16[16,32,128]{2,1,0:T(8,128)(2,1)S(1)} collective-permute-done((bf16[16,32,128]{2,1,0:T(8,128)(2,1)S(1)}, bf16[16,32,128]{2,1,0:T(8,128)(2,1)S(1)}, u32[]{:S(2)}, u32[]{:S(2)}) %collective-permute-start.7) | collective-permute-done | bytes 131104 | tf_op jit(solution)/shard_map/ppermute | solution.py:54
  11.0 2.1 %collective-permute-done.8.refs_3_ = bf16[16,32,128]{2,1,0:T(8,128)(2,1)S(1)} collective-permute-done((bf16[16,32,128]{2,1,0:T(8,128)(2,1)S(1)}, bf16[16,32,128]{2,1,0:T(8,128)(2,1)S(1)}, u32[]{:S(2)}, u32[]{:S(2)}) %collective-permute-start.8) | collective-permute-done | bytes 131104 | tf_op jit(solution)/shard_map/ppermute | solution.py:54
  13.1 0.8 in_order.1
  14.0 12.9 %all-to-all-start.1 = ((bf16[64,32,128]{2,1,0:T(8,128)(2,1)}), bf16[64,32,128]{2,1,0:T(8,128)(2,1)}, u32[]{:S(2)}, u32[]{:S(2)}) async-start(bf16[64,32,128]{2,1,0:T(8,128)(2,1)} %bitcast.3), calls=%async_computation.1 | async-start | bytes 1048576 | tf_op jit(solution)/shard_map/all_to_all | solution.py:248
  26.9 0.0 collective-permute-done.1.p_ref
  26.9 0.0 copy-start.10
  26.9 0.8 copy-done.10
  27.7 1.6 %copy-done.3 = bf16[128,8192]{1,0:T(8,128)(2,1)S(1)} copy-done((bf16[128,8192]{1,0:T(8,128)(2,1)S(1)}, bf16[128,8192]{1,0:T(8,128)(2,1)}, u32[]{:S(2)}) %copy-start.3) | copy-done | bytes 2097176
  29.3 1.2 %copy-done.9 = bf16[64,8192]{1,0:T(8,128)(2,1)S(1)} copy-done((bf16[64,8192]{1,0:T(8,128)(2,1)S(1)}, bf16[64,8192]{1,0:T(8,128)(2,1)}, u32[]{:S(2)}) %copy-start.9) | copy-done | bytes 1048600
  30.5 1.0 %copy-done.11 = bf16[32,8192]{1,0:T(8,128)(2,1)S(1)} copy-done((bf16[32,8192]{1,0:T(8,128)(2,1)S(1)}, bf16[32,8192]{1,0:T(8,128)(2,1)}, u32[]{:S(2)}) %copy-start.11) | copy-done | bytes 524312
  31.6 0.4 average_rows.1.avg_ref
  31.9 1.0 %cut_columns.1 = (bf16[16,32,128]{2,1,0:T(8,128)(2,1)}, bf16[16,32,128]{2,1,0:T(8,128)(2,1)}, bf16[16,32,128]{2,1,0:T(8,128)(2,1)}, bf16[16,32,128]{2,1,0:T(8,128)(2,1)}) custom-call(s32[1]{0:T(128)} %bitcast.1.r_ref, f32[32,8192]{1,0:T(8,128)S(1)} %average_rows.1.avg_ref), custom_call_target="tpu_custom_call" | custom-call | flops 1572864 | bytes 1572864 | tf_op jit(solution)/shard_map/cut_columns/pallas_call | solution.py:141
  32.9 8.7 %collective-permute-start.2 = (bf16[16,32,128]{2,1,0:T(8,128)(2,1)}, bf16[16,32,128]{2,1,0:T(8,128)(2,1)S(1)}, u32[]{:S(2)}, u32[]{:S(2)}) collective-permute-start(bf16[16,32,128]{2,1,0:T(8,128)(2,1)} %get-tuple-element.18), channel_id=1, source_target_pairs={{0,0},{1,1},{2,2},{3,3},{4,4},{5,5},{6,6},{7,7},{8,8},{9,9},{10,10... | collective-permute-start | bytes 393224 | tf_op jit(solution)/shard_map/ppermute | solution.py:232
  41.6 0.1 collective-permute-start.3
  41.7 0.1 collective-permute-start.4
  41.8 7.0 %collective-permute-start.5 = (bf16[16,32,128]{2,1,0:T(8,128)(2,1)}, bf16[16,32,128]{2,1,0:T(8,128)(2,1)}, u32[]{:S(2)}, u32[]{:S(2)}) collective-permute-start(bf16[16,32,128]{2,1,0:T(8,128)(2,1)} %get-tuple-element.21), channel_id=1, source_target_pairs={{0,48},{1,49},{2,50},{3,51},{4,52},{5,53},{6,54},{7,55},{8,56},{9,... | collective-permute-start | bytes 393224 | tf_op jit(solution)/shard_map/ppermute | solution.py:232
  48.8 0.0 all-to-all-done.1.m_ref
  48.8 2.2 %change_rows.1.refs_0_ = bf16[32,8192]{1,0:T(8,128)(2,1)} custom-call(f32[32,8192]{1,0:T(8,128)S(1)} %average_rows.1.avg_ref, bf16[64,32,128]{2,1,0:T(8,128)(2,1)} %all-to-all-done.1.m_ref), custom_call_target="tpu_custom_call" | custom-call | flops 2097152 | bytes 2097152 | tf_op jit(solution)/shard_map/change_rows/pallas_call | solution.py:165
  51.0 0.0 collective-permute-start.9
  51.0 1.0 %collective-permute-done.3.refs_1_ = bf16[16,32,128]{2,1,0:T(8,128)(2,1)S(1)} collective-permute-done((bf16[16,32,128]{2,1,0:T(8,128)(2,1)}, bf16[16,32,128]{2,1,0:T(8,128)(2,1)S(1)}, u32[]{:S(2)}, u32[]{:S(2)}) %collective-permute-start.3) | collective-permute-done | bytes 131104 | tf_op jit(solution)/shard_map/ppermute | solution.py:232
  52.0 0.5 collective-permute-done.4.refs_2_
  52.6 1.7 %stack_pieces.1 = bf16[16,4,32,128]{3,2,1,0:T(8,128)(2,1)} custom-call(bf16[16,32,128]{2,1,0:T(8,128)(2,1)S(1)} %collective-permute-done.2.refs_0_, bf16[16,32,128]{2,1,0:T(8,128)(2,1)S(1)} %collective-permute-done.3.refs_1_, bf16[16,32,128]{2,1,0:T(8,128)(2,1)S(1)} %collective-permute-done.4.refs_2_, bf16[16,32,128]{2,1,0:T(8,128)(2,1)} %collective-permute-done.5.refs_3_), custom_call_target="tpu_custom_call" | custom-call | flops 1048576 | bytes 1048576 | tf_op jit(solution)/shard_map/stack_pieces/pallas_call | solution.py:151
  54.3 13.7 %all-to-all-start = ((bf16[16,4,32,128]{3,2,1,0:T(8,128)(2,1)}), bf16[16,4,32,128]{3,2,1,0:T(8,128)(2,1)}, u32[]{:S(2)}, u32[]{:S(2)}) async-start(bf16[16,4,32,128]{3,2,1,0:T(8,128)(2,1)} %stack_pieces.1), calls=%async_computation | async-start | bytes 1048576 | tf_op jit(solution)/shard_map/all_to_all | solution.py:253
  68.0 0.1 collective-permute-start.11
  68.1 0.5 collective-permute-start.10
  68.6 1.6 %collective-permute-done.11.refs_1_ = bf16[32,8192]{1,0:T(8,128)(2,1)S(1)} collective-permute-done((bf16[32,8192]{1,0:T(8,128)(2,1)}, bf16[32,8192]{1,0:T(8,128)(2,1)S(1)}, u32[]{:S(2)}, u32[]{:S(2)}) %collective-permute-start.11) | collective-permute-done | bytes 524320 | tf_op jit(solution)/shard_map/ppermute | solution.py:54
  70.2 1.6 %copy-done.4 = bf16[128,8192]{1,0:T(8,128)(2,1)S(1)} copy-done((bf16[128,8192]{1,0:T(8,128)(2,1)S(1)}, bf16[128,8192]{1,0:T(8,128)(2,1)}, u32[]{:S(2)}) %copy-start.4) | copy-done | bytes 2097176
  71.8 2.6 %outputs_of.3 = (bf16[128,8192]{1,0:T(8,128)(2,1)}, bf16[128,8192]{1,0:T(8,128)(2,1)}) custom-call(s32[1]{0:T(128)} %bitcast.1.r_ref, bf16[128,8192]{1,0:T(8,128)(2,1)S(1)} %bitcast.8, bf16[128,8192]{1,0:T(8,128)(2,1)S(1)} %copy-done.4, bf16[32,8192]{1,0:T(8,128)(2,1)} %change_rows.1.refs_0_, bf16[32,8192]{1,0:T(8,128)(2,1)S(1)} %collective-permute-done.11.refs_1_), custom_call_target="tpu_custom_call" | custom-call | flops 2097152 | bytes 2097152 | tf_op jit(solution)/shard_map/outputs_of/pallas_call | solution.py:213
  74.4 0.0 copy-start.7
  74.4 2.3 %outputs_of.4 = (bf16[128,8192]{1,0:T(8,128)(2,1)}, bf16[128,8192]{1,0:T(8,128)(2,1)}) custom-call(s32[1]{0:T(128)} %bitcast.1.r_ref, bf16[128,8192]{1,0:T(8,128)(2,1)S(1)} %bitcast.9, bf16[128,8192]{1,0:T(8,128)(2,1)S(1)} %copy-done.4, bf16[32,8192]{1,0:T(8,128)(2,1)} %collective-permute-done.9.refs_0_, ...), custom_call_target="tpu_custom_call", output_to_operand_aliasing={{0}: (4, {}), {1}: (5, {})} | custom-call | flops 2097152 | bytes 2097152 | tf_op jit(solution)/shard_map/outputs_of/pallas_call | solution.py:213
  76.7 3.6 %all-to-all-done.p_ref = bf16[16,4,32,128]{3,2,1,0:T(8,128)(2,1)} async-done(((bf16[16,4,32,128]{3,2,1,0:T(8,128)(2,1)}), bf16[16,4,32,128]{3,2,1,0:T(8,128)(2,1)}, u32[]{:S(2)}, u32[]{:S(2)}) %all-to-all-start) | async-done | bytes 524320 | tf_op jit(solution)/shard_map/all_to_all | solution.py:253
  80.4 2.3 %new_momentum_of.1 = f32[2048,128]{1,0:T(8,128)} custom-call(s32[1]{0:T(128)} %bitcast.g_ref, f32[2048,128]{1,0:T(8,128)S(1)} %copy-done.7, bf16[16,4,32,128]{3,2,1,0:T(8,128)(2,1)} %all-to-all-done.p_ref), custom_call_target="tpu_custom_call" | custom-call | flops 2621440 | bytes 2621440 | tf_op jit(solution)/shard_map/new_momentum_of/pallas_call | solution.py:176
  82.6 0.0 collective-permute-done.10.refs_0_
  82.6 2.2 %outputs_of.5 = (bf16[128,8192]{1,0:T(8,128)(2,1)}, bf16[128,8192]{1,0:T(8,128)(2,1)}) custom-call(s32[1]{0:T(128)} %bitcast.1.r_ref, bf16[128,8192]{1,0:T(8,128)(2,1)S(1)} %bitcast.10, bf16[128,8192]{1,0:T(8,128)(2,1)S(1)} %copy-done.5, bf16[32,8192]{1,0:T(8,128)(2,1)} %collective-permute-done.10.refs_0_, ...), custom_call_target="tpu_custom_call", output_to_operand_aliasing={{0}: (4, {}), {1}: (5, {})} | custom-call | flops 2097152 | bytes 2097152 | tf_op jit(solution)/shard_map/outputs_of/pallas_call | solution.py:213
  (16 shorter events, 0.0 us)
Async XLA Ops:
  0.6 1.6 %copy-start = (bf16[1,128,8192]{2,1,0:T(8,128)(2,1)S(1)}, bf16[1,128,8192]{2,1,0:T(8,128)(2,1)}, u32[]{:S(2)}) copy-start(bf16[1,128,8192]{2,1,0:T(8,128)(2,1)} %param.3) | copy-start | bytes 6291460
  2.2 4.3 %copy-start.1 = (bf16[1,128,8192]{2,1,0:T(8,128)(2,1)S(1)}, bf16[1,128,8192]{2,1,0:T(8,128)(2,1)}, u32[]{:S(2)}) copy-start(bf16[1,128,8192]{2,1,0:T(8,128)(2,1)} %param.3) | copy-start | bytes 6291460
  2.2 4.3 %copy-start.2 = (bf16[128,8192]{1,0:T(8,128)(2,1)S(1)}, bf16[128,8192]{1,0:T(8,128)(2,1)}, u32[]{:S(2)}) copy-start(bf16[128,8192]{1,0:T(8,128)(2,1)} %a_ref.9) | copy-start | bytes 6291460
  2.3 4.2 %collective-permute-start = (bf16[64,8192]{1,0:T(8,128)(2,1)S(1)}, bf16[64,8192]{1,0:T(8,128)(2,1)S(1)}, u32[]{:S(2)}, u32[]{:S(2)}) collective-permute-start(bf16[64,8192]{1,0:T(8,128)(2,1)S(1)} %half_for_core.1), channel_id=1, source_target_pairs={{0,64},{64,0},{128,192},{192,128},{1,65},{65,1},{129,193},{193,129... | collective-permute-start | bytes 3145736 | tf_op jit(solution)/shard_map/ppermute | solution.py:54
  2.4 1.4 %copy-start.6 = (f32[2048,128]{1,0:T(8,128)S(1)}, f32[2048,128]{1,0:T(8,128)}, u32[]{:S(2)}) copy-start(f32[2048,128]{1,0:T(8,128)} %m_ref.3) | copy-start | bytes 3145732
  3.9 5.1 %collective-permute-start.6 = (bf16[16,32,128]{2,1,0:T(8,128)(2,1)S(1)}, bf16[16,32,128]{2,1,0:T(8,128)(2,1)S(1)}, u32[]{:S(2)}, u32[]{:S(2)}) collective-permute-start(bf16[16,32,128]{2,1,0:T(8,128)(2,1)S(1)} %get-tuple-element.22), channel_id=1, source_target_pairs={{0,64},{64,0},{128,192},{192,128},{1,65},{65,1},{129,193},{193,129... | collective-permute-start | bytes 393224 | tf_op jit(solution)/shard_map/ppermute | solution.py:54
  4.7 6.3 %collective-permute-start.7 = (bf16[16,32,128]{2,1,0:T(8,128)(2,1)S(1)}, bf16[16,32,128]{2,1,0:T(8,128)(2,1)S(1)}, u32[]{:S(2)}, u32[]{:S(2)}) collective-permute-start(bf16[16,32,128]{2,1,0:T(8,128)(2,1)S(1)} %get-tuple-element.23), channel_id=1, source_target_pairs={{0,128},{64,192},{128,0},{192,64},{1,129},{65,193},{129,1},{193,65... | collective-permute-start | bytes 393224 | tf_op jit(solution)/shard_map/ppermute | solution.py:54
  6.5 6.7 %collective-permute-start.8 = (bf16[16,32,128]{2,1,0:T(8,128)(2,1)S(1)}, bf16[16,32,128]{2,1,0:T(8,128)(2,1)S(1)}, u32[]{:S(2)}, u32[]{:S(2)}) collective-permute-start(bf16[16,32,128]{2,1,0:T(8,128)(2,1)S(1)} %get-tuple-element.24), channel_id=1, source_target_pairs={{0,192},{64,128},{128,64},{192,0},{1,193},{65,129},{129,65},{193,1... | collective-permute-start | bytes 393224 | tf_op jit(solution)/shard_map/ppermute | solution.py:54
  6.5 1.0 %copy-start.8 = (bf16[64,8192]{1,0:T(8,128)(2,1)}, bf16[64,8192]{1,0:T(8,128)(2,1)S(1)}, u32[]{:S(2)}) copy-start(bf16[64,8192]{1,0:T(8,128)(2,1)S(1)} %collective-permute-done.t_ref) | copy-start | bytes 3145732
  7.4 19.5 %collective-permute-start.1 = (bf16[32,8192]{1,0:T(8,128)(2,1)S(1)}, bf16[32,8192]{1,0:T(8,128)(2,1)S(1)}, u32[]{:S(2)}, u32[]{:S(2)}) collective-permute-start(bf16[32,8192]{1,0:T(8,128)(2,1)S(1)} %partial_for_other.1.refs_4_), channel_id=1, source_target_pairs={{0,128},{64,192},{128,0},{192,64},{1,129},{65,193},{129,1},{193,65... | collective-permute-start | bytes 1572872 | tf_op jit(solution)/shard_map/ppermute | solution.py:54
  14.0 34.8 %all-to-all-start.1 = ((bf16[64,32,128]{2,1,0:T(8,128)(2,1)}), bf16[64,32,128]{2,1,0:T(8,128)(2,1)}, u32[]{:S(2)}, u32[]{:S(2)}) async-start(bf16[64,32,128]{2,1,0:T(8,128)(2,1)} %bitcast.3), calls=%async_computation.1 | async-start | bytes 1048576 | tf_op jit(solution)/shard_map/all_to_all | solution.py:248
  26.9 0.8 copy-start.10
  27.7 1.6 %copy-start.3 = (bf16[128,8192]{1,0:T(8,128)(2,1)S(1)}, bf16[128,8192]{1,0:T(8,128)(2,1)}, u32[]{:S(2)}) copy-start(bf16[128,8192]{1,0:T(8,128)(2,1)} %a_ref.9) | copy-start | bytes 6291460
  29.3 1.2 %copy-start.9 = (bf16[64,8192]{1,0:T(8,128)(2,1)S(1)}, bf16[64,8192]{1,0:T(8,128)(2,1)}, u32[]{:S(2)}) copy-start(bf16[64,8192]{1,0:T(8,128)(2,1)} %copy-done.8) | copy-start | bytes 3145732
  30.5 1.0 %copy-start.11 = (bf16[32,8192]{1,0:T(8,128)(2,1)S(1)}, bf16[32,8192]{1,0:T(8,128)(2,1)}, u32[]{:S(2)}) copy-start(bf16[32,8192]{1,0:T(8,128)(2,1)} %copy-done.10) | copy-start | bytes 1572868
  32.9 18.1 %collective-permute-start.2 = (bf16[16,32,128]{2,1,0:T(8,128)(2,1)}, bf16[16,32,128]{2,1,0:T(8,128)(2,1)S(1)}, u32[]{:S(2)}, u32[]{:S(2)}) collective-permute-start(bf16[16,32,128]{2,1,0:T(8,128)(2,1)} %get-tuple-element.18), channel_id=1, source_target_pairs={{0,0},{1,1},{2,2},{3,3},{4,4},{5,5},{6,6},{7,7},{8,8},{9,9},{10,10... | collective-permute-start | bytes 393224 | tf_op jit(solution)/shard_map/ppermute | solution.py:232
  41.6 10.4 %collective-permute-start.3 = (bf16[16,32,128]{2,1,0:T(8,128)(2,1)}, bf16[16,32,128]{2,1,0:T(8,128)(2,1)S(1)}, u32[]{:S(2)}, u32[]{:S(2)}) collective-permute-start(bf16[16,32,128]{2,1,0:T(8,128)(2,1)} %get-tuple-element.19), channel_id=1, source_target_pairs={{0,16},{1,17},{2,18},{3,19},{4,20},{5,21},{6,22},{7,23},{8,24},{9,... | collective-permute-start | bytes 393224 | tf_op jit(solution)/shard_map/ppermute | solution.py:232
  41.7 10.9 %collective-permute-start.4 = (bf16[16,32,128]{2,1,0:T(8,128)(2,1)}, bf16[16,32,128]{2,1,0:T(8,128)(2,1)S(1)}, u32[]{:S(2)}, u32[]{:S(2)}) collective-permute-start(bf16[16,32,128]{2,1,0:T(8,128)(2,1)} %get-tuple-element.20), channel_id=1, source_target_pairs={{0,32},{1,33},{2,34},{3,35},{4,36},{5,37},{6,38},{7,39},{8,40},{9,... | collective-permute-start | bytes 393224 | tf_op jit(solution)/shard_map/ppermute | solution.py:232
  41.8 10.8 %collective-permute-start.5 = (bf16[16,32,128]{2,1,0:T(8,128)(2,1)}, bf16[16,32,128]{2,1,0:T(8,128)(2,1)}, u32[]{:S(2)}, u32[]{:S(2)}) collective-permute-start(bf16[16,32,128]{2,1,0:T(8,128)(2,1)} %get-tuple-element.21), channel_id=1, source_target_pairs={{0,48},{1,49},{2,50},{3,51},{4,52},{5,53},{6,54},{7,55},{8,56},{9,... | collective-permute-start | bytes 393224 | tf_op jit(solution)/shard_map/ppermute | solution.py:232
  51.0 17.1 %collective-permute-start.9 = (bf16[32,8192]{1,0:T(8,128)(2,1)}, bf16[32,8192]{1,0:T(8,128)(2,1)}, u32[]{:S(2)}, u32[]{:S(2)}) collective-permute-start(bf16[32,8192]{1,0:T(8,128)(2,1)} %change_rows.1.refs_0_), channel_id=1, source_target_pairs={{0,128},{64,192},{128,0},{192,64},{1,129},{65,193},{129,1},{193,65... | collective-permute-start | bytes 1572872 | tf_op jit(solution)/shard_map/ppermute | solution.py:54
  54.3 26.1 %all-to-all-start = ((bf16[16,4,32,128]{3,2,1,0:T(8,128)(2,1)}), bf16[16,4,32,128]{3,2,1,0:T(8,128)(2,1)}, u32[]{:S(2)}, u32[]{:S(2)}) async-start(bf16[16,4,32,128]{3,2,1,0:T(8,128)(2,1)} %stack_pieces.1), calls=%async_computation | async-start | bytes 1048576 | tf_op jit(solution)/shard_map/all_to_all | solution.py:253
  68.0 2.2 %collective-permute-start.11 = (bf16[32,8192]{1,0:T(8,128)(2,1)}, bf16[32,8192]{1,0:T(8,128)(2,1)S(1)}, u32[]{:S(2)}, u32[]{:S(2)}) collective-permute-start(bf16[32,8192]{1,0:T(8,128)(2,1)} %change_rows.1.refs_0_), channel_id=1, source_target_pairs={{0,64},{64,0},{128,192},{192,128},{1,65},{65,1},{129,193},{193,129... | collective-permute-start | bytes 1572872 | tf_op jit(solution)/shard_map/ppermute | solution.py:54
  68.1 14.5 %collective-permute-start.10 = (bf16[32,8192]{1,0:T(8,128)(2,1)}, bf16[32,8192]{1,0:T(8,128)(2,1)}, u32[]{:S(2)}, u32[]{:S(2)}) collective-permute-start(bf16[32,8192]{1,0:T(8,128)(2,1)} %collective-permute-done.9.refs_0_), channel_id=1, source_target_pairs={{0,64},{64,0},{128,192},{192,128},{1,65},{65,1},{129,193},{193,129... | collective-permute-start | bytes 1572872 | tf_op jit(solution)/shard_map/ppermute | solution.py:54
  70.2 1.6 %copy-start.4 = (bf16[128,8192]{1,0:T(8,128)(2,1)S(1)}, bf16[128,8192]{1,0:T(8,128)(2,1)}, u32[]{:S(2)}) copy-start(bf16[128,8192]{1,0:T(8,128)(2,1)} %a_ref.9) | copy-start | bytes 6291460
  74.4 5.9 %copy-start.7 = (f32[2048,128]{1,0:T(8,128)S(1)}, f32[2048,128]{1,0:T(8,128)}, u32[]{:S(2)}) copy-start(f32[2048,128]{1,0:T(8,128)} %m_ref.3) | copy-start | bytes 3145732
  80.4 2.3 %copy-start.5 = (bf16[128,8192]{1,0:T(8,128)(2,1)S(1)}, bf16[128,8192]{1,0:T(8,128)(2,1)}, u32[]{:S(2)}) copy-start(bf16[128,8192]{1,0:T(8,128)(2,1)} %a_ref.9) | copy-start | bytes 6291460

commit v3 on v0

v3 whole, which is shorter than its diff:
```python
import jax
import jax.numpy as jnp
from jax import lax
from jax.experimental import pallas as pl
from jax.experimental.pallas import tpu as pltpu
from jax.sharding import PartitionSpec as P

outer_rate = 0.7
outer_beta = 0.9
mix_weight = 0.5

BF = jnp.bfloat16
F32 = jnp.float32
PARTS = 4
WIDTH = 8192 // PARTS
INNER = 512
SHORT = 2 << 20
LONG = 1 << 34
VMEM_MIB = 16


def seg_of(r):
    return 2 * (r % 2) + r // 2


def peer(r, k):
    return jnp.bitwise_xor(r, k)


def shape(*dims, dtype=BF):
    return jax.ShapeDtypeStruct(dims, dtype)


def at(start, count):
    return pl.ds(pl.multiple_of(start, count), count)


class Copies:
    def __init__(self, sems):
        self.sems, self.count, self.open = sems, 0, []

    def start(self, src, dst):
        copy = pltpu.make_async_copy(src, dst, self.sems.at[self.count])
        copy.start()
        self.count += 1
        return copy

    def send(self, src, dst):
        self.open.append(self.start(src, dst))

    def finish(self):
        for copy in self.open:
            copy.wait()


def call(body, name, cost, outs, args, scratch, copies, aliases=None, near=None, out_near=False):
    anywhere = pl.BlockSpec(memory_space=pl.ANY)
    whole = pl.BlockSpec(memory_space=pltpu.VMEM)
    near = len(args) if near is None else near
    out_spec = whole if out_near else anywhere
    single = not isinstance(outs, list)
    count = 1 if single else len(outs)
    return pl.pallas_call(
        body,
        out_shape=outs,
        in_specs=[pl.BlockSpec(memory_space=pltpu.SMEM)]
        + [anywhere] * (near - 1)
        + [whole] * (len(args) - near),
        out_specs=out_spec if single else [out_spec] * count,
        scratch_shapes=[pltpu.VMEM(x.shape, x.dtype) for x in scratch]
        + [pltpu.SemaphoreType.DMA((copies,))],
        input_output_aliases=aliases or {},
        compiler_params=pltpu.CompilerParams(vmem_limit_bytes=VMEM_MIB * 2**20),
        cost_estimate=pl.CostEstimate(flops=cost, bytes_accessed=cost, transcendentals=0),
        name=name,
    )(*args)


def swap(x, k):
    return lax.ppermute(x, "replica", [(i, i ^ k) for i in range(4)])


def swap_around(x):
    pairs = [(64 * i + f, 64 * (i ^ 3) + (f ^ 4)) for i in range(4) for f in range(64)]
    return lax.ppermute(x, ("replica", "fsdp"), pairs)


def prologue(r, local, momentum):
    def body(r_ref, l_ref, m_ref, half_ref, *refs):
        outs, (m, sems) = refs[:4], refs[4:]
        copies = Copies(sems)
        loads = [
            copies.start(m_ref.at[pl.ds(p * 512, 512), :], m.at[pl.ds(p * 512, 512), :])
            for p in range(4)
        ]
        other = 1 - r_ref[0] % 2
        copies.send(l_ref.at[at(other * 64, 64), :], half_ref)
        for p in range(4):
            loads[p].wait()
            for k in range(4):
                seg = seg_of(peer(r_ref[0], k))
                for j in range(4 * p, 4 * p + 4):
                    outs[k][j] = m[at(j * 128 + seg * 32, 32), :].astype(BF)
        copies.finish()

    return call(
        body, "prologue", SHORT, [shape(64, 8192)] + [shape(16, 32, 128)] * 4,
        [r, local, momentum], [shape(2048, 128, dtype=F32)], 5, out_near=True,
    )


def in_order(r, pieces, after):
    def body(r_ref, after_ref, *refs):
        for k in range(4):
            refs[4][peer(r_ref[0], k)] = refs[k][...]

    return call(
        body, "in_order", LONG, shape(4, 16, 32, 128), [r, after, *pieces], [], 1,
        near=2, out_near=True,
    )


def inner(step):
    lax.fori_loop(0, WIDTH // INNER, lambda i, c: (step(at(i * INNER, INNER)), c)[1], 0)


def partial_for_other(r, local, theirs, anchor, after):
    def body(r_ref, l_ref, t_ref, a_ref, after_ref, o_ref, l, t, a, o, sems):
        mine = at(seg_of(peer(r_ref[0], 2)) * 32, 32)
        half = at((1 - r_ref[0] // 2) * 32, 32)
        copies = Copies(sems)
        loads = []
        for p in range(PARTS):
            cols = pl.ds(p * WIDTH, WIDTH)
            loads.append([
                copies.start(l_ref.at[mine, cols], l.at[p]),
                copies.start(t_ref.at[half, cols], t.at[p]),
                copies.start(a_ref.at[mine, cols], a.at[p]),
            ])
        for p in range(PARTS):
            for load in loads[p]:
                load.wait()

            def step(cols, p=p):
                x = a[p, :, cols].astype(F32)
                total = (x - l[p, :, cols].astype(F32)) + (x - t[p, :, cols].astype(F32))
                o[p, :, cols] = total.astype(BF)

            inner(step)
            copies.send(o.at[p], o_ref.at[:, pl.ds(p * WIDTH, WIDTH)])
        copies.finish()

    return call(
        body, "partial_for_other", SHORT, shape(32, 8192), [r, local, theirs, anchor, after],
        [shape(PARTS, 32, WIDTH)] * 4, 4 * PARTS,
    )


def average_rows(r, local, theirs, anchor, partial):
    def body(r_ref, l_ref, t_ref, a_ref, p_ref, avg_ref, *refs):
        outs, (l, t, a, q, avg, cut, sems) = refs[:4], refs[4:]
        mine = at(seg_of(r_ref[0]) * 32, 32)
        half = at((r_ref[0] // 2) * 32, 32)
        copies = Copies(sems)
        loads = []
        for k in range(4):
            cols = at(peer(r_ref[0], k) * WIDTH, WIDTH)
            loads.append([
                copies.start(l_ref.at[mine, cols], l.at[k]),
                copies.start(t_ref.at[half, cols], t.at[k]),
                copies.start(a_ref.at[mine, cols], a.at[k]),
                copies.start(p_ref.at[:, cols], q.at[k]),
            ])
        for k in range(4):
            for load in loads[k]:
                load.wait()

            def step(i, carry, k=k):
                cols = at(i * INNER, INNER)
                x = a[k, :, cols].astype(F32)
                own = (x - l[k, :, cols].astype(F32)) + (x - t[k, :, cols].astype(F32))
                y = (own + q[k, :, cols].astype(F32)) * 0.25
                avg[k, :, cols] = y
                narrow = y.astype(BF)
                for n in range(INNER // 128):
                    cut[k, i * (INNER // 128) + n] = narrow[:, n * 128 : (n + 1) * 128]
                return carry

            lax.fori_loop(0, WIDTH // INNER, step, 0)
            copies.send(cut.at[k], outs[k])
            copies.send(avg.at[k], avg_ref.at[:, at(peer(r_ref[0], k) * WIDTH, WIDTH)])
        copies.finish()

    return call(
        body, "average_rows", LONG, [shape(32, 8192, dtype=F32)] + [shape(16, 32, 128)] * 4,
        [r, local, theirs, anchor, partial],
        [shape(4, 32, WIDTH)] * 4 + [shape(4, 32, WIDTH, dtype=F32), shape(4, 16, 32, 128)], 24,
    )


def stack_pieces(r, pieces):
    def body(r_ref, *refs):
        for k in range(4):
            refs[4][:, k] = refs[k][...]

    return call(
        body, "stack_pieces", SHORT, shape(16, 4, 32, 128), [r, *pieces], [], 1,
        near=1, out_near=True,
    )


def change_rows(rg, average, m_rows):
    def body(rg_ref, avg_ref, m_ref, o_ref, avg, m, o, sems):
        flip = jnp.where(peer(rg_ref[0], rg_ref[1]) == 3, 4, 0)
        copies = Copies(sems)
        loads = [
            (
                copies.start(avg_ref.at[:, pl.ds(p * WIDTH, WIDTH)], avg.at[p]),
                copies.start(m_ref.at[pl.ds(p * 16, 16)], m.at[p]),
            )
            for p in range(PARTS)
        ]
        for p in range(PARTS):
            for load in loads[p]:
                load.wait()

            def step(n, carry, p=p):
                cols = at(n * 128, 128)
                x = avg[p, :, cols]
                momentum = outer_beta * m[p, peer(n, flip)].astype(F32) + x
                o[p, :, cols] = (outer_rate * (x + outer_beta * momentum)).astype(BF)
                return carry

            lax.fori_loop(0, 16, step, 0, unroll=4)
            copies.send(o.at[p], o_ref.at[:, pl.ds(p * WIDTH, WIDTH)])
        copies.finish()

    return call(
        body, "change_rows", SHORT, shape(32, 8192), [rg, average, m_rows],
        [shape(PARTS, 32, WIDTH, dtype=F32), shape(4, 16, 32, 128), shape(PARTS, 32, WIDTH)],
        3 * PARTS,
    )


def new_momentum_of(rg, momentum, pieces, after):
    def body(rg_ref, after_ref, p_ref, m_ref, o_ref, q, o, sems):
        copies = Copies(sems)
        copies.send(p_ref, q)
        copies.finish()
        copies.open = []
        r, g = rg_ref[0], rg_ref[1]
        for p in range(4):
            for k in range(4):
                other = peer(g, k)
                flip = jnp.where(other // 2 == r // 2, 0, 4)
                for j in range(4):
                    rows = at(j * 128 + seg_of(other) * 32, 32)
                    all_rows = at((4 * p + j) * 128 + seg_of(other) * 32, 32)
                    piece = q[peer(4 * p + j, flip), k].astype(F32)
                    o[p, rows, :] = outer_beta * m_ref[all_rows, :] + piece
            copies.send(o.at[p], o_ref.at[pl.ds(p * 512, 512), :])
        copies.finish()

    return call(
        body, "new_momentum_of", SHORT, shape(2048, 128, dtype=F32),
        [rg, after, pieces, momentum], [shape(16, 4, 32, 128), shape(4, 512, 128, dtype=F32)], 5,
        near=3,
    )


def outputs_of(r, local, anchor, changes, before):
    ks = sorted(changes)
    n = len(ks)

    def body(r_ref, l_ref, a_ref, *refs):
        new_ref, mixed_ref, l, a, c, new, mixed, sems = refs[-8:]
        copies = Copies(sems)
        loads = []
        for m, k in enumerate(ks):
            rows = at(seg_of(peer(r_ref[0], k)) * 32, 32)
            for p in range(PARTS):
                cols = pl.ds(p * WIDTH, WIDTH)
                i = m * PARTS + p
                loads.append((
                    rows,
                    cols,
                    copies.start(l_ref.at[rows, cols], l.at[i]),
                    copies.start(a_ref.at[rows, cols], a.at[i]),
                    copies.start(refs[m].at[:, cols], c.at[i]),
                ))
        for i, (rows, cols, *waits) in enumerate(loads):
            for load in waits:
                load.wait()

            def step(x, i=i):
                global_new = a[i, :, x].astype(F32) - c[i, :, x].astype(F32)
                new[i, :, x] = global_new.astype(BF)
                mixed[i, :, x] = (
                    mix_weight * l[i, :, x].astype(F32) + (1.0 - mix_weight) * global_new
                ).astype(BF)

            inner(step)
            copies.send(new.at[i], new_ref.at[rows, cols])
            copies.send(mixed.at[i], mixed_ref.at[rows, cols])
        copies.finish()

    return call(
        body, "outputs_of", SHORT, [shape(128, 8192)] * 2,
        [r, local, anchor, *[changes[k] for k in ks], *before],
        [shape(n * PARTS, 32, WIDTH)] * 5, 5 * n * PARTS,
        {3 + n + b: b for b in range(len(before))},
    )


def across(x, k):
    pairs = [
        (64 * r + 16 * g + q, 64 * g + 16 * (r ^ k) + (q if r // 2 == g // 2 else q ^ 4))
        for r in range(4)
        for g in range(4)
        for q in range(16)
    ]
    return lax.ppermute(x, ("replica", "fsdp"), pairs)


def in_hbm(x):
    return pltpu.with_memory_space_constraint(x, pltpu.HBM)


def local(local_weights, anchor, momentum):
    own, anchor = in_hbm(local_weights[0]), in_hbm(anchor)
    r = lax.axis_index("replica")[None].astype(jnp.int32)
    g = (lax.axis_index("fsdp") // 16)[None].astype(jnp.int32)
    rg = jnp.concatenate([r, g])

    half, *pieces = prologue(r, own, in_hbm(momentum))
    theirs = swap(half, 1)
    pieces = [pieces[0], swap(pieces[1], 1), swap(pieces[2], 2), swap_around(pieces[3])]
    for_other = partial_for_other(r, own, theirs, anchor, pieces[0])
    partial = swap(for_other, 2)
    by_row = in_order(r, pieces, for_other).reshape(64, 32, 128)
    m_rows = lax.all_to_all(by_row, "fsdp", 0, 0, tiled=True)

    average, *cut = average_rows(r, own, theirs, anchor, in_hbm(partial))
    cut = stack_pieces(r, [across(x, k) for k, x in enumerate(cut)])
    groups = [[16 * i + q for q in range(16)] for i in range(4)]
    cut = lax.all_to_all(cut, "fsdp", 0, 0, axis_index_groups=groups, tiled=True)

    change = change_rows(rg, average, m_rows)
    change2 = swap(change, 2)
    change1 = swap(change, 1)
    change3 = swap(change2, 1)
    outs = outputs_of(r, own, anchor, {0: change, 1: change1}, ())
    outs = outputs_of(r, own, anchor, {2: change2}, outs)
    new_anchor, mixed = outputs_of(r, own, anchor, {3: change3}, outs)
    new_momentum = new_momentum_of(rg, momentum, cut, in_hbm(mixed))
    return new_momentum, new_anchor, mixed[None]


def solution(mesh):
    return jax.shard_map(
        local,
        mesh=mesh,
        in_specs=(P("replica", "fsdp", None), P("fsdp", None), P("replica", "fsdp")),
        out_specs=(P("replica", "fsdp"), P("fsdp", None), P("replica", "fsdp", None)),
        check_vma=False,
    )
```

time: 238 us -> 76.5 us (0.32)
  blocking collectives: 129 us -> 0 us
  waiting for transfers between devices: 58.9 us -> 13.4 us
  starting transfers between devices: 0.08 us -> 43 us
  local copies, waits for them, and re-layouts: 22.5 us -> 0.01 us
  Pallas kernels: 0 us -> 18.8 us
  between operations: 14 us -> 0.77 us
  other arithmetic: 11.2 us -> 0.07 us
    all_to_all x2 -> x0, blocking collectives: 129 us -> none  [the longest x1 64.9 us: local(): lax.all_to_all(delta, 'fsdp', split_axis=1, concat_axis=0, tiled=True)]
    all_gather x1 -> x0, waiting for transfers between devices: 32.8 us -> none  [local(): rows_all = lax.all_gather(change, 'replica', axis=0, tiled=True)]
    reduce_scatter x1 -> x0, waiting for transfers between devices: 26.1 us -> none  [local(): lax.psum_scatter(delta_cols.astype(jnp.float32).astype(jnp.bfloat16), 're...]
    ppermute x0 -> x12, starting transfers between devices: none -> 23.8 us  [the longest x4 14 us: across(): return lax.ppermute(x, ('replica', 'fsdp'), pairs)]
    all_to_all x0 -> x2, starting transfers between devices: none -> 19.3 us  [the longest x1 13.4 us: local(): m_rows = lax.all_to_all(by_row, 'fsdp', 0, 0, tiled=True)]
    pallas_call x0 -> x10, Pallas kernels: none -> 18.8 us  [call(): pl.pallas_call(body, out_shape=outs, in_specs=[pl.BlockSpec(memory_space=...]
    unnamed x8 -> x2, local copies, waits for them, and re-layouts: 14.4 us -> 0.01 us
    convert_element_type x3 -> x0, other arithmetic: 11.2 us -> none  [the longest x1 5.28 us: local(): (mix_weight * local_wide + (1.0 - mix_weight) * global_new).astype(jnp.bf...]
  transfers between devices with their start and end apart: 2 -> 14, of which waited for: 2 -> 5; matrix products, arithmetic and copies ran while one was open for 0% -> 0% of each run, Pallas kernels for 0% -> 20%
where the time goes in v3:
time: 76.5 us; the launch traced here: 76.1 us
  starting transfers between devices  43 us (56%)
  Pallas kernels  18.8 us (25%)
  waiting for transfers between devices  13.4 us (18%)
  between operations  0.77 us (1%)
    pallas_call x10, Pallas kernels, call(): pl.pallas_call(body, out_shape=outs, in_specs=[pl.BlockSpec(memory_space=...  18.8 us
    ppermute x4, starting transfers between devices, across(): return lax.ppermute(x, ('replica', 'fsdp'), pairs)  14 us
    all_to_all x1, starting transfers between devices, local(): m_rows = lax.all_to_all(by_row, 'fsdp', 0, 0, tiled=True)  13.4 us
    ppermute x7, starting transfers between devices, swap(): return lax.ppermute(x, 'replica', [(i, i ^ k) for i in range(4)])  9.68 us
    all_to_all x1, starting transfers between devices, local(): lax.all_to_all(cut, 'fsdp', 0, 0, axis_index_groups=groups, tiled=True)  5.82 us
    all_to_all x1, waiting for transfers between devices, local(): lax.all_to_all(cut, 'fsdp', 0, 0, axis_index_groups=groups, tiled=True)  3.71 us
    ppermute x4, waiting for transfers between devices, across(): return lax.ppermute(x, ('replica', 'fsdp'), pairs)  3.43 us
    all_to_all x1, waiting for transfers between devices, local(): m_rows = lax.all_to_all(by_row, 'fsdp', 0, 0, tiled=True)  2.97 us
  transfers between devices with their start and end apart: 14, of which 5 were waited for; matrix products, arithmetic and copies ran while one was open for 0% of the time, Pallas kernels for 20%

profile of v3, /device:TPU:8, one launch (start us, length us, event | category | flops | bytes accessed | tf_op | source)
XLA Modules:
  0.0 76.1 jit_solution(2492693521546882413)
XLA Ops:
  0.6 1.6 %prologue.1 = (bf16[64,8192]{1,0:T(8,128)(2,1)S(1)}, bf16[16,32,128]{2,1,0:T(8,128)(2,1)S(1)}, bf16[16,32,128]{2,1,0:T(8,128)(2,1)S(1)}, bf16[16,32,128]{2,1,0:T(8,128)(2,1)S(1)}, bf16[16,32,128]{2,1,0:T(8,128)(2,1)S(1)}) custom-call(s32[1]{0:T(128)} %bitcast.r_ref, bf16[128,8192]{1,0:T(8,128)(2,1)} %bitcast.5, f32[2048,128]{1,0:T(8,128)} %m_ref.3), custom_call_target="tpu_custom_call" | custom-call | flops 2097152 | bytes 2097152 | tf_op jit(solution)/shard_map/prologue/pallas_call | solution.py:63
  2.2 0.1 collective-permute-start
  2.3 0.5 collective-permute-start.2
  2.8 2.2 %collective-permute-start.3 = (bf16[16,32,128]{2,1,0:T(8,128)(2,1)S(1)}, bf16[16,32,128]{2,1,0:T(8,128)(2,1)S(1)}, u32[]{:S(2)}, u32[]{:S(2)}) collective-permute-start(bf16[16,32,128]{2,1,0:T(8,128)(2,1)S(1)} %get-tuple-element.23), channel_id=1, source_target_pairs={{0,128},{64,192},{128,0},{192,64},{1,129},{65,193},{129,1},{193,65... | collective-permute-start | bytes 393224 | tf_op jit(solution)/shard_map/ppermute | solution.py:80
  5.0 0.1 collective-permute-start.4
  5.1 0.0 collective-permute-done.t_ref
  5.1 1.7 %partial_for_other.1.after_ref = bf16[32,8192]{1,0:T(8,128)(2,1)S(1)} custom-call(s32[1]{0:T(128)} %bitcast.r_ref, bf16[128,8192]{1,0:T(8,128)(2,1)} %bitcast.6, bf16[64,8192]{1,0:T(8,128)(2,1)S(1)} %collective-permute-done.t_ref, bf16[128,8192]{1,0:T(8,128)(2,1)} %a_ref.9, bf16[16,32,128]{2,1,0:T(8,128)(2,1)S(1)} %get-tuple-element.20.after_ref.refs_0_), custom_call_target="tpu_custom_call" | custom-call | flops 2097152 | bytes 2097152 | tf_op jit(solution)/shard_map/partial_for_other/pallas_call | solution.py:63
  6.8 2.1 %collective-permute-start.1 = (bf16[32,8192]{1,0:T(8,128)(2,1)S(1)}, bf16[32,8192]{1,0:T(8,128)(2,1)}, u32[]{:S(2)}, u32[]{:S(2)}) collective-permute-start(bf16[32,8192]{1,0:T(8,128)(2,1)S(1)} %partial_for_other.1.after_ref), channel_id=1, source_target_pairs={{0,128},{64,192},{128,0},{192,64},{1,129},{65,193},{129,1},{193,65... | collective-permute-start | bytes 1572872 | tf_op jit(solution)/shard_map/ppermute | solution.py:80
  8.9 0.0 collective-permute-done.2.refs_1_
  8.9 0.0 collective-permute-done.3.refs_2_
  8.9 1.9 %collective-permute-done.4.refs_3_ = bf16[16,32,128]{2,1,0:T(8,128)(2,1)S(1)} collective-permute-done((bf16[16,32,128]{2,1,0:T(8,128)(2,1)S(1)}, bf16[16,32,128]{2,1,0:T(8,128)(2,1)S(1)}, u32[]{:S(2)}, u32[]{:S(2)}) %collective-permute-start.4) | collective-permute-done | bytes 131104 | tf_op jit(solution)/shard_map/ppermute | solution.py:85
  10.8 0.8 %in_order.1 = bf16[4,16,32,128]{3,2,1,0:T(8,128)(2,1)} custom-call(s32[1]{0:T(128)} %bitcast.r_ref, bf16[32,8192]{1,0:T(8,128)(2,1)S(1)} %partial_for_other.1.after_ref, bf16[16,32,128]{2,1,0:T(8,128)(2,1)S(1)} %get-tuple-element.20.after_ref.refs_0_, bf16[16,32,128]{2,1,0:T(8,128)(2,1)S(1)} %collective-permute-done.2.refs_1_, ...), custom_call_target="tpu_custom_call" | custom-call | flops 17179869184 | bytes 17179869184 | tf_op jit(solution)/shard_map/in_order/pallas_call | solution.py:63
  11.7 13.4 %all-to-all-start = ((bf16[64,32,128]{2,1,0:T(8,128)(2,1)}), bf16[64,32,128]{2,1,0:T(8,128)(2,1)S(1)}, u32[]{:S(2)}, u32[]{:S(2)}) async-start(bf16[64,32,128]{2,1,0:T(8,128)(2,1)} %bitcast.3), calls=%async_computation | async-start | bytes 1048576 | tf_op jit(solution)/shard_map/all_to_all | solution.py:341
  25.1 0.0 collective-permute-done.1.p_ref
  25.1 2.6 %average_rows.1 = (f32[32,8192]{1,0:T(8,128)S(1)}, bf16[16,32,128]{2,1,0:T(8,128)(2,1)S(1)}, bf16[16,32,128]{2,1,0:T(8,128)(2,1)S(1)}, bf16[16,32,128]{2,1,0:T(8,128)(2,1)}, bf16[16,32,128]{2,1,0:T(8,128)(2,1)S(1)}) custom-call(s32[1]{0:T(128)} %bitcast.r_ref, bf16[128,8192]{1,0:T(8,128)(2,1)} %bitcast.7, bf16[64,8192]{1,0:T(8,128)(2,1)S(1)} %collective-permute-done.t_ref, ...), custom_call_target="tpu_custom_call" | custom-call | flops 17179869184 | bytes 17179869184 | tf_op jit(solution)/shard_map/average_rows/pallas_call | solution.py:63
  27.8 1.8 %collective-permute-start.10 = (bf16[16,32,128]{2,1,0:T(8,128)(2,1)}, bf16[16,32,128]{2,1,0:T(8,128)(2,1)S(1)}, u32[]{:S(2)}, u32[]{:S(2)}) collective-permute-start(bf16[16,32,128]{2,1,0:T(8,128)(2,1)} %get-tuple-element.32), channel_id=1, source_target_pairs={{0,32},{1,33},{2,34},{3,35},{4,36},{5,37},{6,38},{7,39},{8,40},{9,... | collective-permute-start | bytes 393224 | tf_op jit(solution)/shard_map/ppermute | solution.py:322
  29.5 4.7 %collective-permute-start.11 = (bf16[16,32,128]{2,1,0:T(8,128)(2,1)S(1)}, bf16[16,32,128]{2,1,0:T(8,128)(2,1)S(1)}, u32[]{:S(2)}, u32[]{:S(2)}) collective-permute-start(bf16[16,32,128]{2,1,0:T(8,128)(2,1)S(1)} %get-tuple-element.33), channel_id=1, source_target_pairs={{0,48},{1,49},{2,50},{3,51},{4,52},{5,53},{6,54},{7,55},{8,56},{9,... | collective-permute-start | bytes 393224 | tf_op jit(solution)/shard_map/ppermute | solution.py:322
  34.2 2.8 %collective-permute-start.8 = (bf16[16,32,128]{2,1,0:T(8,128)(2,1)S(1)}, bf16[16,32,128]{2,1,0:T(8,128)(2,1)S(1)}, u32[]{:S(2)}, u32[]{:S(2)}) collective-permute-start(bf16[16,32,128]{2,1,0:T(8,128)(2,1)S(1)} %get-tuple-element.30), channel_id=1, source_target_pairs={{0,0},{1,1},{2,2},{3,3},{4,4},{5,5},{6,6},{7,7},{8,8},{9,9},{10,10... | collective-permute-start | bytes 393224 | tf_op jit(solution)/shard_map/ppermute | solution.py:322
  37.0 4.8 %collective-permute-start.9 = (bf16[16,32,128]{2,1,0:T(8,128)(2,1)S(1)}, bf16[16,32,128]{2,1,0:T(8,128)(2,1)S(1)}, u32[]{:S(2)}, u32[]{:S(2)}) collective-permute-start(bf16[16,32,128]{2,1,0:T(8,128)(2,1)S(1)} %get-tuple-element.31), channel_id=1, source_target_pairs={{0,16},{1,17},{2,18},{3,19},{4,20},{5,21},{6,22},{7,23},{8,24},{9,... | collective-permute-start | bytes 393224 | tf_op jit(solution)/shard_map/ppermute | solution.py:322
  41.8 0.1 pad_add_fusion.rg_ref
  41.9 3.0 %all-to-all-done.m_ref = bf16[64,32,128]{2,1,0:T(8,128)(2,1)S(1)} async-done(((bf16[64,32,128]{2,1,0:T(8,128)(2,1)}), bf16[64,32,128]{2,1,0:T(8,128)(2,1)S(1)}, u32[]{:S(2)}, u32[]{:S(2)}) %all-to-all-start) | async-done | bytes 524320 | tf_op jit(solution)/shard_map/all_to_all | solution.py:341
  44.8 2.0 %change_rows.1.refs_0_ = bf16[32,8192]{1,0:T(8,128)(2,1)S(1)} custom-call(s32[2]{0:T(128)S(1)} %pad_add_fusion.rg_ref, f32[32,8192]{1,0:T(8,128)S(1)} %get-tuple-element.21.avg_ref, bf16[64,32,128]{2,1,0:T(8,128)(2,1)S(1)} %all-to-all-done.m_ref), custom_call_target="tpu_custom_call" | custom-call | flops 2097152 | bytes 2097152 | tf_op jit(solution)/shard_map/change_rows/pallas_call | solution.py:63
  46.8 4.2 %collective-permute-start.5 = (bf16[32,8192]{1,0:T(8,128)(2,1)S(1)}, bf16[32,8192]{1,0:T(8,128)(2,1)S(1)}, u32[]{:S(2)}, u32[]{:S(2)}) collective-permute-start(bf16[32,8192]{1,0:T(8,128)(2,1)S(1)} %change_rows.1.refs_0_), channel_id=1, source_target_pairs={{0,128},{64,192},{128,0},{192,64},{1,129},{65,193},{129,1},{193,65... | collective-permute-start | bytes 1572872 | tf_op jit(solution)/shard_map/ppermute | solution.py:80
  51.0 0.0 collective-permute-done.10.refs_2_
  51.0 0.0 collective-permute-done.11.refs_3_
  51.0 3.4 %collective-permute-done.8.refs_0_ = bf16[16,32,128]{2,1,0:T(8,128)(2,1)S(1)} collective-permute-done((bf16[16,32,128]{2,1,0:T(8,128)(2,1)S(1)}, bf16[16,32,128]{2,1,0:T(8,128)(2,1)S(1)}, u32[]{:S(2)}, u32[]{:S(2)}) %collective-permute-start.8) | collective-permute-done | bytes 131104 | tf_op jit(solution)/shard_map/ppermute | solution.py:322
  54.4 0.0 collective-permute-done.9.refs_1_
  54.5 0.8 %stack_pieces.1 = bf16[16,4,32,128]{3,2,1,0:T(8,128)(2,1)} custom-call(s32[1]{0:T(128)} %bitcast.r_ref, bf16[16,32,128]{2,1,0:T(8,128)(2,1)S(1)} %collective-permute-done.8.refs_0_, bf16[16,32,128]{2,1,0:T(8,128)(2,1)S(1)} %collective-permute-done.9.refs_1_, bf16[16,32,128]{2,1,0:T(8,128)(2,1)S(1)} %collective-permute-done.10.refs_2_, ...), custom_call_target="tpu_custom_call" | custom-call | flops 2097152 | bytes 2097152 | tf_op jit(solution)/shard_map/stack_pieces/pallas_call | solution.py:63
  55.3 5.8 %all-to-all-start.1 = ((bf16[16,4,32,128]{3,2,1,0:T(8,128)(2,1)}), bf16[16,4,32,128]{3,2,1,0:T(8,128)(2,1)S(1)}, u32[]{:S(2)}, u32[]{:S(2)}) async-start(bf16[16,4,32,128]{3,2,1,0:T(8,128)(2,1)} %stack_pieces.1), calls=%async_computation.1 | async-start | bytes 1048576 | tf_op jit(solution)/shard_map/all_to_all | solution.py:346
  61.1 0.2 collective-permute-start.7
  61.3 0.0 collective-permute-done.5.refs_0_
  61.3 0.4 collective-permute-start.6
  61.7 1.4 %collective-permute-done.7.refs_1_ = bf16[32,8192]{1,0:T(8,128)(2,1)S(1)} collective-permute-done((bf16[32,8192]{1,0:T(8,128)(2,1)S(1)}, bf16[32,8192]{1,0:T(8,128)(2,1)S(1)}, u32[]{:S(2)}, u32[]{:S(2)}) %collective-permute-start.7) | collective-permute-done | bytes 524320 | tf_op jit(solution)/shard_map/ppermute | solution.py:80
  63.1 2.8 %outputs_of.3 = (bf16[128,8192]{1,0:T(8,128)(2,1)}, bf16[128,8192]{1,0:T(8,128)(2,1)}) custom-call(s32[1]{0:T(128)} %bitcast.r_ref, bf16[128,8192]{1,0:T(8,128)(2,1)} %bitcast.8, bf16[128,8192]{1,0:T(8,128)(2,1)} %a_ref.9, bf16[32,8192]{1,0:T(8,128)(2,1)S(1)} %change_rows.1.refs_0_, bf16[32,8192]{1,0:T(8,128)(2,1)S(1)} %collective-permute-done.7.refs_1_), custom_call_target="tpu_custom_call" | custom-call | flops 2097152 | bytes 2097152 | tf_op jit(solution)/shard_map/outputs_of/pallas_call | solution.py:63
  66.0 2.3 %outputs_of.4 = (bf16[128,8192]{1,0:T(8,128)(2,1)}, bf16[128,8192]{1,0:T(8,128)(2,1)}) custom-call(s32[1]{0:T(128)} %bitcast.r_ref, bf16[128,8192]{1,0:T(8,128)(2,1)} %bitcast.9, bf16[128,8192]{1,0:T(8,128)(2,1)} %a_ref.9, bf16[32,8192]{1,0:T(8,128)(2,1)S(1)} %collective-permute-done.5.refs_0_, ...), custom_call_target="tpu_custom_call", output_to_operand_aliasing={{0}: (4, {}), {1}: (5, {})} | custom-call | flops 2097152 | bytes 2097152 | tf_op jit(solution)/shard_map/outputs_of/pallas_call | solution.py:63
  68.3 0.0 collective-permute-done.6.refs_0_
  68.3 0.0 copy-start
  68.3 2.4 %outputs_of.5 = (bf16[128,8192]{1,0:T(8,128)(2,1)}, bf16[128,8192]{1,0:T(8,128)(2,1)}) custom-call(s32[1]{0:T(128)} %bitcast.r_ref, bf16[128,8192]{1,0:T(8,128)(2,1)} %bitcast.10, bf16[128,8192]{1,0:T(8,128)(2,1)} %a_ref.9, bf16[32,8192]{1,0:T(8,128)(2,1)S(1)} %collective-permute-done.6.refs_0_, ...), custom_call_target="tpu_custom_call", output_to_operand_aliasing={{0}: (4, {}), {1}: (5, {})} | custom-call | flops 2097152 | bytes 2097152 | tf_op jit(solution)/shard_map/outputs_of/pallas_call | solution.py:63
  70.6 3.7 %all-to-all-done.1.p_ref = bf16[16,4,32,128]{3,2,1,0:T(8,128)(2,1)S(1)} async-done(((bf16[16,4,32,128]{3,2,1,0:T(8,128)(2,1)}), bf16[16,4,32,128]{3,2,1,0:T(8,128)(2,1)S(1)}, u32[]{:S(2)}, u32[]{:S(2)}) %all-to-all-start.1) | async-done | bytes 524320 | tf_op jit(solution)/shard_map/all_to_all | solution.py:346
  74.3 0.0 copy-done
  74.3 1.7 %new_momentum_of.1 = f32[2048,128]{1,0:T(8,128)} custom-call(s32[2]{0:T(128)S(1)} %pad_add_fusion.rg_ref, bf16[128,8192]{1,0:T(8,128)(2,1)} %get-tuple-element.29.after_ref, bf16[16,4,32,128]{3,2,1,0:T(8,128)(2,1)S(1)} %all-to-all-done.1.p_ref, f32[2048,128]{1,0:T(8,128)S(1)} %copy-done), custom_call_target="tpu_custom_call" | custom-call | flops 2097152 | bytes 2097152 | tf_op jit(solution)/shard_map/new_momentum_of/pallas_call | solution.py:63
Async XLA Ops:
  2.2 2.9 %collective-permute-start = (bf16[64,8192]{1,0:T(8,128)(2,1)S(1)}, bf16[64,8192]{1,0:T(8,128)(2,1)S(1)}, u32[]{:S(2)}, u32[]{:S(2)}) collective-permute-start(bf16[64,8192]{1,0:T(8,128)(2,1)S(1)} %get-tuple-element.19), channel_id=1, source_target_pairs={{0,64},{64,0},{128,192},{192,128},{1,65},{65,1},{129,193},{193,129... | collective-permute-start | bytes 3145736 | tf_op jit(solution)/shard_map/ppermute | solution.py:80
  2.3 6.6 %collective-permute-start.2 = (bf16[16,32,128]{2,1,0:T(8,128)(2,1)S(1)}, bf16[16,32,128]{2,1,0:T(8,128)(2,1)S(1)}, u32[]{:S(2)}, u32[]{:S(2)}) collective-permute-start(bf16[16,32,128]{2,1,0:T(8,128)(2,1)S(1)} %get-tuple-element.22), channel_id=1, source_target_pairs={{0,64},{64,0},{128,192},{192,128},{1,65},{65,1},{129,193},{193,129... | collective-permute-start | bytes 393224 | tf_op jit(solution)/shard_map/ppermute | solution.py:80
  2.8 6.1 %collective-permute-start.3 = (bf16[16,32,128]{2,1,0:T(8,128)(2,1)S(1)}, bf16[16,32,128]{2,1,0:T(8,128)(2,1)S(1)}, u32[]{:S(2)}, u32[]{:S(2)}) collective-permute-start(bf16[16,32,128]{2,1,0:T(8,128)(2,1)S(1)} %get-tuple-element.23), channel_id=1, source_target_pairs={{0,128},{64,192},{128,0},{192,64},{1,129},{65,193},{129,1},{193,65... | collective-permute-start | bytes 393224 | tf_op jit(solution)/shard_map/ppermute | solution.py:80
  5.0 5.8 %collective-permute-start.4 = (bf16[16,32,128]{2,1,0:T(8,128)(2,1)S(1)}, bf16[16,32,128]{2,1,0:T(8,128)(2,1)S(1)}, u32[]{:S(2)}, u32[]{:S(2)}) collective-permute-start(bf16[16,32,128]{2,1,0:T(8,128)(2,1)S(1)} %get-tuple-element.24), channel_id=1, source_target_pairs={{0,196},{1,197},{2,198},{3,199},{4,192},{5,193},{6,194},{7,195},{8... | collective-permute-start | bytes 393224 | tf_op jit(solution)/shard_map/ppermute | solution.py:85
  6.8 18.3 %collective-permute-start.1 = (bf16[32,8192]{1,0:T(8,128)(2,1)S(1)}, bf16[32,8192]{1,0:T(8,128)(2,1)}, u32[]{:S(2)}, u32[]{:S(2)}) collective-permute-start(bf16[32,8192]{1,0:T(8,128)(2,1)S(1)} %partial_for_other.1.after_ref), channel_id=1, source_target_pairs={{0,128},{64,192},{128,0},{192,64},{1,129},{65,193},{129,1},{193,65... | collective-permute-start | bytes 1572872 | tf_op jit(solution)/shard_map/ppermute | solution.py:80
  11.7 33.2 %all-to-all-start = ((bf16[64,32,128]{2,1,0:T(8,128)(2,1)}), bf16[64,32,128]{2,1,0:T(8,128)(2,1)S(1)}, u32[]{:S(2)}, u32[]{:S(2)}) async-start(bf16[64,32,128]{2,1,0:T(8,128)(2,1)} %bitcast.3), calls=%async_computation | async-start | bytes 1048576 | tf_op jit(solution)/shard_map/all_to_all | solution.py:341
  27.8 23.2 %collective-permute-start.10 = (bf16[16,32,128]{2,1,0:T(8,128)(2,1)}, bf16[16,32,128]{2,1,0:T(8,128)(2,1)S(1)}, u32[]{:S(2)}, u32[]{:S(2)}) collective-permute-start(bf16[16,32,128]{2,1,0:T(8,128)(2,1)} %get-tuple-element.32), channel_id=1, source_target_pairs={{0,32},{1,33},{2,34},{3,35},{4,36},{5,37},{6,38},{7,39},{8,40},{9,... | collective-permute-start | bytes 393224 | tf_op jit(solution)/shard_map/ppermute | solution.py:322
  29.5 21.5 %collective-permute-start.11 = (bf16[16,32,128]{2,1,0:T(8,128)(2,1)S(1)}, bf16[16,32,128]{2,1,0:T(8,128)(2,1)S(1)}, u32[]{:S(2)}, u32[]{:S(2)}) collective-permute-start(bf16[16,32,128]{2,1,0:T(8,128)(2,1)S(1)} %get-tuple-element.33), channel_id=1, source_target_pairs={{0,48},{1,49},{2,50},{3,51},{4,52},{5,53},{6,54},{7,55},{8,56},{9,... | collective-permute-start | bytes 393224 | tf_op jit(solution)/shard_map/ppermute | solution.py:322
  34.2 20.3 %collective-permute-start.8 = (bf16[16,32,128]{2,1,0:T(8,128)(2,1)S(1)}, bf16[16,32,128]{2,1,0:T(8,128)(2,1)S(1)}, u32[]{:S(2)}, u32[]{:S(2)}) collective-permute-start(bf16[16,32,128]{2,1,0:T(8,128)(2,1)S(1)} %get-tuple-element.30), channel_id=1, source_target_pairs={{0,0},{1,1},{2,2},{3,3},{4,4},{5,5},{6,6},{7,7},{8,8},{9,9},{10,10... | collective-permute-start | bytes 393224 | tf_op jit(solution)/shard_map/ppermute | solution.py:322
  37.0 17.4 %collective-permute-start.9 = (bf16[16,32,128]{2,1,0:T(8,128)(2,1)S(1)}, bf16[16,32,128]{2,1,0:T(8,128)(2,1)S(1)}, u32[]{:S(2)}, u32[]{:S(2)}) collective-permute-start(bf16[16,32,128]{2,1,0:T(8,128)(2,1)S(1)} %get-tuple-element.31), channel_id=1, source_target_pairs={{0,16},{1,17},{2,18},{3,19},{4,20},{5,21},{6,22},{7,23},{8,24},{9,... | collective-permute-start | bytes 393224 | tf_op jit(solution)/shard_map/ppermute | solution.py:322
  46.8 14.5 %collective-permute-start.5 = (bf16[32,8192]{1,0:T(8,128)(2,1)S(1)}, bf16[32,8192]{1,0:T(8,128)(2,1)S(1)}, u32[]{:S(2)}, u32[]{:S(2)}) collective-permute-start(bf16[32,8192]{1,0:T(8,128)(2,1)S(1)} %change_rows.1.refs_0_), channel_id=1, source_target_pairs={{0,128},{64,192},{128,0},{192,64},{1,129},{65,193},{129,1},{193,65... | collective-permute-start | bytes 1572872 | tf_op jit(solution)/shard_map/ppermute | solution.py:80
  55.3 19.0 %all-to-all-start.1 = ((bf16[16,4,32,128]{3,2,1,0:T(8,128)(2,1)}), bf16[16,4,32,128]{3,2,1,0:T(8,128)(2,1)S(1)}, u32[]{:S(2)}, u32[]{:S(2)}) async-start(bf16[16,4,32,128]{3,2,1,0:T(8,128)(2,1)} %stack_pieces.1), calls=%async_computation.1 | async-start | bytes 1048576 | tf_op jit(solution)/shard_map/all_to_all | solution.py:346
  61.1 2.0 %collective-permute-start.7 = (bf16[32,8192]{1,0:T(8,128)(2,1)S(1)}, bf16[32,8192]{1,0:T(8,128)(2,1)S(1)}, u32[]{:S(2)}, u32[]{:S(2)}) collective-permute-start(bf16[32,8192]{1,0:T(8,128)(2,1)S(1)} %change_rows.1.refs_0_), channel_id=1, source_target_pairs={{0,64},{64,0},{128,192},{192,128},{1,65},{65,1},{129,193},{193,129... | collective-permute-start | bytes 1572872 | tf_op jit(solution)/shard_map/ppermute | solution.py:80
  61.3 6.9 %collective-permute-start.6 = (bf16[32,8192]{1,0:T(8,128)(2,1)S(1)}, bf16[32,8192]{1,0:T(8,128)(2,1)S(1)}, u32[]{:S(2)}, u32[]{:S(2)}) collective-permute-start(bf16[32,8192]{1,0:T(8,128)(2,1)S(1)} %collective-permute-done.5.refs_0_), channel_id=1, source_target_pairs={{0,64},{64,0},{128,192},{192,128},{1,65},{65,1},{129,193},{193,129... | collective-permute-start | bytes 1572872 | tf_op jit(solution)/shard_map/ppermute | solution.py:80
  68.3 6.1 %copy-start = (f32[2048,128]{1,0:T(8,128)S(1)}, f32[2048,128]{1,0:T(8,128)}, u32[]{:S(2)}) copy-start(f32[2048,128]{1,0:T(8,128)} %m_ref.3) | copy-start | bytes 3145732

commit v4 on v3

--- a/solution.py
+++ b/solution.py
@@ -112,10 +112,10 @@
 def in_order(r, pieces, after):
     def body(r_ref, after_ref, *refs):
         for k in range(4):
-            refs[4][peer(r_ref[0], k)] = refs[k][...]
-
-    return call(
-        body, "in_order", LONG, shape(4, 16, 32, 128), [r, after, *pieces], [], 1,
+            refs[4][peer(r_ref[0], k)] = refs[3 - k][...]
+
+    return call(
+        body, "in_order", LONG, shape(4, 16, 32, 128), [r, after, *pieces[::-1]], [], 1,
         near=2, out_near=True,
     )
 

time: 76.5 us -> 75.4 us (0.986)
  waiting for transfers between devices: 13.4 us -> 11 us
  starting transfers between devices: 43 us -> 44.3 us
    ppermute x1, waiting for transfers between devices: 1.88 us -> 0.01 us  [swap_around(): return lax.ppermute(x, ('replica', 'fsdp'), pairs)]
    ppermute x1, starting transfers between devices: 0.1 us -> 1.7 us  [swap_around(): return lax.ppermute(x, ('replica', 'fsdp'), pairs)]
    ppermute x4, waiting for transfers between devices: 3.43 us -> 2.07 us  [across(): return lax.ppermute(x, ('replica', 'fsdp'), pairs)]
  transfers between devices with their start and end apart: 14 -> 14, of which waited for: 5 -> 5; matrix products, arithmetic and copies ran while one was open for 0% -> 0% of each run, Pallas kernels for 20% -> 21%
where the time goes in v4:
time: 75.4 us; the launch traced here: 75 us
  starting transfers between devices  44.3 us (59%)
  Pallas kernels  18.8 us (25%)
  waiting for transfers between devices  11 us (15%)
  between operations  0.77 us (1%)
    pallas_call x10, Pallas kernels, call(): pl.pallas_call(body, out_shape=outs, in_specs=[pl.BlockSpec(memory_space=...  18.8 us
    ppermute x4, starting transfers between devices, across(): return lax.ppermute(x, ('replica', 'fsdp'), pairs)  14.4 us
    all_to_all x1, starting transfers between devices, local(): m_rows = lax.all_to_all(by_row, 'fsdp', 0, 0, tiled=True)  12.9 us
    ppermute x7, starting transfers between devices, swap(): return lax.ppermute(x, 'replica', [(i, i ^ k) for i in range(4)])  9.21 us
    all_to_all x1, starting transfers between devices, local(): lax.all_to_all(cut, 'fsdp', 0, 0, axis_index_groups=groups, tiled=True)  6.12 us
    all_to_all x1, waiting for transfers between devices, local(): lax.all_to_all(cut, 'fsdp', 0, 0, axis_index_groups=groups, tiled=True)  3.99 us
    all_to_all x1, waiting for transfers between devices, local(): m_rows = lax.all_to_all(by_row, 'fsdp', 0, 0, tiled=True)  2.83 us
    ppermute x7, waiting for transfers between devices, swap(): return lax.ppermute(x, 'replica', [(i, i ^ k) for i in range(4)])  2.14 us
  transfers between devices with their start and end apart: 14, of which 5 were waited for; matrix products, arithmetic and copies ran while one was open for 0% of the time, Pallas kernels for 21%

profile of v4, /device:TPU:8, one launch (start us, length us, event | category | flops | bytes accessed | tf_op | source)
XLA Modules:
  0.0 75.0 jit_solution(7800146629012240338)
XLA Ops:
  0.6 1.6 %prologue.1 = (bf16[64,8192]{1,0:T(8,128)(2,1)S(1)}, bf16[16,32,128]{2,1,0:T(8,128)(2,1)S(1)}, bf16[16,32,128]{2,1,0:T(8,128)(2,1)S(1)}, bf16[16,32,128]{2,1,0:T(8,128)(2,1)S(1)}, bf16[16,32,128]{2,1,0:T(8,128)(2,1)S(1)}) custom-call(s32[1]{0:T(128)} %bitcast.r_ref, bf16[128,8192]{1,0:T(8,128)(2,1)} %bitcast.5, f32[2048,128]{1,0:T(8,128)} %m_ref.3), custom_call_target="tpu_custom_call" | custom-call | flops 2097152 | bytes 2097152 | tf_op jit(solution)/shard_map/prologue/pallas_call | solution.py:63
  2.2 0.1 collective-permute-start
  2.3 1.7 %collective-permute-start.2 = (bf16[16,32,128]{2,1,0:T(8,128)(2,1)S(1)}, bf16[16,32,128]{2,1,0:T(8,128)(2,1)S(1)}, u32[]{:S(2)}, u32[]{:S(2)}) collective-permute-start(bf16[16,32,128]{2,1,0:T(8,128)(2,1)S(1)} %get-tuple-element.22), channel_id=1, source_target_pairs={{0,196},{1,197},{2,198},{3,199},{4,192},{5,193},{6,194},{7,195},{8... | collective-permute-start | bytes 393224 | tf_op jit(solution)/shard_map/ppermute | solution.py:85
  4.0 1.9 %collective-permute-start.3 = (bf16[16,32,128]{2,1,0:T(8,128)(2,1)S(1)}, bf16[16,32,128]{2,1,0:T(8,128)(2,1)S(1)}, u32[]{:S(2)}, u32[]{:S(2)}) collective-permute-start(bf16[16,32,128]{2,1,0:T(8,128)(2,1)S(1)} %get-tuple-element.23), channel_id=1, source_target_pairs={{0,128},{64,192},{128,0},{192,64},{1,129},{65,193},{129,1},{193,65... | collective-permute-start | bytes 393224 | tf_op jit(solution)/shard_map/ppermute | solution.py:80
  5.9 0.0 collective-permute-start.4
  5.9 0.0 collective-permute-done.t_ref
  5.9 1.7 %partial_for_other.1.after_ref = bf16[32,8192]{1,0:T(8,128)(2,1)S(1)} custom-call(s32[1]{0:T(128)} %bitcast.r_ref, bf16[128,8192]{1,0:T(8,128)(2,1)} %bitcast.6, bf16[64,8192]{1,0:T(8,128)(2,1)S(1)} %collective-permute-done.t_ref, bf16[128,8192]{1,0:T(8,128)(2,1)} %a_ref.9, bf16[16,32,128]{2,1,0:T(8,128)(2,1)S(1)} %get-tuple-element.20.after_ref.refs_3_), custom_call_target="tpu_custom_call" | custom-call | flops 2097152 | bytes 2097152 | tf_op jit(solution)/shard_map/partial_for_other/pallas_call | solution.py:63
  7.6 1.3 %collective-permute-start.1 = (bf16[32,8192]{1,0:T(8,128)(2,1)S(1)}, bf16[32,8192]{1,0:T(8,128)(2,1)}, u32[]{:S(2)}, u32[]{:S(2)}) collective-permute-start(bf16[32,8192]{1,0:T(8,128)(2,1)S(1)} %partial_for_other.1.after_ref), channel_id=1, source_target_pairs={{0,128},{64,192},{128,0},{192,64},{1,129},{65,193},{129,1},{193,65... | collective-permute-start | bytes 1572872 | tf_op jit(solution)/shard_map/ppermute | solution.py:80
  8.9 0.0 collective-permute-done.2.refs_0_
  8.9 0.7 collective-permute-done.3.refs_1_
  9.7 0.0 collective-permute-done.4.refs_2_
  9.7 0.8 %in_order.1 = bf16[4,16,32,128]{3,2,1,0:T(8,128)(2,1)} custom-call(s32[1]{0:T(128)} %bitcast.r_ref, bf16[32,8192]{1,0:T(8,128)(2,1)S(1)} %partial_for_other.1.after_ref, bf16[16,32,128]{2,1,0:T(8,128)(2,1)S(1)} %collective-permute-done.2.refs_0_, bf16[16,32,128]{2,1,0:T(8,128)(2,1)S(1)} %collective-permute-done.3.refs_1_, ...), custom_call_target="tpu_custom_call" | custom-call | flops 17179869184 | bytes 17179869184 | tf_op jit(solution)/shard_map/in_order/pallas_call | solution.py:63
  10.5 12.9 %all-to-all-start = ((bf16[64,32,128]{2,1,0:T(8,128)(2,1)}), bf16[64,32,128]{2,1,0:T(8,128)(2,1)S(1)}, u32[]{:S(2)}, u32[]{:S(2)}) async-start(bf16[64,32,128]{2,1,0:T(8,128)(2,1)} %bitcast.3), calls=%async_computation | async-start | bytes 1048576 | tf_op jit(solution)/shard_map/all_to_all | solution.py:341
  23.4 0.0 collective-permute-done.1.p_ref
  23.4 2.6 %average_rows.1 = (f32[32,8192]{1,0:T(8,128)S(1)}, bf16[16,32,128]{2,1,0:T(8,128)(2,1)S(1)}, bf16[16,32,128]{2,1,0:T(8,128)(2,1)S(1)}, bf16[16,32,128]{2,1,0:T(8,128)(2,1)}, bf16[16,32,128]{2,1,0:T(8,128)(2,1)S(1)}) custom-call(s32[1]{0:T(128)} %bitcast.r_ref, bf16[128,8192]{1,0:T(8,128)(2,1)} %bitcast.7, bf16[64,8192]{1,0:T(8,128)(2,1)S(1)} %collective-permute-done.t_ref, ...), custom_call_target="tpu_custom_call" | custom-call | flops 17179869184 | bytes 17179869184 | tf_op jit(solution)/shard_map/average_rows/pallas_call | solution.py:63
  26.1 2.1 %collective-permute-start.10 = (bf16[16,32,128]{2,1,0:T(8,128)(2,1)}, bf16[16,32,128]{2,1,0:T(8,128)(2,1)S(1)}, u32[]{:S(2)}, u32[]{:S(2)}) collective-permute-start(bf16[16,32,128]{2,1,0:T(8,128)(2,1)} %get-tuple-element.32), channel_id=1, source_target_pairs={{0,32},{1,33},{2,34},{3,35},{4,36},{5,37},{6,38},{7,39},{8,40},{9,... | collective-permute-start | bytes 393224 | tf_op jit(solution)/shard_map/ppermute | solution.py:322
  28.2 4.3 %collective-permute-start.11 = (bf16[16,32,128]{2,1,0:T(8,128)(2,1)S(1)}, bf16[16,32,128]{2,1,0:T(8,128)(2,1)S(1)}, u32[]{:S(2)}, u32[]{:S(2)}) collective-permute-start(bf16[16,32,128]{2,1,0:T(8,128)(2,1)S(1)} %get-tuple-element.33), channel_id=1, source_target_pairs={{0,48},{1,49},{2,50},{3,51},{4,52},{5,53},{6,54},{7,55},{8,56},{9,... | collective-permute-start | bytes 393224 | tf_op jit(solution)/shard_map/ppermute | solution.py:322
  32.5 3.9 %collective-permute-start.8 = (bf16[16,32,128]{2,1,0:T(8,128)(2,1)S(1)}, bf16[16,32,128]{2,1,0:T(8,128)(2,1)S(1)}, u32[]{:S(2)}, u32[]{:S(2)}) collective-permute-start(bf16[16,32,128]{2,1,0:T(8,128)(2,1)S(1)} %get-tuple-element.30), channel_id=1, source_target_pairs={{0,0},{1,1},{2,2},{3,3},{4,4},{5,5},{6,6},{7,7},{8,8},{9,9},{10,10... | collective-permute-start | bytes 393224 | tf_op jit(solution)/shard_map/ppermute | solution.py:322
  36.4 4.1 %collective-permute-start.9 = (bf16[16,32,128]{2,1,0:T(8,128)(2,1)S(1)}, bf16[16,32,128]{2,1,0:T(8,128)(2,1)S(1)}, u32[]{:S(2)}, u32[]{:S(2)}) collective-permute-start(bf16[16,32,128]{2,1,0:T(8,128)(2,1)S(1)} %get-tuple-element.31), channel_id=1, source_target_pairs={{0,16},{1,17},{2,18},{3,19},{4,20},{5,21},{6,22},{7,23},{8,24},{9,... | collective-permute-start | bytes 393224 | tf_op jit(solution)/shard_map/ppermute | solution.py:322
  40.5 0.1 pad_add_fusion.rg_ref
  40.5 2.8 %all-to-all-done.m_ref = bf16[64,32,128]{2,1,0:T(8,128)(2,1)S(1)} async-done(((bf16[64,32,128]{2,1,0:T(8,128)(2,1)}), bf16[64,32,128]{2,1,0:T(8,128)(2,1)S(1)}, u32[]{:S(2)}, u32[]{:S(2)}) %all-to-all-start) | async-done | bytes 524320 | tf_op jit(solution)/shard_map/all_to_all | solution.py:341
  43.4 2.0 %change_rows.1.refs_0_ = bf16[32,8192]{1,0:T(8,128)(2,1)S(1)} custom-call(s32[2]{0:T(128)S(1)} %pad_add_fusion.rg_ref, f32[32,8192]{1,0:T(8,128)S(1)} %get-tuple-element.21.avg_ref, bf16[64,32,128]{2,1,0:T(8,128)(2,1)S(1)} %all-to-all-done.m_ref), custom_call_target="tpu_custom_call" | custom-call | flops 2097152 | bytes 2097152 | tf_op jit(solution)/shard_map/change_rows/pallas_call | solution.py:63
  45.4 5.3 %collective-permute-start.5 = (bf16[32,8192]{1,0:T(8,128)(2,1)S(1)}, bf16[32,8192]{1,0:T(8,128)(2,1)S(1)}, u32[]{:S(2)}, u32[]{:S(2)}) collective-permute-start(bf16[32,8192]{1,0:T(8,128)(2,1)S(1)} %change_rows.1.refs_0_), channel_id=1, source_target_pairs={{0,128},{64,192},{128,0},{192,64},{1,129},{65,193},{129,1},{193,65... | collective-permute-start | bytes 1572872 | tf_op jit(solution)/shard_map/ppermute | solution.py:80
  50.7 0.0 collective-permute-done.10.refs_2_
  50.7 0.0 collective-permute-done.11.refs_3_
  50.7 2.1 %collective-permute-done.8.refs_0_ = bf16[16,32,128]{2,1,0:T(8,128)(2,1)S(1)} collective-permute-done((bf16[16,32,128]{2,1,0:T(8,128)(2,1)S(1)}, bf16[16,32,128]{2,1,0:T(8,128)(2,1)S(1)}, u32[]{:S(2)}, u32[]{:S(2)}) %collective-permute-start.8) | collective-permute-done | bytes 131104 | tf_op jit(solution)/shard_map/ppermute | solution.py:322
  52.8 0.0 collective-permute-done.9.refs_1_
  52.8 0.8 %stack_pieces.1 = bf16[16,4,32,128]{3,2,1,0:T(8,128)(2,1)} custom-call(s32[1]{0:T(128)} %bitcast.r_ref, bf16[16,32,128]{2,1,0:T(8,128)(2,1)S(1)} %collective-permute-done.8.refs_0_, bf16[16,32,128]{2,1,0:T(8,128)(2,1)S(1)} %collective-permute-done.9.refs_1_, bf16[16,32,128]{2,1,0:T(8,128)(2,1)S(1)} %collective-permute-done.10.refs_2_, ...), custom_call_target="tpu_custom_call" | custom-call | flops 2097152 | bytes 2097152 | tf_op jit(solution)/shard_map/stack_pieces/pallas_call | solution.py:63
  53.6 6.1 %all-to-all-start.1 = ((bf16[16,4,32,128]{3,2,1,0:T(8,128)(2,1)}), bf16[16,4,32,128]{3,2,1,0:T(8,128)(2,1)S(1)}, u32[]{:S(2)}, u32[]{:S(2)}) async-start(bf16[16,4,32,128]{3,2,1,0:T(8,128)(2,1)} %stack_pieces.1), calls=%async_computation.1 | async-start | bytes 1048576 | tf_op jit(solution)/shard_map/all_to_all | solution.py:346
  59.7 0.5 collective-permute-start.7
  60.2 0.0 collective-permute-done.5.refs_0_
  60.2 0.1 collective-permute-start.6
  60.3 1.4 %collective-permute-done.7.refs_1_ = bf16[32,8192]{1,0:T(8,128)(2,1)S(1)} collective-permute-done((bf16[32,8192]{1,0:T(8,128)(2,1)S(1)}, bf16[32,8192]{1,0:T(8,128)(2,1)S(1)}, u32[]{:S(2)}, u32[]{:S(2)}) %collective-permute-start.7) | collective-permute-done | bytes 524320 | tf_op jit(solution)/shard_map/ppermute | solution.py:80
  61.7 2.8 %outputs_of.3 = (bf16[128,8192]{1,0:T(8,128)(2,1)}, bf16[128,8192]{1,0:T(8,128)(2,1)}) custom-call(s32[1]{0:T(128)} %bitcast.r_ref, bf16[128,8192]{1,0:T(8,128)(2,1)} %bitcast.8, bf16[128,8192]{1,0:T(8,128)(2,1)} %a_ref.9, bf16[32,8192]{1,0:T(8,128)(2,1)S(1)} %change_rows.1.refs_0_, bf16[32,8192]{1,0:T(8,128)(2,1)S(1)} %collective-permute-done.7.refs_1_), custom_call_target="tpu_custom_call" | custom-call | flops 2097152 | bytes 2097152 | tf_op jit(solution)/shard_map/outputs_of/pallas_call | solution.py:63
  64.6 2.3 %outputs_of.4 = (bf16[128,8192]{1,0:T(8,128)(2,1)}, bf16[128,8192]{1,0:T(8,128)(2,1)}) custom-call(s32[1]{0:T(128)} %bitcast.r_ref, bf16[128,8192]{1,0:T(8,128)(2,1)} %bitcast.9, bf16[128,8192]{1,0:T(8,128)(2,1)} %a_ref.9, bf16[32,8192]{1,0:T(8,128)(2,1)S(1)} %collective-permute-done.5.refs_0_, ...), custom_call_target="tpu_custom_call", output_to_operand_aliasing={{0}: (4, {}), {1}: (5, {})} | custom-call | flops 2097152 | bytes 2097152 | tf_op jit(solution)/shard_map/outputs_of/pallas_call | solution.py:63
  66.9 0.0 collective-permute-done.6.refs_0_
  66.9 0.0 copy-start
  66.9 2.4 %outputs_of.5 = (bf16[128,8192]{1,0:T(8,128)(2,1)}, bf16[128,8192]{1,0:T(8,128)(2,1)}) custom-call(s32[1]{0:T(128)} %bitcast.r_ref, bf16[128,8192]{1,0:T(8,128)(2,1)} %bitcast.10, bf16[128,8192]{1,0:T(8,128)(2,1)} %a_ref.9, bf16[32,8192]{1,0:T(8,128)(2,1)S(1)} %collective-permute-done.6.refs_0_, ...), custom_call_target="tpu_custom_call", output_to_operand_aliasing={{0}: (4, {}), {1}: (5, {})} | custom-call | flops 2097152 | bytes 2097152 | tf_op jit(solution)/shard_map/outputs_of/pallas_call | solution.py:63
  69.3 4.0 %all-to-all-done.1.p_ref = bf16[16,4,32,128]{3,2,1,0:T(8,128)(2,1)S(1)} async-done(((bf16[16,4,32,128]{3,2,1,0:T(8,128)(2,1)}), bf16[16,4,32,128]{3,2,1,0:T(8,128)(2,1)S(1)}, u32[]{:S(2)}, u32[]{:S(2)}) %all-to-all-start.1) | async-done | bytes 524320 | tf_op jit(solution)/shard_map/all_to_all | solution.py:346
  73.2 0.0 copy-done
  73.3 1.7 %new_momentum_of.1 = f32[2048,128]{1,0:T(8,128)} custom-call(s32[2]{0:T(128)S(1)} %pad_add_fusion.rg_ref, bf16[128,8192]{1,0:T(8,128)(2,1)} %get-tuple-element.29.after_ref, bf16[16,4,32,128]{3,2,1,0:T(8,128)(2,1)S(1)} %all-to-all-done.1.p_ref, f32[2048,128]{1,0:T(8,128)S(1)} %copy-done), custom_call_target="tpu_custom_call" | custom-call | flops 2097152 | bytes 2097152 | tf_op jit(solution)/shard_map/new_momentum_of/pallas_call | solution.py:63
Async XLA Ops:
  2.2 3.7 %collective-permute-start = (bf16[64,8192]{1,0:T(8,128)(2,1)S(1)}, bf16[64,8192]{1,0:T(8,128)(2,1)S(1)}, u32[]{:S(2)}, u32[]{:S(2)}) collective-permute-start(bf16[64,8192]{1,0:T(8,128)(2,1)S(1)} %get-tuple-element.19), channel_id=1, source_target_pairs={{0,64},{64,0},{128,192},{192,128},{1,65},{65,1},{129,193},{193,129... | collective-permute-start | bytes 3145736 | tf_op jit(solution)/shard_map/ppermute | solution.py:80
  2.3 6.6 %collective-permute-start.2 = (bf16[16,32,128]{2,1,0:T(8,128)(2,1)S(1)}, bf16[16,32,128]{2,1,0:T(8,128)(2,1)S(1)}, u32[]{:S(2)}, u32[]{:S(2)}) collective-permute-start(bf16[16,32,128]{2,1,0:T(8,128)(2,1)S(1)} %get-tuple-element.22), channel_id=1, source_target_pairs={{0,196},{1,197},{2,198},{3,199},{4,192},{5,193},{6,194},{7,195},{8... | collective-permute-start | bytes 393224 | tf_op jit(solution)/shard_map/ppermute | solution.py:85
  4.0 5.6 %collective-permute-start.3 = (bf16[16,32,128]{2,1,0:T(8,128)(2,1)S(1)}, bf16[16,32,128]{2,1,0:T(8,128)(2,1)S(1)}, u32[]{:S(2)}, u32[]{:S(2)}) collective-permute-start(bf16[16,32,128]{2,1,0:T(8,128)(2,1)S(1)} %get-tuple-element.23), channel_id=1, source_target_pairs={{0,128},{64,192},{128,0},{192,64},{1,129},{65,193},{129,1},{193,65... | collective-permute-start | bytes 393224 | tf_op jit(solution)/shard_map/ppermute | solution.py:80
  5.9 3.7 %collective-permute-start.4 = (bf16[16,32,128]{2,1,0:T(8,128)(2,1)S(1)}, bf16[16,32,128]{2,1,0:T(8,128)(2,1)S(1)}, u32[]{:S(2)}, u32[]{:S(2)}) collective-permute-start(bf16[16,32,128]{2,1,0:T(8,128)(2,1)S(1)} %get-tuple-element.24), channel_id=1, source_target_pairs={{0,64},{64,0},{128,192},{192,128},{1,65},{65,1},{129,193},{193,129... | collective-permute-start | bytes 393224 | tf_op jit(solution)/shard_map/ppermute | solution.py:80
  7.6 15.8 %collective-permute-start.1 = (bf16[32,8192]{1,0:T(8,128)(2,1)S(1)}, bf16[32,8192]{1,0:T(8,128)(2,1)}, u32[]{:S(2)}, u32[]{:S(2)}) collective-permute-start(bf16[32,8192]{1,0:T(8,128)(2,1)S(1)} %partial_for_other.1.after_ref), channel_id=1, source_target_pairs={{0,128},{64,192},{128,0},{192,64},{1,129},{65,193},{129,1},{193,65... | collective-permute-start | bytes 1572872 | tf_op jit(solution)/shard_map/ppermute | solution.py:80
  10.5 32.9 %all-to-all-start = ((bf16[64,32,128]{2,1,0:T(8,128)(2,1)}), bf16[64,32,128]{2,1,0:T(8,128)(2,1)S(1)}, u32[]{:S(2)}, u32[]{:S(2)}) async-start(bf16[64,32,128]{2,1,0:T(8,128)(2,1)} %bitcast.3), calls=%async_computation | async-start | bytes 1048576 | tf_op jit(solution)/shard_map/all_to_all | solution.py:341
  26.1 24.6 %collective-permute-start.10 = (bf16[16,32,128]{2,1,0:T(8,128)(2,1)}, bf16[16,32,128]{2,1,0:T(8,128)(2,1)S(1)}, u32[]{:S(2)}, u32[]{:S(2)}) collective-permute-start(bf16[16,32,128]{2,1,0:T(8,128)(2,1)} %get-tuple-element.32), channel_id=1, source_target_pairs={{0,32},{1,33},{2,34},{3,35},{4,36},{5,37},{6,38},{7,39},{8,40},{9,... | collective-permute-start | bytes 393224 | tf_op jit(solution)/shard_map/ppermute | solution.py:322
  28.2 22.5 %collective-permute-start.11 = (bf16[16,32,128]{2,1,0:T(8,128)(2,1)S(1)}, bf16[16,32,128]{2,1,0:T(8,128)(2,1)S(1)}, u32[]{:S(2)}, u32[]{:S(2)}) collective-permute-start(bf16[16,32,128]{2,1,0:T(8,128)(2,1)S(1)} %get-tuple-element.33), channel_id=1, source_target_pairs={{0,48},{1,49},{2,50},{3,51},{4,52},{5,53},{6,54},{7,55},{8,56},{9,... | collective-permute-start | bytes 393224 | tf_op jit(solution)/shard_map/ppermute | solution.py:322
  32.5 20.3 %collective-permute-start.8 = (bf16[16,32,128]{2,1,0:T(8,128)(2,1)S(1)}, bf16[16,32,128]{2,1,0:T(8,128)(2,1)S(1)}, u32[]{:S(2)}, u32[]{:S(2)}) collective-permute-start(bf16[16,32,128]{2,1,0:T(8,128)(2,1)S(1)} %get-tuple-element.30), channel_id=1, source_target_pairs={{0,0},{1,1},{2,2},{3,3},{4,4},{5,5},{6,6},{7,7},{8,8},{9,9},{10,10... | collective-permute-start | bytes 393224 | tf_op jit(solution)/shard_map/ppermute | solution.py:322
  36.4 16.4 %collective-permute-start.9 = (bf16[16,32,128]{2,1,0:T(8,128)(2,1)S(1)}, bf16[16,32,128]{2,1,0:T(8,128)(2,1)S(1)}, u32[]{:S(2)}, u32[]{:S(2)}) collective-permute-start(bf16[16,32,128]{2,1,0:T(8,128)(2,1)S(1)} %get-tuple-element.31), channel_id=1, source_target_pairs={{0,16},{1,17},{2,18},{3,19},{4,20},{5,21},{6,22},{7,23},{8,24},{9,... | collective-permute-start | bytes 393224 | tf_op jit(solution)/shard_map/ppermute | solution.py:322
  45.4 14.8 %collective-permute-start.5 = (bf16[32,8192]{1,0:T(8,128)(2,1)S(1)}, bf16[32,8192]{1,0:T(8,128)(2,1)S(1)}, u32[]{:S(2)}, u32[]{:S(2)}) collective-permute-start(bf16[32,8192]{1,0:T(8,128)(2,1)S(1)} %change_rows.1.refs_0_), channel_id=1, source_target_pairs={{0,128},{64,192},{128,0},{192,64},{1,129},{65,193},{129,1},{193,65... | collective-permute-start | bytes 1572872 | tf_op jit(solution)/shard_map/ppermute | solution.py:80
  53.6 19.6 %all-to-all-start.1 = ((bf16[16,4,32,128]{3,2,1,0:T(8,128)(2,1)}), bf16[16,4,32,128]{3,2,1,0:T(8,128)(2,1)S(1)}, u32[]{:S(2)}, u32[]{:S(2)}) async-start(bf16[16,4,32,128]{3,2,1,0:T(8,128)(2,1)} %stack_pieces.1), calls=%async_computation.1 | async-start | bytes 1048576 | tf_op jit(solution)/shard_map/all_to_all | solution.py:346
  59.7 2.0 %collective-permute-start.7 = (bf16[32,8192]{1,0:T(8,128)(2,1)S(1)}, bf16[32,8192]{1,0:T(8,128)(2,1)S(1)}, u32[]{:S(2)}, u32[]{:S(2)}) collective-permute-start(bf16[32,8192]{1,0:T(8,128)(2,1)S(1)} %change_rows.1.refs_0_), channel_id=1, source_target_pairs={{0,64},{64,0},{128,192},{192,128},{1,65},{65,1},{129,193},{193,129... | collective-permute-start | bytes 1572872 | tf_op jit(solution)/shard_map/ppermute | solution.py:80
  60.2 6.7 %collective-permute-start.6 = (bf16[32,8192]{1,0:T(8,128)(2,1)S(1)}, bf16[32,8192]{1,0:T(8,128)(2,1)S(1)}, u32[]{:S(2)}, u32[]{:S(2)}) collective-permute-start(bf16[32,8192]{1,0:T(8,128)(2,1)S(1)} %collective-permute-done.5.refs_0_), channel_id=1, source_target_pairs={{0,64},{64,0},{128,192},{192,128},{1,65},{65,1},{129,193},{193,129... | collective-permute-start | bytes 1572872 | tf_op jit(solution)/shard_map/ppermute | solution.py:80
  66.9 6.4 %copy-start = (f32[2048,128]{1,0:T(8,128)S(1)}, f32[2048,128]{1,0:T(8,128)}, u32[]{:S(2)}) copy-start(f32[2048,128]{1,0:T(8,128)} %m_ref.3) | copy-start | bytes 3145732

commit v5 on v4

--- a/solution.py
+++ b/solution.py
@@ -53,6 +53,11 @@
             copy.wait()
 
 
+class Place:
+    def __getitem__(self, i):
+        return lax.axis_index("fsdp") // 16 if i else lax.axis_index("replica")
+
+
 def call(body, name, cost, outs, args, scratch, copies, aliases=None, near=None, out_near=False):
     anywhere = pl.BlockSpec(memory_space=pl.ANY)
     whole = pl.BlockSpec(memory_space=pltpu.VMEM)
@@ -61,11 +66,9 @@
     single = not isinstance(outs, list)
     count = 1 if single else len(outs)
     return pl.pallas_call(
-        body,
+        lambda *refs: body(Place(), *refs),
         out_shape=outs,
-        in_specs=[pl.BlockSpec(memory_space=pltpu.SMEM)]
-        + [anywhere] * (near - 1)
-        + [whole] * (len(args) - near),
+        in_specs=[anywhere] * near + [whole] * (len(args) - near),
         out_specs=out_spec if single else [out_spec] * count,
         scratch_shapes=[pltpu.VMEM(x.shape, x.dtype) for x in scratch]
         + [pltpu.SemaphoreType.DMA((copies,))],
@@ -85,7 +88,7 @@
     return lax.ppermute(x, ("replica", "fsdp"), pairs)
 
 
-def prologue(r, local, momentum):
+def prologue(local, momentum):
     def body(r_ref, l_ref, m_ref, half_ref, *refs):
         outs, (m, sems) = refs[:4], refs[4:]
         copies = Copies(sems)
@@ -105,26 +108,28 @@
 
     return call(
         body, "prologue", SHORT, [shape(64, 8192)] + [shape(16, 32, 128)] * 4,
-        [r, local, momentum], [shape(2048, 128, dtype=F32)], 5, out_near=True,
-    )
-
-
-def in_order(r, pieces, after):
+        [local, momentum], [shape(2048, 128, dtype=F32)], 5, out_near=True,
+    )
+
+
+def in_order(pieces, after):
     def body(r_ref, after_ref, *refs):
         for k in range(4):
             refs[4][peer(r_ref[0], k)] = refs[3 - k][...]
 
     return call(
-        body, "in_order", LONG, shape(4, 16, 32, 128), [r, after, *pieces[::-1]], [], 1,
-        near=2, out_near=True,
+        body, "in_order", LONG, shape(4, 16, 32, 128), [after, *pieces[::-1]], [], 1,
+        near=1, out_near=True,
     )
 
 
 def inner(step):
-    lax.fori_loop(0, WIDTH // INNER, lambda i, c: (step(at(i * INNER, INNER)), c)[1], 0)
-
-
-def partial_for_other(r, local, theirs, anchor, after):
+    lax.fori_loop(
+        0, WIDTH // INNER, lambda i, c: (step(at(i * INNER, INNER)), c)[1], 0, unroll=True
+    )
+
+
+def partial_for_other(local, theirs, anchor, after):
     def body(r_ref, l_ref, t_ref, a_ref, after_ref, o_ref, l, t, a, o, sems):
         mine = at(seg_of(peer(r_ref[0], 2)) * 32, 32)
         half = at((1 - r_ref[0] // 2) * 32, 32)
@@ -151,12 +156,12 @@
         copies.finish()
 
     return call(
-        body, "partial_for_other", SHORT, shape(32, 8192), [r, local, theirs, anchor, after],
+        body, "partial_for_other", SHORT, shape(32, 8192), [local, theirs, anchor, after],
         [shape(PARTS, 32, WIDTH)] * 4, 4 * PARTS,
     )
 
 
-def average_rows(r, local, theirs, anchor, partial):
+def average_rows(local, theirs, anchor, partial):
     def body(r_ref, l_ref, t_ref, a_ref, p_ref, avg_ref, *refs):
         outs, (l, t, a, q, avg, cut, sems) = refs[:4], refs[4:]
         mine = at(seg_of(r_ref[0]) * 32, 32)
@@ -186,30 +191,30 @@
                     cut[k, i * (INNER // 128) + n] = narrow[:, n * 128 : (n + 1) * 128]
                 return carry
 
-            lax.fori_loop(0, WIDTH // INNER, step, 0)
+            lax.fori_loop(0, WIDTH // INNER, step, 0, unroll=True)
             copies.send(cut.at[k], outs[k])
             copies.send(avg.at[k], avg_ref.at[:, at(peer(r_ref[0], k) * WIDTH, WIDTH)])
         copies.finish()
 
     return call(
         body, "average_rows", LONG, [shape(32, 8192, dtype=F32)] + [shape(16, 32, 128)] * 4,
-        [r, local, theirs, anchor, partial],
+        [local, theirs, anchor, partial],
         [shape(4, 32, WIDTH)] * 4 + [shape(4, 32, WIDTH, dtype=F32), shape(4, 16, 32, 128)], 24,
     )
 
 
-def stack_pieces(r, pieces):
+def stack_pieces(pieces):
     def body(r_ref, *refs):
         for k in range(4):
             refs[4][:, k] = refs[k][...]
 
     return call(
-        body, "stack_pieces", SHORT, shape(16, 4, 32, 128), [r, *pieces], [], 1,
-        near=1, out_near=True,
-    )
-
-
-def change_rows(rg, average, m_rows):
+        body, "stack_pieces", SHORT, shape(16, 4, 32, 128), [*pieces], [], 1,
+        near=0, out_near=True,
+    )
+
+
+def change_rows(average, m_rows):
     def body(rg_ref, avg_ref, m_ref, o_ref, avg, m, o, sems):
         flip = jnp.where(peer(rg_ref[0], rg_ref[1]) == 3, 4, 0)
         copies = Copies(sems)
@@ -236,13 +241,13 @@
         copies.finish()
 
     return call(
-        body, "change_rows", SHORT, shape(32, 8192), [rg, average, m_rows],
+        body, "change_rows", SHORT, shape(32, 8192), [average, m_rows],
         [shape(PARTS, 32, WIDTH, dtype=F32), shape(4, 16, 32, 128), shape(PARTS, 32, WIDTH)],
         3 * PARTS,
     )
 
 
-def new_momentum_of(rg, momentum, pieces, after):
+def new_momentum_of(momentum, pieces, after):
     def body(rg_ref, after_ref, p_ref, m_ref, o_ref, q, o, sems):
         copies = Copies(sems)
         copies.send(p_ref, q)
@@ -263,12 +268,12 @@
 
     return call(
         body, "new_momentum_of", SHORT, shape(2048, 128, dtype=F32),
-        [rg, after, pieces, momentum], [shape(16, 4, 32, 128), shape(4, 512, 128, dtype=F32)], 5,
-        near=3,
-    )
-
-
-def outputs_of(r, local, anchor, changes, before):
+        [after, pieces, momentum], [shape(16, 4, 32, 128), shape(4, 512, 128, dtype=F32)], 5,
+        near=2,
+    )
+
+
+def outputs_of(local, anchor, changes, before):
     ks = sorted(changes)
     n = len(ks)
 
@@ -306,9 +311,9 @@
 
     return call(
         body, "outputs_of", SHORT, [shape(128, 8192)] * 2,
-        [r, local, anchor, *[changes[k] for k in ks], *before],
+        [local, anchor, *[changes[k] for k in ks], *before],
         [shape(n * PARTS, 32, WIDTH)] * 5, 5 * n * PARTS,
-        {3 + n + b: b for b in range(len(before))},
+        {2 + n + b: b for b in range(len(before))},
     )
 
 
@@ -328,31 +333,28 @@
 
 def local(local_weights, anchor, momentum):
     own, anchor = in_hbm(local_weights[0]), in_hbm(anchor)
-    r = lax.axis_index("replica")[None].astype(jnp.int32)
-    g = (lax.axis_index("fsdp") // 16)[None].astype(jnp.int32)
-    rg = jnp.concatenate([r, g])
-
-    half, *pieces = prologue(r, own, in_hbm(momentum))
+
+    half, *pieces = prologue(own, in_hbm(momentum))
     theirs = swap(half, 1)
     pieces = [pieces[0], swap(pieces[1], 1), swap(pieces[2], 2), swap_around(pieces[3])]
-    for_other = partial_for_other(r, own, theirs, anchor, pieces[0])
+    for_other = partial_for_other(own, theirs, anchor, pieces[0])
     partial = swap(for_other, 2)
-    by_row = in_order(r, pieces, for_other).reshape(64, 32, 128)
+    by_row = in_order(pieces, for_other).reshape(64, 32, 128)
     m_rows = lax.all_to_all(by_row, "fsdp", 0, 0, tiled=True)
 
-    average, *cut = average_rows(r, own, theirs, anchor, in_hbm(partial))
-    cut = stack_pieces(r, [across(x, k) for k, x in enumerate(cut)])
+    average, *cut = average_rows(own, theirs, anchor, in_hbm(partial))
+    cut = stack_pieces([across(x, k) for k, x in enumerate(cut)])
     groups = [[16 * i + q for q in range(16)] for i in range(4)]
     cut = lax.all_to_all(cut, "fsdp", 0, 0, axis_index_groups=groups, tiled=True)
 
-    change = change_rows(rg, average, m_rows)
+    change = change_rows(average, m_rows)
     change2 = swap(change, 2)
     change1 = swap(change, 1)
     change3 = swap(change2, 1)
-    outs = outputs_of(r, own, anchor, {0: change, 1: change1}, ())
-    outs = outputs_of(r, own, anchor, {2: change2}, outs)
-    new_anchor, mixed = outputs_of(r, own, anchor, {3: change3}, outs)
-    new_momentum = new_momentum_of(rg, momentum, cut, in_hbm(mixed))
+    outs = outputs_of(own, anchor, {0: change, 1: change1}, ())
+    outs = outputs_of(own, anchor, {2: change2}, outs)
+    new_anchor, mixed = outputs_of(own, anchor, {3: change3}, outs)
+    new_momentum = new_momentum_of(momentum, cut, in_hbm(mixed))
     return new_momentum, new_anchor, mixed[None]
 
 

time: 75.4 us -> 74.8 us (level)
  Pallas kernels: 18.8 us -> 17.4 us
  waiting for transfers between devices: 11 us -> 12 us
    pallas_call x10, Pallas kernels: 18.8 us -> 17.4 us  [call(): pl.pallas_call(lambda *refs: body(Place(), *refs), out_shape=outs, in_spe...]
  transfers between devices with their start and end apart: 14 -> 14, of which waited for: 5 -> 5; matrix products, arithmetic and copies ran while one was open for 0% -> 0% of each run, Pallas kernels for 21% -> 20%
where the time goes in v5:
time: 74.8 us; the launch traced here: 74.4 us
  starting transfers between devices  44.2 us (59%)
  Pallas kernels  17.4 us (23%)
  waiting for transfers between devices  12 us (16%)
  between operations  0.77 us (1%)
    pallas_call x10, Pallas kernels, call(): pl.pallas_call(lambda *refs: body(Place(), *refs), out_shape=outs, in_spe...  17.4 us
    ppermute x4, starting transfers between devices, across(): return lax.ppermute(x, ('replica', 'fsdp'), pairs)  14.4 us
    all_to_all x1, starting transfers between devices, local(): m_rows = lax.all_to_all(by_row, 'fsdp', 0, 0, tiled=True)  12.9 us
    ppermute x7, starting transfers between devices, swap(): return lax.ppermute(x, 'replica', [(i, i ^ k) for i in range(4)])  9.21 us
    all_to_all x1, starting transfers between devices, local(): lax.all_to_all(cut, 'fsdp', 0, 0, axis_index_groups=groups, tiled=True)  5.97 us
    all_to_all x1, waiting for transfers between devices, local(): lax.all_to_all(cut, 'fsdp', 0, 0, axis_index_groups=groups, tiled=True)  4.16 us
    all_to_all x1, waiting for transfers between devices, local(): m_rows = lax.all_to_all(by_row, 'fsdp', 0, 0, tiled=True)  2.94 us
    ppermute x4, waiting for transfers between devices, across(): return lax.ppermute(x, ('replica', 'fsdp'), pairs)  2.63 us
  transfers between devices with their start and end apart: 14, of which 5 were waited for; matrix products, arithmetic and copies ran while one was open for 0% of the time, Pallas kernels for 20%

profile of v5, /device:TPU:8, one launch (start us, length us, event | category | flops | bytes accessed | tf_op | source)
XLA Modules:
  0.0 74.4 jit_solution(10230459803674061665)
XLA Ops:
  0.6 1.6 %prologue.1 = (bf16[64,8192]{1,0:T(8,128)(2,1)S(1)}, bf16[16,32,128]{2,1,0:T(8,128)(2,1)S(1)}, bf16[16,32,128]{2,1,0:T(8,128)(2,1)S(1)}, bf16[16,32,128]{2,1,0:T(8,128)(2,1)S(1)}, bf16[16,32,128]{2,1,0:T(8,128)(2,1)S(1)}) custom-call(bf16[128,8192]{1,0:T(8,128)(2,1)} %bitcast.3, f32[2048,128]{1,0:T(8,128)} %refs_2_.5), custom_call_target="tpu_custom_call" | custom-call | flops 2097152 | bytes 2097152 | tf_op jit(solution)/shard_map/prologue/pallas_call | solution.py:68
  2.2 0.1 collective-permute-start
  2.3 1.7 %collective-permute-start.2 = (bf16[16,32,128]{2,1,0:T(8,128)(2,1)S(1)}, bf16[16,32,128]{2,1,0:T(8,128)(2,1)S(1)}, u32[]{:S(2)}, u32[]{:S(2)}) collective-permute-start(bf16[16,32,128]{2,1,0:T(8,128)(2,1)S(1)} %get-tuple-element.22), channel_id=1, source_target_pairs={{0,196},{1,197},{2,198},{3,199},{4,192},{5,193},{6,194},{7,195},{8... | collective-permute-start | bytes 393224 | tf_op jit(solution)/shard_map/ppermute | solution.py:88
  4.0 1.9 %collective-permute-start.3 = (bf16[16,32,128]{2,1,0:T(8,128)(2,1)S(1)}, bf16[16,32,128]{2,1,0:T(8,128)(2,1)S(1)}, u32[]{:S(2)}, u32[]{:S(2)}) collective-permute-start(bf16[16,32,128]{2,1,0:T(8,128)(2,1)S(1)} %get-tuple-element.23), channel_id=1, source_target_pairs={{0,128},{64,192},{128,0},{192,64},{1,129},{65,193},{129,1},{193,65... | collective-permute-start | bytes 393224 | tf_op jit(solution)/shard_map/ppermute | solution.py:83
  5.9 0.0 collective-permute-start.4
  5.9 0.0 collective-permute-done.refs_1_
  5.9 1.6 %partial_for_other.1.refs_0_ = bf16[32,8192]{1,0:T(8,128)(2,1)S(1)} custom-call(bf16[128,8192]{1,0:T(8,128)(2,1)} %bitcast.4, bf16[64,8192]{1,0:T(8,128)(2,1)S(1)} %collective-permute-done.refs_1_, bf16[128,8192]{1,0:T(8,128)(2,1)} %refs_1_.7, bf16[16,32,128]{2,1,0:T(8,128)(2,1)S(1)} %get-tuple-element.20.refs_3_.refs_4_), custom_call_target="tpu_custom_call" | custom-call | flops 2097152 | bytes 2097152 | tf_op jit(solution)/shard_map/partial_for_other/pallas_call | solution.py:68
  7.5 1.3 %collective-permute-start.1 = (bf16[32,8192]{1,0:T(8,128)(2,1)S(1)}, bf16[32,8192]{1,0:T(8,128)(2,1)}, u32[]{:S(2)}, u32[]{:S(2)}) collective-permute-start(bf16[32,8192]{1,0:T(8,128)(2,1)S(1)} %partial_for_other.1.refs_0_), channel_id=1, source_target_pairs={{0,128},{64,192},{128,0},{192,64},{1,129},{65,193},{129,1},{193,65... | collective-permute-start | bytes 1572872 | tf_op jit(solution)/shard_map/ppermute | solution.py:83
  8.9 0.0 collective-permute-done.2.refs_1_
  8.9 0.8 %collective-permute-done.3.refs_2_ = bf16[16,32,128]{2,1,0:T(8,128)(2,1)S(1)} collective-permute-done((bf16[16,32,128]{2,1,0:T(8,128)(2,1)S(1)}, bf16[16,32,128]{2,1,0:T(8,128)(2,1)S(1)}, u32[]{:S(2)}, u32[]{:S(2)}) %collective-permute-start.3) | collective-permute-done | bytes 131104 | tf_op jit(solution)/shard_map/ppermute | solution.py:83
  9.7 0.0 collective-permute-done.4.refs_3_
  9.7 0.8 %in_order.1 = bf16[4,16,32,128]{3,2,1,0:T(8,128)(2,1)} custom-call(bf16[32,8192]{1,0:T(8,128)(2,1)S(1)} %partial_for_other.1.refs_0_, bf16[16,32,128]{2,1,0:T(8,128)(2,1)S(1)} %collective-permute-done.2.refs_1_, bf16[16,32,128]{2,1,0:T(8,128)(2,1)S(1)} %collective-permute-done.3.refs_2_, bf16[16,32,128]{2,1,0:T(8,128)(2,1)S(1)} %collective-permute-done.4.refs_3_, ...), custom_call_target="tpu_custom_call" | custom-call | flops 17179869184 | bytes 17179869184 | tf_op jit(solution)/shard_map/in_order/pallas_call | solution.py:68
  10.5 12.9 %all-to-all-start = ((bf16[64,32,128]{2,1,0:T(8,128)(2,1)}), bf16[64,32,128]{2,1,0:T(8,128)(2,1)S(1)}, u32[]{:S(2)}, u32[]{:S(2)}) async-start(bf16[64,32,128]{2,1,0:T(8,128)(2,1)} %bitcast.1), calls=%async_computation | async-start | bytes 1048576 | tf_op jit(solution)/shard_map/all_to_all | solution.py:343
  23.4 0.0 collective-permute-done.1.refs_3_
  23.5 2.6 %average_rows.1 = (f32[32,8192]{1,0:T(8,128)S(1)}, bf16[16,32,128]{2,1,0:T(8,128)(2,1)S(1)}, bf16[16,32,128]{2,1,0:T(8,128)(2,1)S(1)}, bf16[16,32,128]{2,1,0:T(8,128)(2,1)}, bf16[16,32,128]{2,1,0:T(8,128)(2,1)S(1)}) custom-call(bf16[128,8192]{1,0:T(8,128)(2,1)} %bitcast.5, bf16[64,8192]{1,0:T(8,128)(2,1)S(1)} %collective-permute-done.refs_1_, ...), custom_call_target="tpu_custom_call" | custom-call | flops 17179869184 | bytes 17179869184 | tf_op jit(solution)/shard_map/average_rows/pallas_call | solution.py:68
  26.0 2.2 %collective-permute-start.10 = (bf16[16,32,128]{2,1,0:T(8,128)(2,1)}, bf16[16,32,128]{2,1,0:T(8,128)(2,1)S(1)}, u32[]{:S(2)}, u32[]{:S(2)}) collective-permute-start(bf16[16,32,128]{2,1,0:T(8,128)(2,1)} %get-tuple-element.32), channel_id=1, source_target_pairs={{0,32},{1,33},{2,34},{3,35},{4,36},{5,37},{6,38},{7,39},{8,40},{9,... | collective-permute-start | bytes 393224 | tf_op jit(solution)/shard_map/ppermute | solution.py:327
  28.2 4.2 %collective-permute-start.11 = (bf16[16,32,128]{2,1,0:T(8,128)(2,1)S(1)}, bf16[16,32,128]{2,1,0:T(8,128)(2,1)S(1)}, u32[]{:S(2)}, u32[]{:S(2)}) collective-permute-start(bf16[16,32,128]{2,1,0:T(8,128)(2,1)S(1)} %get-tuple-element.33), channel_id=1, source_target_pairs={{0,48},{1,49},{2,50},{3,51},{4,52},{5,53},{6,54},{7,55},{8,56},{9,... | collective-permute-start | bytes 393224 | tf_op jit(solution)/shard_map/ppermute | solution.py:327
  32.5 3.8 %collective-permute-start.8 = (bf16[16,32,128]{2,1,0:T(8,128)(2,1)S(1)}, bf16[16,32,128]{2,1,0:T(8,128)(2,1)S(1)}, u32[]{:S(2)}, u32[]{:S(2)}) collective-permute-start(bf16[16,32,128]{2,1,0:T(8,128)(2,1)S(1)} %get-tuple-element.30), channel_id=1, source_target_pairs={{0,0},{1,1},{2,2},{3,3},{4,4},{5,5},{6,6},{7,7},{8,8},{9,9},{10,10... | collective-permute-start | bytes 393224 | tf_op jit(solution)/shard_map/ppermute | solution.py:327
  36.3 4.2 %collective-permute-start.9 = (bf16[16,32,128]{2,1,0:T(8,128)(2,1)S(1)}, bf16[16,32,128]{2,1,0:T(8,128)(2,1)S(1)}, u32[]{:S(2)}, u32[]{:S(2)}) collective-permute-start(bf16[16,32,128]{2,1,0:T(8,128)(2,1)S(1)} %get-tuple-element.31), channel_id=1, source_target_pairs={{0,16},{1,17},{2,18},{3,19},{4,20},{5,21},{6,22},{7,23},{8,24},{9,... | collective-permute-start | bytes 393224 | tf_op jit(solution)/shard_map/ppermute | solution.py:327
  40.5 2.9 %all-to-all-done.refs_1_ = bf16[64,32,128]{2,1,0:T(8,128)(2,1)S(1)} async-done(((bf16[64,32,128]{2,1,0:T(8,128)(2,1)}), bf16[64,32,128]{2,1,0:T(8,128)(2,1)S(1)}, u32[]{:S(2)}, u32[]{:S(2)}) %all-to-all-start) | async-done | bytes 524320 | tf_op jit(solution)/shard_map/all_to_all | solution.py:343
  43.4 1.5 %change_rows.1.refs_2_ = bf16[32,8192]{1,0:T(8,128)(2,1)S(1)} custom-call(f32[32,8192]{1,0:T(8,128)S(1)} %get-tuple-element.21.refs_0_, bf16[64,32,128]{2,1,0:T(8,128)(2,1)S(1)} %all-to-all-done.refs_1_), custom_call_target="tpu_custom_call" | custom-call | flops 2097152 | bytes 2097152 | tf_op jit(solution)/shard_map/change_rows/pallas_call | solution.py:68
  44.9 5.3 %collective-permute-start.5 = (bf16[32,8192]{1,0:T(8,128)(2,1)S(1)}, bf16[32,8192]{1,0:T(8,128)(2,1)S(1)}, u32[]{:S(2)}, u32[]{:S(2)}) collective-permute-start(bf16[32,8192]{1,0:T(8,128)(2,1)S(1)} %change_rows.1.refs_2_), channel_id=1, source_target_pairs={{0,128},{64,192},{128,0},{192,64},{1,129},{65,193},{129,1},{193,65... | collective-permute-start | bytes 1572872 | tf_op jit(solution)/shard_map/ppermute | solution.py:83
  50.2 0.0 collective-permute-done.10.refs_2_
  50.2 0.0 collective-permute-done.11.refs_3_
  50.2 2.6 %collective-permute-done.8.refs_0_ = bf16[16,32,128]{2,1,0:T(8,128)(2,1)S(1)} collective-permute-done((bf16[16,32,128]{2,1,0:T(8,128)(2,1)S(1)}, bf16[16,32,128]{2,1,0:T(8,128)(2,1)S(1)}, u32[]{:S(2)}, u32[]{:S(2)}) %collective-permute-start.8) | collective-permute-done | bytes 131104 | tf_op jit(solution)/shard_map/ppermute | solution.py:327
  52.8 0.0 collective-permute-done.9.refs_1_
  52.8 0.8 %stack_pieces.1 = bf16[16,4,32,128]{3,2,1,0:T(8,128)(2,1)} custom-call(bf16[16,32,128]{2,1,0:T(8,128)(2,1)S(1)} %collective-permute-done.8.refs_0_, bf16[16,32,128]{2,1,0:T(8,128)(2,1)S(1)} %collective-permute-done.9.refs_1_, bf16[16,32,128]{2,1,0:T(8,128)(2,1)S(1)} %collective-permute-done.10.refs_2_, bf16[16,32,128]{2,1,0:T(8,128)(2,1)S(1)} %collective-permute-done.11.refs_3_), custom_call_target="tpu_custom_call" | custom-call | flops 2097152 | bytes 2097152 | tf_op jit(solution)/shard_map/stack_pieces/pallas_call | solution.py:68
  53.6 6.0 %all-to-all-start.1 = ((bf16[16,4,32,128]{3,2,1,0:T(8,128)(2,1)}), bf16[16,4,32,128]{3,2,1,0:T(8,128)(2,1)S(1)}, u32[]{:S(2)}, u32[]{:S(2)}) async-start(bf16[16,4,32,128]{3,2,1,0:T(8,128)(2,1)} %stack_pieces.1), calls=%async_computation.1 | async-start | bytes 1048576 | tf_op jit(solution)/shard_map/all_to_all | solution.py:348
  59.6 0.5 collective-permute-start.7
  60.1 0.0 collective-permute-done.5.refs_2_
  60.1 0.1 collective-permute-start.6
  60.2 1.4 %collective-permute-done.7.refs_3_ = bf16[32,8192]{1,0:T(8,128)(2,1)S(1)} collective-permute-done((bf16[32,8192]{1,0:T(8,128)(2,1)S(1)}, bf16[32,8192]{1,0:T(8,128)(2,1)S(1)}, u32[]{:S(2)}, u32[]{:S(2)}) %collective-permute-start.7) | collective-permute-done | bytes 524320 | tf_op jit(solution)/shard_map/ppermute | solution.py:83
  61.7 2.7 %outputs_of.3 = (bf16[128,8192]{1,0:T(8,128)(2,1)}, bf16[128,8192]{1,0:T(8,128)(2,1)}) custom-call(bf16[128,8192]{1,0:T(8,128)(2,1)} %bitcast.6, bf16[128,8192]{1,0:T(8,128)(2,1)} %refs_1_.7, bf16[32,8192]{1,0:T(8,128)(2,1)S(1)} %change_rows.1.refs_2_, bf16[32,8192]{1,0:T(8,128)(2,1)S(1)} %collective-permute-done.7.refs_3_), custom_call_target="tpu_custom_call" | custom-call | flops 2097152 | bytes 2097152 | tf_op jit(solution)/shard_map/outputs_of/pallas_call | solution.py:68
  64.4 2.2 %outputs_of.4 = (bf16[128,8192]{1,0:T(8,128)(2,1)}, bf16[128,8192]{1,0:T(8,128)(2,1)}) custom-call(bf16[128,8192]{1,0:T(8,128)(2,1)} %bitcast.7, bf16[128,8192]{1,0:T(8,128)(2,1)} %refs_1_.7, bf16[32,8192]{1,0:T(8,128)(2,1)S(1)} %collective-permute-done.5.refs_2_, ...), custom_call_target="tpu_custom_call", output_to_operand_aliasing={{0}: (3, {}), {1}: (4, {})} | custom-call | flops 2097152 | bytes 2097152 | tf_op jit(solution)/shard_map/outputs_of/pallas_call | solution.py:68
  66.7 0.0 collective-permute-done.6.refs_2_
  66.7 0.0 copy-start
  66.7 2.3 %outputs_of.5 = (bf16[128,8192]{1,0:T(8,128)(2,1)}, bf16[128,8192]{1,0:T(8,128)(2,1)}) custom-call(bf16[128,8192]{1,0:T(8,128)(2,1)} %bitcast.8, bf16[128,8192]{1,0:T(8,128)(2,1)} %refs_1_.7, bf16[32,8192]{1,0:T(8,128)(2,1)S(1)} %collective-permute-done.6.refs_2_, ...), custom_call_target="tpu_custom_call", output_to_operand_aliasing={{0}: (3, {}), {1}: (4, {})} | custom-call | flops 2097152 | bytes 2097152 | tf_op jit(solution)/shard_map/outputs_of/pallas_call | solution.py:68
  69.0 4.2 %all-to-all-done.1.refs_1_ = bf16[16,4,32,128]{3,2,1,0:T(8,128)(2,1)S(1)} async-done(((bf16[16,4,32,128]{3,2,1,0:T(8,128)(2,1)}), bf16[16,4,32,128]{3,2,1,0:T(8,128)(2,1)S(1)}, u32[]{:S(2)}, u32[]{:S(2)}) %all-to-all-start.1) | async-done | bytes 524320 | tf_op jit(solution)/shard_map/all_to_all | solution.py:348
  73.2 0.0 copy-done
  73.2 1.2 %new_momentum_of.1 = f32[2048,128]{1,0:T(8,128)} custom-call(bf16[128,8192]{1,0:T(8,128)(2,1)} %get-tuple-element.29.refs_0_, bf16[16,4,32,128]{3,2,1,0:T(8,128)(2,1)S(1)} %all-to-all-done.1.refs_1_, f32[2048,128]{1,0:T(8,128)S(1)} %copy-done), custom_call_target="tpu_custom_call" | custom-call | flops 2097152 | bytes 2097152 | tf_op jit(solution)/shard_map/new_momentum_of/pallas_call | solution.py:68
Async XLA Ops:
  2.2 3.7 %collective-permute-start = (bf16[64,8192]{1,0:T(8,128)(2,1)S(1)}, bf16[64,8192]{1,0:T(8,128)(2,1)S(1)}, u32[]{:S(2)}, u32[]{:S(2)}) collective-permute-start(bf16[64,8192]{1,0:T(8,128)(2,1)S(1)} %get-tuple-element.19), channel_id=1, source_target_pairs={{0,64},{64,0},{128,192},{192,128},{1,65},{65,1},{129,193},{193,129... | collective-permute-start | bytes 3145736 | tf_op jit(solution)/shard_map/ppermute | solution.py:83
  2.3 6.5 %collective-permute-start.2 = (bf16[16,32,128]{2,1,0:T(8,128)(2,1)S(1)}, bf16[16,32,128]{2,1,0:T(8,128)(2,1)S(1)}, u32[]{:S(2)}, u32[]{:S(2)}) collective-permute-start(bf16[16,32,128]{2,1,0:T(8,128)(2,1)S(1)} %get-tuple-element.22), channel_id=1, source_target_pairs={{0,196},{1,197},{2,198},{3,199},{4,192},{5,193},{6,194},{7,195},{8... | collective-permute-start | bytes 393224 | tf_op jit(solution)/shard_map/ppermute | solution.py:88
  4.0 5.6 %collective-permute-start.3 = (bf16[16,32,128]{2,1,0:T(8,128)(2,1)S(1)}, bf16[16,32,128]{2,1,0:T(8,128)(2,1)S(1)}, u32[]{:S(2)}, u32[]{:S(2)}) collective-permute-start(bf16[16,32,128]{2,1,0:T(8,128)(2,1)S(1)} %get-tuple-element.23), channel_id=1, source_target_pairs={{0,128},{64,192},{128,0},{192,64},{1,129},{65,193},{129,1},{193,65... | collective-permute-start | bytes 393224 | tf_op jit(solution)/shard_map/ppermute | solution.py:83
  5.9 3.7 %collective-permute-start.4 = (bf16[16,32,128]{2,1,0:T(8,128)(2,1)S(1)}, bf16[16,32,128]{2,1,0:T(8,128)(2,1)S(1)}, u32[]{:S(2)}, u32[]{:S(2)}) collective-permute-start(bf16[16,32,128]{2,1,0:T(8,128)(2,1)S(1)} %get-tuple-element.24), channel_id=1, source_target_pairs={{0,64},{64,0},{128,192},{192,128},{1,65},{65,1},{129,193},{193,129... | collective-permute-start | bytes 393224 | tf_op jit(solution)/shard_map/ppermute | solution.py:83
  7.5 15.9 %collective-permute-start.1 = (bf16[32,8192]{1,0:T(8,128)(2,1)S(1)}, bf16[32,8192]{1,0:T(8,128)(2,1)}, u32[]{:S(2)}, u32[]{:S(2)}) collective-permute-start(bf16[32,8192]{1,0:T(8,128)(2,1)S(1)} %partial_for_other.1.refs_0_), channel_id=1, source_target_pairs={{0,128},{64,192},{128,0},{192,64},{1,129},{65,193},{129,1},{193,65... | collective-permute-start | bytes 1572872 | tf_op jit(solution)/shard_map/ppermute | solution.py:83
  10.5 32.9 %all-to-all-start = ((bf16[64,32,128]{2,1,0:T(8,128)(2,1)}), bf16[64,32,128]{2,1,0:T(8,128)(2,1)S(1)}, u32[]{:S(2)}, u32[]{:S(2)}) async-start(bf16[64,32,128]{2,1,0:T(8,128)(2,1)} %bitcast.1), calls=%async_computation | async-start | bytes 1048576 | tf_op jit(solution)/shard_map/all_to_all | solution.py:343
  26.0 24.1 %collective-permute-start.10 = (bf16[16,32,128]{2,1,0:T(8,128)(2,1)}, bf16[16,32,128]{2,1,0:T(8,128)(2,1)S(1)}, u32[]{:S(2)}, u32[]{:S(2)}) collective-permute-start(bf16[16,32,128]{2,1,0:T(8,128)(2,1)} %get-tuple-element.32), channel_id=1, source_target_pairs={{0,32},{1,33},{2,34},{3,35},{4,36},{5,37},{6,38},{7,39},{8,40},{9,... | collective-permute-start | bytes 393224 | tf_op jit(solution)/shard_map/ppermute | solution.py:327
  28.2 21.9 %collective-permute-start.11 = (bf16[16,32,128]{2,1,0:T(8,128)(2,1)S(1)}, bf16[16,32,128]{2,1,0:T(8,128)(2,1)S(1)}, u32[]{:S(2)}, u32[]{:S(2)}) collective-permute-start(bf16[16,32,128]{2,1,0:T(8,128)(2,1)S(1)} %get-tuple-element.33), channel_id=1, source_target_pairs={{0,48},{1,49},{2,50},{3,51},{4,52},{5,53},{6,54},{7,55},{8,56},{9,... | collective-permute-start | bytes 393224 | tf_op jit(solution)/shard_map/ppermute | solution.py:327
  32.5 20.3 %collective-permute-start.8 = (bf16[16,32,128]{2,1,0:T(8,128)(2,1)S(1)}, bf16[16,32,128]{2,1,0:T(8,128)(2,1)S(1)}, u32[]{:S(2)}, u32[]{:S(2)}) collective-permute-start(bf16[16,32,128]{2,1,0:T(8,128)(2,1)S(1)} %get-tuple-element.30), channel_id=1, source_target_pairs={{0,0},{1,1},{2,2},{3,3},{4,4},{5,5},{6,6},{7,7},{8,8},{9,9},{10,10... | collective-permute-start | bytes 393224 | tf_op jit(solution)/shard_map/ppermute | solution.py:327
  36.3 16.5 %collective-permute-start.9 = (bf16[16,32,128]{2,1,0:T(8,128)(2,1)S(1)}, bf16[16,32,128]{2,1,0:T(8,128)(2,1)S(1)}, u32[]{:S(2)}, u32[]{:S(2)}) collective-permute-start(bf16[16,32,128]{2,1,0:T(8,128)(2,1)S(1)} %get-tuple-element.31), channel_id=1, source_target_pairs={{0,16},{1,17},{2,18},{3,19},{4,20},{5,21},{6,22},{7,23},{8,24},{9,... | collective-permute-start | bytes 393224 | tf_op jit(solution)/shard_map/ppermute | solution.py:327
  44.9 15.3 %collective-permute-start.5 = (bf16[32,8192]{1,0:T(8,128)(2,1)S(1)}, bf16[32,8192]{1,0:T(8,128)(2,1)S(1)}, u32[]{:S(2)}, u32[]{:S(2)}) collective-permute-start(bf16[32,8192]{1,0:T(8,128)(2,1)S(1)} %change_rows.1.refs_2_), channel_id=1, source_target_pairs={{0,128},{64,192},{128,0},{192,64},{1,129},{65,193},{129,1},{193,65... | collective-permute-start | bytes 1572872 | tf_op jit(solution)/shard_map/ppermute | solution.py:83
  53.6 19.5 %all-to-all-start.1 = ((bf16[16,4,32,128]{3,2,1,0:T(8,128)(2,1)}), bf16[16,4,32,128]{3,2,1,0:T(8,128)(2,1)S(1)}, u32[]{:S(2)}, u32[]{:S(2)}) async-start(bf16[16,4,32,128]{3,2,1,0:T(8,128)(2,1)} %stack_pieces.1), calls=%async_computation.1 | async-start | bytes 1048576 | tf_op jit(solution)/shard_map/all_to_all | solution.py:348
  59.6 2.1 %collective-permute-start.7 = (bf16[32,8192]{1,0:T(8,128)(2,1)S(1)}, bf16[32,8192]{1,0:T(8,128)(2,1)S(1)}, u32[]{:S(2)}, u32[]{:S(2)}) collective-permute-start(bf16[32,8192]{1,0:T(8,128)(2,1)S(1)} %change_rows.1.refs_2_), channel_id=1, source_target_pairs={{0,64},{64,0},{128,192},{192,128},{1,65},{65,1},{129,193},{193,129... | collective-permute-start | bytes 1572872 | tf_op jit(solution)/shard_map/ppermute | solution.py:83
  60.1 6.5 %collective-permute-start.6 = (bf16[32,8192]{1,0:T(8,128)(2,1)S(1)}, bf16[32,8192]{1,0:T(8,128)(2,1)S(1)}, u32[]{:S(2)}, u32[]{:S(2)}) collective-permute-start(bf16[32,8192]{1,0:T(8,128)(2,1)S(1)} %collective-permute-done.5.refs_2_), channel_id=1, source_target_pairs={{0,64},{64,0},{128,192},{192,128},{1,65},{65,1},{129,193},{193,129... | collective-permute-start | bytes 1572872 | tf_op jit(solution)/shard_map/ppermute | solution.py:83
  66.7 6.5 %copy-start = (f32[2048,128]{1,0:T(8,128)S(1)}, f32[2048,128]{1,0:T(8,128)}, u32[]{:S(2)}) copy-start(f32[2048,128]{1,0:T(8,128)} %refs_2_.5) | copy-start | bytes 3145732

commit v6 on v5

--- a/solution.py
+++ b/solution.py
@@ -129,51 +129,55 @@
     )
 
 
-def partial_for_other(local, theirs, anchor, after):
-    def body(r_ref, l_ref, t_ref, a_ref, after_ref, o_ref, l, t, a, o, sems):
-        mine = at(seg_of(peer(r_ref[0], 2)) * 32, 32)
-        half = at((1 - r_ref[0] // 2) * 32, 32)
+def partial_rows(local, theirs, anchor):
+    def body(r_ref, l_ref, t_ref, a_ref, other_ref, own_ref, l, t, a, o, own, sems):
         copies = Copies(sems)
         loads = []
-        for p in range(PARTS):
-            cols = pl.ds(p * WIDTH, WIDTH)
-            loads.append([
-                copies.start(l_ref.at[mine, cols], l.at[p]),
-                copies.start(t_ref.at[half, cols], t.at[p]),
-                copies.start(a_ref.at[mine, cols], a.at[p]),
-            ])
-        for p in range(PARTS):
-            for load in loads[p]:
+        for k in (2, 0):
+            device = peer(r_ref[0], k)
+            mine = at(seg_of(device) * 32, 32)
+            half = at((device // 2) * 32, 32)
+            for p in range(PARTS):
+                cols = pl.ds(p * WIDTH, WIDTH)
+                i = len(loads)
+                loads.append([
+                    copies.start(l_ref.at[mine, cols], l.at[i]),
+                    copies.start(t_ref.at[half, cols], t.at[i]),
+                    copies.start(a_ref.at[mine, cols], a.at[i]),
+                ])
+        for i, waits in enumerate(loads):
+            for load in waits:
                 load.wait()
-
-            def step(cols, p=p):
-                x = a[p, :, cols].astype(F32)
-                total = (x - l[p, :, cols].astype(F32)) + (x - t[p, :, cols].astype(F32))
-                o[p, :, cols] = total.astype(BF)
+            to, p = (o if i < PARTS else own), i % PARTS
+
+            def step(cols, i=i, p=p, to=to):
+                x = a[i, :, cols].astype(F32)
+                total = (x - l[i, :, cols].astype(F32)) + (x - t[i, :, cols].astype(F32))
+                to[p, :, cols] = total.astype(to.dtype)
 
             inner(step)
-            copies.send(o.at[p], o_ref.at[:, pl.ds(p * WIDTH, WIDTH)])
-        copies.finish()
-
-    return call(
-        body, "partial_for_other", SHORT, shape(32, 8192), [local, theirs, anchor, after],
-        [shape(PARTS, 32, WIDTH)] * 4, 4 * PARTS,
-    )
-
-
-def average_rows(local, theirs, anchor, partial):
-    def body(r_ref, l_ref, t_ref, a_ref, p_ref, avg_ref, *refs):
-        outs, (l, t, a, q, avg, cut, sems) = refs[:4], refs[4:]
-        mine = at(seg_of(r_ref[0]) * 32, 32)
-        half = at((r_ref[0] // 2) * 32, 32)
+            to_ref = other_ref if i < PARTS else own_ref
+            copies.send(to.at[p], to_ref.at[:, pl.ds(p * WIDTH, WIDTH)])
+        copies.finish()
+
+    return call(
+        body, "partial_rows", SHORT, [shape(32, 8192)] * 2,
+        [local, theirs, anchor],
+        [shape(2 * PARTS, 32, WIDTH)] * 3
+        + [shape(PARTS, 32, WIDTH)] * 2,
+        8 * PARTS,
+    )
+
+
+def average_rows(own, partial):
+    def body(r_ref, own_ref, p_ref, avg_ref, *refs):
+        outs, (x, q, avg, cut, sems) = refs[:4], refs[4:]
         copies = Copies(sems)
         loads = []
         for k in range(4):
             cols = at(peer(r_ref[0], k) * WIDTH, WIDTH)
             loads.append([
-                copies.start(l_ref.at[mine, cols], l.at[k]),
-                copies.start(t_ref.at[half, cols], t.at[k]),
-                copies.start(a_ref.at[mine, cols], a.at[k]),
+                copies.start(own_ref.at[:, cols], x.at[k]),
                 copies.start(p_ref.at[:, cols], q.at[k]),
             ])
         for k in range(4):
@@ -182,9 +186,7 @@
 
             def step(i, carry, k=k):
                 cols = at(i * INNER, INNER)
-                x = a[k, :, cols].astype(F32)
-                own = (x - l[k, :, cols].astype(F32)) + (x - t[k, :, cols].astype(F32))
-                y = (own + q[k, :, cols].astype(F32)) * 0.25
+                y = (x[k, :, cols].astype(F32) + q[k, :, cols].astype(F32)) * 0.25
                 avg[k, :, cols] = y
                 narrow = y.astype(BF)
                 for n in range(INNER // 128):
@@ -198,8 +200,8 @@
 
     return call(
         body, "average_rows", LONG, [shape(32, 8192, dtype=F32)] + [shape(16, 32, 128)] * 4,
-        [local, theirs, anchor, partial],
-        [shape(4, 32, WIDTH)] * 4 + [shape(4, 32, WIDTH, dtype=F32), shape(4, 16, 32, 128)], 24,
+        [own, partial],
+        [shape(4, 32, WIDTH)] * 2 + [shape(4, 32, WIDTH, dtype=F32), shape(4, 16, 32, 128)], 16,
     )
 
 
@@ -337,12 +339,12 @@
     half, *pieces = prologue(own, in_hbm(momentum))
     theirs = swap(half, 1)
     pieces = [pieces[0], swap(pieces[1], 1), swap(pieces[2], 2), swap_around(pieces[3])]
-    for_other = partial_for_other(own, theirs, anchor, pieces[0])
+    for_other, mine = partial_rows(own, theirs, anchor)
     partial = swap(for_other, 2)
     by_row = in_order(pieces, for_other).reshape(64, 32, 128)
     m_rows = lax.all_to_all(by_row, "fsdp", 0, 0, tiled=True)
 
-    average, *cut = average_rows(own, theirs, anchor, in_hbm(partial))
+    average, *cut = average_rows(mine, partial)
     cut = stack_pieces([across(x, k) for k, x in enumerate(cut)])
     groups = [[16 * i + q for q in range(16)] for i in range(4)]
     cut = lax.all_to_all(cut, "fsdp", 0, 0, axis_index_groups=groups, tiled=True)

time: 74.8 us -> 73.8 us (0.987)
  starting transfers between devices: 44.2 us -> 41.5 us
  waiting for transfers between devices: 12 us -> 14.2 us
    all_to_all x1, waiting for transfers between devices: 2.94 us -> 5.31 us  [local(): m_rows = lax.all_to_all(by_row, 'fsdp', 0, 0, tiled=True)]
    ppermute x7, starting transfers between devices: 9.21 us -> 7.01 us  [swap(): return lax.ppermute(x, 'replica', [(i, i ^ k) for i in range(4)])]
    ppermute x4, waiting for transfers between devices: 2.63 us -> 3.72 us  [across(): return lax.ppermute(x, ('replica', 'fsdp'), pairs)]
  transfers between devices with their start and end apart: 14 -> 14, of which waited for: 5 -> 5; matrix products, arithmetic and copies ran while one was open for 0% -> 0% of each run, Pallas kernels for 20% -> 19%
where the time goes in v6:
time: 73.8 us; the launch traced here: 73.4 us
  starting transfers between devices  41.5 us (56%)
  Pallas kernels  16.9 us (23%)
  waiting for transfers between devices  14.2 us (19%)
  between operations  0.78 us (1%)
    pallas_call x10, Pallas kernels, call(): pl.pallas_call(lambda *refs: body(Place(), *refs), out_shape=outs, in_spe...  16.9 us
    ppermute x4, starting transfers between devices, across(): return lax.ppermute(x, ('replica', 'fsdp'), pairs)  14.4 us
    all_to_all x1, starting transfers between devices, local(): m_rows = lax.all_to_all(by_row, 'fsdp', 0, 0, tiled=True)  12.9 us
    ppermute x7, starting transfers between devices, swap(): return lax.ppermute(x, 'replica', [(i, i ^ k) for i in range(4)])  7.01 us
    all_to_all x1, starting transfers between devices, local(): lax.all_to_all(cut, 'fsdp', 0, 0, axis_index_groups=groups, tiled=True)  5.51 us
    all_to_all x1, waiting for transfers between devices, local(): m_rows = lax.all_to_all(by_row, 'fsdp', 0, 0, tiled=True)  5.31 us
    ppermute x4, waiting for transfers between devices, across(): return lax.ppermute(x, ('replica', 'fsdp'), pairs)  3.72 us
    all_to_all x1, waiting for transfers between devices, local(): lax.all_to_all(cut, 'fsdp', 0, 0, axis_index_groups=groups, tiled=True)  3.61 us
  transfers between devices with their start and end apart: 14, of which 5 were waited for; matrix products, arithmetic and copies ran while one was open for 0% of the time, Pallas kernels for 19%

profile of v6, /device:TPU:8, one launch (start us, length us, event | category | flops | bytes accessed | tf_op | source)
XLA Modules:
  0.0 73.4 jit_solution(14524849924408035377)
XLA Ops:
  0.6 1.6 %prologue.1 = (bf16[64,8192]{1,0:T(8,128)(2,1)S(1)}, bf16[16,32,128]{2,1,0:T(8,128)(2,1)S(1)}, bf16[16,32,128]{2,1,0:T(8,128)(2,1)S(1)}, bf16[16,32,128]{2,1,0:T(8,128)(2,1)S(1)}, bf16[16,32,128]{2,1,0:T(8,128)(2,1)S(1)}) custom-call(bf16[128,8192]{1,0:T(8,128)(2,1)} %bitcast.3, f32[2048,128]{1,0:T(8,128)} %refs_2_.3), custom_call_target="tpu_custom_call" | custom-call | flops 2097152 | bytes 2097152 | tf_op jit(solution)/shard_map/prologue/pallas_call | solution.py:68
  2.2 0.1 collective-permute-start
  2.3 1.7 %collective-permute-start.2 = (bf16[16,32,128]{2,1,0:T(8,128)(2,1)S(1)}, bf16[16,32,128]{2,1,0:T(8,128)(2,1)S(1)}, u32[]{:S(2)}, u32[]{:S(2)}) collective-permute-start(bf16[16,32,128]{2,1,0:T(8,128)(2,1)S(1)} %get-tuple-element.25), channel_id=1, source_target_pairs={{0,196},{1,197},{2,198},{3,199},{4,192},{5,193},{6,194},{7,195},{8... | collective-permute-start | bytes 393224 | tf_op jit(solution)/shard_map/ppermute | solution.py:88
  4.0 1.9 %collective-permute-start.3 = (bf16[16,32,128]{2,1,0:T(8,128)(2,1)S(1)}, bf16[16,32,128]{2,1,0:T(8,128)(2,1)S(1)}, u32[]{:S(2)}, u32[]{:S(2)}) collective-permute-start(bf16[16,32,128]{2,1,0:T(8,128)(2,1)S(1)} %get-tuple-element.26), channel_id=1, source_target_pairs={{0,128},{64,192},{128,0},{192,64},{1,129},{65,193},{129,1},{193,65... | collective-permute-start | bytes 393224 | tf_op jit(solution)/shard_map/ppermute | solution.py:83
  5.9 0.0 collective-permute-start.4
  5.9 0.0 collective-permute-done.refs_1_
  5.9 2.2 %partial_rows.1 = (bf16[32,8192]{1,0:T(8,128)(2,1)S(1)}, bf16[32,8192]{1,0:T(8,128)(2,1)S(1)}) custom-call(bf16[128,8192]{1,0:T(8,128)(2,1)} %bitcast.4, bf16[64,8192]{1,0:T(8,128)(2,1)S(1)} %collective-permute-done.refs_1_, bf16[128,8192]{1,0:T(8,128)(2,1)} %refs_1_.7), custom_call_target="tpu_custom_call" | custom-call | flops 2097152 | bytes 2097152 | tf_op jit(solution)/shard_map/partial_rows/pallas_call | solution.py:68
  8.1 1.3 %collective-permute-start.1 = (bf16[32,8192]{1,0:T(8,128)(2,1)S(1)}, bf16[32,8192]{1,0:T(8,128)(2,1)S(1)}, u32[]{:S(2)}, u32[]{:S(2)}) collective-permute-start(bf16[32,8192]{1,0:T(8,128)(2,1)S(1)} %get-tuple-element.23.refs_0_), channel_id=1, source_target_pairs={{0,128},{64,192},{128,0},{192,64},{1,129},{65,193},{129,1},{193,65... | collective-permute-start | bytes 1572872 | tf_op jit(solution)/shard_map/ppermute | solution.py:83
  9.5 0.0 collective-permute-done.2.refs_1_
  9.5 0.2 collective-permute-done.3.refs_2_
  9.7 0.0 collective-permute-done.4.refs_3_
  9.7 0.8 %in_order.1 = bf16[4,16,32,128]{3,2,1,0:T(8,128)(2,1)} custom-call(bf16[32,8192]{1,0:T(8,128)(2,1)S(1)} %get-tuple-element.23.refs_0_, bf16[16,32,128]{2,1,0:T(8,128)(2,1)S(1)} %collective-permute-done.2.refs_1_, bf16[16,32,128]{2,1,0:T(8,128)(2,1)S(1)} %collective-permute-done.3.refs_2_, bf16[16,32,128]{2,1,0:T(8,128)(2,1)S(1)} %collective-permute-done.4.refs_3_, ...), custom_call_target="tpu_custom_call" | custom-call | flops 17179869184 | bytes 17179869184 | tf_op jit(solution)/shard_map/in_order/pallas_call | solution.py:68
  10.5 12.9 %all-to-all-start = ((bf16[64,32,128]{2,1,0:T(8,128)(2,1)}), bf16[64,32,128]{2,1,0:T(8,128)(2,1)S(1)}, u32[]{:S(2)}, u32[]{:S(2)}) async-start(bf16[64,32,128]{2,1,0:T(8,128)(2,1)} %bitcast.1), calls=%async_computation | async-start | bytes 1048576 | tf_op jit(solution)/shard_map/all_to_all | solution.py:345
  23.4 0.0 collective-permute-done.1.refs_1_
  23.5 1.4 %average_rows.1 = (f32[32,8192]{1,0:T(8,128)S(1)}, bf16[16,32,128]{2,1,0:T(8,128)(2,1)S(1)}, bf16[16,32,128]{2,1,0:T(8,128)(2,1)S(1)}, bf16[16,32,128]{2,1,0:T(8,128)(2,1)S(1)}, bf16[16,32,128]{2,1,0:T(8,128)(2,1)S(1)}) custom-call(bf16[32,8192]{1,0:T(8,128)(2,1)S(1)} %get-tuple-element.22.refs_0_, bf16[32,8192]{1,0:T(8,128)(2,1)S(1)} %collective-permute-done.1.refs_1_), custom_call_target="tpu_custom_call" | custom-call | flops 17179869184 | bytes 17179869184 | tf_op jit(solution)/shard_map/average_rows/pallas_call | solution.py:68
  24.9 2.1 %collective-permute-start.10 = (bf16[16,32,128]{2,1,0:T(8,128)(2,1)S(1)}, bf16[16,32,128]{2,1,0:T(8,128)(2,1)S(1)}, u32[]{:S(2)}, u32[]{:S(2)}) collective-permute-start(bf16[16,32,128]{2,1,0:T(8,128)(2,1)S(1)} %get-tuple-element.36), channel_id=1, source_target_pairs={{0,32},{1,33},{2,34},{3,35},{4,36},{5,37},{6,38},{7,39},{8,40},{9,... | collective-permute-start | bytes 393224 | tf_op jit(solution)/shard_map/ppermute | solution.py:329
  27.0 4.4 %collective-permute-start.11 = (bf16[16,32,128]{2,1,0:T(8,128)(2,1)S(1)}, bf16[16,32,128]{2,1,0:T(8,128)(2,1)S(1)}, u32[]{:S(2)}, u32[]{:S(2)}) collective-permute-start(bf16[16,32,128]{2,1,0:T(8,128)(2,1)S(1)} %get-tuple-element.37), channel_id=1, source_target_pairs={{0,48},{1,49},{2,50},{3,51},{4,52},{5,53},{6,54},{7,55},{8,56},{9,... | collective-permute-start | bytes 393224 | tf_op jit(solution)/shard_map/ppermute | solution.py:329
  31.4 4.3 %collective-permute-start.8 = (bf16[16,32,128]{2,1,0:T(8,128)(2,1)S(1)}, bf16[16,32,128]{2,1,0:T(8,128)(2,1)S(1)}, u32[]{:S(2)}, u32[]{:S(2)}) collective-permute-start(bf16[16,32,128]{2,1,0:T(8,128)(2,1)S(1)} %get-tuple-element.34), channel_id=1, source_target_pairs={{0,0},{1,1},{2,2},{3,3},{4,4},{5,5},{6,6},{7,7},{8,8},{9,9},{10,10... | collective-permute-start | bytes 393224 | tf_op jit(solution)/shard_map/ppermute | solution.py:329
  35.7 3.5 %collective-permute-start.9 = (bf16[16,32,128]{2,1,0:T(8,128)(2,1)S(1)}, bf16[16,32,128]{2,1,0:T(8,128)(2,1)S(1)}, u32[]{:S(2)}, u32[]{:S(2)}) collective-permute-start(bf16[16,32,128]{2,1,0:T(8,128)(2,1)S(1)} %get-tuple-element.35), channel_id=1, source_target_pairs={{0,16},{1,17},{2,18},{3,19},{4,20},{5,21},{6,22},{7,23},{8,24},{9,... | collective-permute-start | bytes 393224 | tf_op jit(solution)/shard_map/ppermute | solution.py:329
  39.3 5.3 %all-to-all-done.refs_1_ = bf16[64,32,128]{2,1,0:T(8,128)(2,1)S(1)} async-done(((bf16[64,32,128]{2,1,0:T(8,128)(2,1)}), bf16[64,32,128]{2,1,0:T(8,128)(2,1)S(1)}, u32[]{:S(2)}, u32[]{:S(2)}) %all-to-all-start) | async-done | bytes 524320 | tf_op jit(solution)/shard_map/all_to_all | solution.py:345
  44.6 1.5 %change_rows.1.refs_2_ = bf16[32,8192]{1,0:T(8,128)(2,1)S(1)} custom-call(f32[32,8192]{1,0:T(8,128)S(1)} %get-tuple-element.24.refs_0_, bf16[64,32,128]{2,1,0:T(8,128)(2,1)S(1)} %all-to-all-done.refs_1_), custom_call_target="tpu_custom_call" | custom-call | flops 2097152 | bytes 2097152 | tf_op jit(solution)/shard_map/change_rows/pallas_call | solution.py:68
  46.0 3.1 %collective-permute-start.5 = (bf16[32,8192]{1,0:T(8,128)(2,1)S(1)}, bf16[32,8192]{1,0:T(8,128)(2,1)S(1)}, u32[]{:S(2)}, u32[]{:S(2)}) collective-permute-start(bf16[32,8192]{1,0:T(8,128)(2,1)S(1)} %change_rows.1.refs_2_), channel_id=1, source_target_pairs={{0,128},{64,192},{128,0},{192,64},{1,129},{65,193},{129,1},{193,65... | collective-permute-start | bytes 1572872 | tf_op jit(solution)/shard_map/ppermute | solution.py:83
  49.2 0.0 collective-permute-done.10.refs_2_
  49.2 0.0 collective-permute-done.11.refs_3_
  49.2 3.7 %collective-permute-done.8.refs_0_ = bf16[16,32,128]{2,1,0:T(8,128)(2,1)S(1)} collective-permute-done((bf16[16,32,128]{2,1,0:T(8,128)(2,1)S(1)}, bf16[16,32,128]{2,1,0:T(8,128)(2,1)S(1)}, u32[]{:S(2)}, u32[]{:S(2)}) %collective-permute-start.8) | collective-permute-done | bytes 131104 | tf_op jit(solution)/shard_map/ppermute | solution.py:329
  52.9 0.0 collective-permute-done.9.refs_1_
  52.9 0.8 %stack_pieces.1 = bf16[16,4,32,128]{3,2,1,0:T(8,128)(2,1)} custom-call(bf16[16,32,128]{2,1,0:T(8,128)(2,1)S(1)} %collective-permute-done.8.refs_0_, bf16[16,32,128]{2,1,0:T(8,128)(2,1)S(1)} %collective-permute-done.9.refs_1_, bf16[16,32,128]{2,1,0:T(8,128)(2,1)S(1)} %collective-permute-done.10.refs_2_, bf16[16,32,128]{2,1,0:T(8,128)(2,1)S(1)} %collective-permute-done.11.refs_3_), custom_call_target="tpu_custom_call" | custom-call | flops 2097152 | bytes 2097152 | tf_op jit(solution)/shard_map/stack_pieces/pallas_call | solution.py:68
  53.7 5.5 %all-to-all-start.1 = ((bf16[16,4,32,128]{3,2,1,0:T(8,128)(2,1)}), bf16[16,4,32,128]{3,2,1,0:T(8,128)(2,1)S(1)}, u32[]{:S(2)}, u32[]{:S(2)}) async-start(bf16[16,4,32,128]{3,2,1,0:T(8,128)(2,1)} %stack_pieces.1), calls=%async_computation.1 | async-start | bytes 1048576 | tf_op jit(solution)/shard_map/all_to_all | solution.py:350
  59.2 0.1 collective-permute-start.7
  59.3 0.0 collective-permute-done.5.refs_2_
  59.4 0.5 collective-permute-start.6
  59.8 1.4 %collective-permute-done.7.refs_3_ = bf16[32,8192]{1,0:T(8,128)(2,1)S(1)} collective-permute-done((bf16[32,8192]{1,0:T(8,128)(2,1)S(1)}, bf16[32,8192]{1,0:T(8,128)(2,1)S(1)}, u32[]{:S(2)}, u32[]{:S(2)}) %collective-permute-start.7) | collective-permute-done | bytes 524320 | tf_op jit(solution)/shard_map/ppermute | solution.py:83
  61.2 2.7 %outputs_of.3 = (bf16[128,8192]{1,0:T(8,128)(2,1)}, bf16[128,8192]{1,0:T(8,128)(2,1)}) custom-call(bf16[128,8192]{1,0:T(8,128)(2,1)} %bitcast.5, bf16[128,8192]{1,0:T(8,128)(2,1)} %refs_1_.7, bf16[32,8192]{1,0:T(8,128)(2,1)S(1)} %change_rows.1.refs_2_, bf16[32,8192]{1,0:T(8,128)(2,1)S(1)} %collective-permute-done.7.refs_3_), custom_call_target="tpu_custom_call" | custom-call | flops 2097152 | bytes 2097152 | tf_op jit(solution)/shard_map/outputs_of/pallas_call | solution.py:68
  64.0 2.2 %outputs_of.4 = (bf16[128,8192]{1,0:T(8,128)(2,1)}, bf16[128,8192]{1,0:T(8,128)(2,1)}) custom-call(bf16[128,8192]{1,0:T(8,128)(2,1)} %bitcast.6, bf16[128,8192]{1,0:T(8,128)(2,1)} %refs_1_.7, bf16[32,8192]{1,0:T(8,128)(2,1)S(1)} %collective-permute-done.5.refs_2_, ...), custom_call_target="tpu_custom_call", output_to_operand_aliasing={{0}: (3, {}), {1}: (4, {})} | custom-call | flops 2097152 | bytes 2097152 | tf_op jit(solution)/shard_map/outputs_of/pallas_call | solution.py:68
  66.2 0.0 collective-permute-done.6.refs_2_
  66.3 0.0 copy-start
  66.3 2.3 %outputs_of.5 = (bf16[128,8192]{1,0:T(8,128)(2,1)}, bf16[128,8192]{1,0:T(8,128)(2,1)}) custom-call(bf16[128,8192]{1,0:T(8,128)(2,1)} %bitcast.7, bf16[128,8192]{1,0:T(8,128)(2,1)} %refs_1_.7, bf16[32,8192]{1,0:T(8,128)(2,1)S(1)} %collective-permute-done.6.refs_2_, ...), custom_call_target="tpu_custom_call", output_to_operand_aliasing={{0}: (3, {}), {1}: (4, {})} | custom-call | flops 2097152 | bytes 2097152 | tf_op jit(solution)/shard_map/outputs_of/pallas_call | solution.py:68
  68.6 3.6 %all-to-all-done.1.refs_1_ = bf16[16,4,32,128]{3,2,1,0:T(8,128)(2,1)S(1)} async-done(((bf16[16,4,32,128]{3,2,1,0:T(8,128)(2,1)}), bf16[16,4,32,128]{3,2,1,0:T(8,128)(2,1)S(1)}, u32[]{:S(2)}, u32[]{:S(2)}) %all-to-all-start.1) | async-done | bytes 524320 | tf_op jit(solution)/shard_map/all_to_all | solution.py:350
  72.2 0.0 copy-done
  72.2 1.2 %new_momentum_of.1 = f32[2048,128]{1,0:T(8,128)} custom-call(bf16[128,8192]{1,0:T(8,128)(2,1)} %get-tuple-element.33.refs_0_, bf16[16,4,32,128]{3,2,1,0:T(8,128)(2,1)S(1)} %all-to-all-done.1.refs_1_, f32[2048,128]{1,0:T(8,128)S(1)} %copy-done), custom_call_target="tpu_custom_call" | custom-call | flops 2097152 | bytes 2097152 | tf_op jit(solution)/shard_map/new_momentum_of/pallas_call | solution.py:68
Async XLA Ops:
  2.2 3.7 %collective-permute-start = (bf16[64,8192]{1,0:T(8,128)(2,1)S(1)}, bf16[64,8192]{1,0:T(8,128)(2,1)S(1)}, u32[]{:S(2)}, u32[]{:S(2)}) collective-permute-start(bf16[64,8192]{1,0:T(8,128)(2,1)S(1)} %get-tuple-element.21), channel_id=1, source_target_pairs={{0,64},{64,0},{128,192},{192,128},{1,65},{65,1},{129,193},{193,129... | collective-permute-start | bytes 3145736 | tf_op jit(solution)/shard_map/ppermute | solution.py:83
  2.3 7.1 %collective-permute-start.2 = (bf16[16,32,128]{2,1,0:T(8,128)(2,1)S(1)}, bf16[16,32,128]{2,1,0:T(8,128)(2,1)S(1)}, u32[]{:S(2)}, u32[]{:S(2)}) collective-permute-start(bf16[16,32,128]{2,1,0:T(8,128)(2,1)S(1)} %get-tuple-element.25), channel_id=1, source_target_pairs={{0,196},{1,197},{2,198},{3,199},{4,192},{5,193},{6,194},{7,195},{8... | collective-permute-start | bytes 393224 | tf_op jit(solution)/shard_map/ppermute | solution.py:88
  4.0 5.6 %collective-permute-start.3 = (bf16[16,32,128]{2,1,0:T(8,128)(2,1)S(1)}, bf16[16,32,128]{2,1,0:T(8,128)(2,1)S(1)}, u32[]{:S(2)}, u32[]{:S(2)}) collective-permute-start(bf16[16,32,128]{2,1,0:T(8,128)(2,1)S(1)} %get-tuple-element.26), channel_id=1, source_target_pairs={{0,128},{64,192},{128,0},{192,64},{1,129},{65,193},{129,1},{193,65... | collective-permute-start | bytes 393224 | tf_op jit(solution)/shard_map/ppermute | solution.py:83
  5.9 3.7 %collective-permute-start.4 = (bf16[16,32,128]{2,1,0:T(8,128)(2,1)S(1)}, bf16[16,32,128]{2,1,0:T(8,128)(2,1)S(1)}, u32[]{:S(2)}, u32[]{:S(2)}) collective-permute-start(bf16[16,32,128]{2,1,0:T(8,128)(2,1)S(1)} %get-tuple-element.27), channel_id=1, source_target_pairs={{0,64},{64,0},{128,192},{192,128},{1,65},{65,1},{129,193},{193,129... | collective-permute-start | bytes 393224 | tf_op jit(solution)/shard_map/ppermute | solution.py:83
  8.1 15.3 %collective-permute-start.1 = (bf16[32,8192]{1,0:T(8,128)(2,1)S(1)}, bf16[32,8192]{1,0:T(8,128)(2,1)S(1)}, u32[]{:S(2)}, u32[]{:S(2)}) collective-permute-start(bf16[32,8192]{1,0:T(8,128)(2,1)S(1)} %get-tuple-element.23.refs_0_), channel_id=1, source_target_pairs={{0,128},{64,192},{128,0},{192,64},{1,129},{65,193},{129,1},{193,65... | collective-permute-start | bytes 1572872 | tf_op jit(solution)/shard_map/ppermute | solution.py:83
  10.5 34.0 %all-to-all-start = ((bf16[64,32,128]{2,1,0:T(8,128)(2,1)}), bf16[64,32,128]{2,1,0:T(8,128)(2,1)S(1)}, u32[]{:S(2)}, u32[]{:S(2)}) async-start(bf16[64,32,128]{2,1,0:T(8,128)(2,1)} %bitcast.1), calls=%async_computation | async-start | bytes 1048576 | tf_op jit(solution)/shard_map/all_to_all | solution.py:345
  24.9 24.3 %collective-permute-start.10 = (bf16[16,32,128]{2,1,0:T(8,128)(2,1)S(1)}, bf16[16,32,128]{2,1,0:T(8,128)(2,1)S(1)}, u32[]{:S(2)}, u32[]{:S(2)}) collective-permute-start(bf16[16,32,128]{2,1,0:T(8,128)(2,1)S(1)} %get-tuple-element.36), channel_id=1, source_target_pairs={{0,32},{1,33},{2,34},{3,35},{4,36},{5,37},{6,38},{7,39},{8,40},{9,... | collective-permute-start | bytes 393224 | tf_op jit(solution)/shard_map/ppermute | solution.py:329
  27.0 22.1 %collective-permute-start.11 = (bf16[16,32,128]{2,1,0:T(8,128)(2,1)S(1)}, bf16[16,32,128]{2,1,0:T(8,128)(2,1)S(1)}, u32[]{:S(2)}, u32[]{:S(2)}) collective-permute-start(bf16[16,32,128]{2,1,0:T(8,128)(2,1)S(1)} %get-tuple-element.37), channel_id=1, source_target_pairs={{0,48},{1,49},{2,50},{3,51},{4,52},{5,53},{6,54},{7,55},{8,56},{9,... | collective-permute-start | bytes 393224 | tf_op jit(solution)/shard_map/ppermute | solution.py:329
  31.4 21.5 %collective-permute-start.8 = (bf16[16,32,128]{2,1,0:T(8,128)(2,1)S(1)}, bf16[16,32,128]{2,1,0:T(8,128)(2,1)S(1)}, u32[]{:S(2)}, u32[]{:S(2)}) collective-permute-start(bf16[16,32,128]{2,1,0:T(8,128)(2,1)S(1)} %get-tuple-element.34), channel_id=1, source_target_pairs={{0,0},{1,1},{2,2},{3,3},{4,4},{5,5},{6,6},{7,7},{8,8},{9,9},{10,10... | collective-permute-start | bytes 393224 | tf_op jit(solution)/shard_map/ppermute | solution.py:329
  35.7 17.2 %collective-permute-start.9 = (bf16[16,32,128]{2,1,0:T(8,128)(2,1)S(1)}, bf16[16,32,128]{2,1,0:T(8,128)(2,1)S(1)}, u32[]{:S(2)}, u32[]{:S(2)}) collective-permute-start(bf16[16,32,128]{2,1,0:T(8,128)(2,1)S(1)} %get-tuple-element.35), channel_id=1, source_target_pairs={{0,16},{1,17},{2,18},{3,19},{4,20},{5,21},{6,22},{7,23},{8,24},{9,... | collective-permute-start | bytes 393224 | tf_op jit(solution)/shard_map/ppermute | solution.py:329
  46.0 13.3 %collective-permute-start.5 = (bf16[32,8192]{1,0:T(8,128)(2,1)S(1)}, bf16[32,8192]{1,0:T(8,128)(2,1)S(1)}, u32[]{:S(2)}, u32[]{:S(2)}) collective-permute-start(bf16[32,8192]{1,0:T(8,128)(2,1)S(1)} %change_rows.1.refs_2_), channel_id=1, source_target_pairs={{0,128},{64,192},{128,0},{192,64},{1,129},{65,193},{129,1},{193,65... | collective-permute-start | bytes 1572872 | tf_op jit(solution)/shard_map/ppermute | solution.py:83
  53.7 18.5 %all-to-all-start.1 = ((bf16[16,4,32,128]{3,2,1,0:T(8,128)(2,1)}), bf16[16,4,32,128]{3,2,1,0:T(8,128)(2,1)S(1)}, u32[]{:S(2)}, u32[]{:S(2)}) async-start(bf16[16,4,32,128]{3,2,1,0:T(8,128)(2,1)} %stack_pieces.1), calls=%async_computation.1 | async-start | bytes 1048576 | tf_op jit(solution)/shard_map/all_to_all | solution.py:350
  59.2 2.0 %collective-permute-start.7 = (bf16[32,8192]{1,0:T(8,128)(2,1)S(1)}, bf16[32,8192]{1,0:T(8,128)(2,1)S(1)}, u32[]{:S(2)}, u32[]{:S(2)}) collective-permute-start(bf16[32,8192]{1,0:T(8,128)(2,1)S(1)} %change_rows.1.refs_2_), channel_id=1, source_target_pairs={{0,64},{64,0},{128,192},{192,128},{1,65},{65,1},{129,193},{193,129... | collective-permute-start | bytes 1572872 | tf_op jit(solution)/shard_map/ppermute | solution.py:83
  59.4 6.9 %collective-permute-start.6 = (bf16[32,8192]{1,0:T(8,128)(2,1)S(1)}, bf16[32,8192]{1,0:T(8,128)(2,1)S(1)}, u32[]{:S(2)}, u32[]{:S(2)}) collective-permute-start(bf16[32,8192]{1,0:T(8,128)(2,1)S(1)} %collective-permute-done.5.refs_2_), channel_id=1, source_target_pairs={{0,64},{64,0},{128,192},{192,128},{1,65},{65,1},{129,193},{193,129... | collective-permute-start | bytes 1572872 | tf_op jit(solution)/shard_map/ppermute | solution.py:83
  66.3 5.9 %copy-start = (f32[2048,128]{1,0:T(8,128)S(1)}, f32[2048,128]{1,0:T(8,128)}, u32[]{:S(2)}) copy-start(f32[2048,128]{1,0:T(8,128)} %refs_2_.3) | copy-start | bytes 3145732

commit v7 on v6

--- a/solution.py
+++ b/solution.py
@@ -58,7 +58,8 @@
         return lax.axis_index("fsdp") // 16 if i else lax.axis_index("replica")
 
 
-def call(body, name, cost, outs, args, scratch, copies, aliases=None, near=None, out_near=False):
+def call(body, name, cost, outs, args, scratch, copies, aliases=None, near=None, out_near=False,
+         far=0):
     anywhere = pl.BlockSpec(memory_space=pl.ANY)
     whole = pl.BlockSpec(memory_space=pltpu.VMEM)
     near = len(args) if near is None else near
@@ -69,7 +70,7 @@
         lambda *refs: body(Place(), *refs),
         out_shape=outs,
         in_specs=[anywhere] * near + [whole] * (len(args) - near),
-        out_specs=out_spec if single else [out_spec] * count,
+        out_specs=out_spec if single else [anywhere] * far + [out_spec] * (count - far),
         scratch_shapes=[pltpu.VMEM(x.shape, x.dtype) for x in scratch]
         + [pltpu.SemaphoreType.DMA((copies,))],
         input_output_aliases=aliases or {},
@@ -171,7 +172,7 @@
 
 def average_rows(own, partial):
     def body(r_ref, own_ref, p_ref, avg_ref, *refs):
-        outs, (x, q, avg, cut, sems) = refs[:4], refs[4:]
+        outs, (x, q, avg, sems) = refs[:4], refs[4:]
         copies = Copies(sems)
         loads = []
         for k in range(4):
@@ -190,28 +191,27 @@
                 avg[k, :, cols] = y
                 narrow = y.astype(BF)
                 for n in range(INNER // 128):
-                    cut[k, i * (INNER // 128) + n] = narrow[:, n * 128 : (n + 1) * 128]
+                    outs[k][i * (INNER // 128) + n] = narrow[:, n * 128 : (n + 1) * 128]
                 return carry
 
             lax.fori_loop(0, WIDTH // INNER, step, 0, unroll=True)
-            copies.send(cut.at[k], outs[k])
             copies.send(avg.at[k], avg_ref.at[:, at(peer(r_ref[0], k) * WIDTH, WIDTH)])
         copies.finish()
 
     return call(
         body, "average_rows", LONG, [shape(32, 8192, dtype=F32)] + [shape(16, 32, 128)] * 4,
         [own, partial],
-        [shape(4, 32, WIDTH)] * 2 + [shape(4, 32, WIDTH, dtype=F32), shape(4, 16, 32, 128)], 16,
+        [shape(4, 32, WIDTH)] * 2 + [shape(4, 32, WIDTH, dtype=F32)], 12, out_near=True, far=1,
     )
 
 
 def stack_pieces(pieces):
     def body(r_ref, *refs):
         for k in range(4):
-            refs[4][:, k] = refs[k][...]
-
-    return call(
-        body, "stack_pieces", SHORT, shape(16, 4, 32, 128), [*pieces], [], 1,
+            refs[4][:, k] = refs[3 - k][...]
+
+    return call(
+        body, "stack_pieces", SHORT, shape(16, 4, 32, 128), pieces[::-1], [], 1,
         near=0, out_near=True,
     )
 

time: 73.8 us -> 73.1 us (level)
  starting transfers between devices: 41.5 us -> 39.8 us
  waiting for transfers between devices: 14.2 us -> 15.9 us
    ppermute x7, starting transfers between devices: 7.01 us -> 3.98 us  [swap(): return lax.ppermute(x, 'replica', [(i, i ^ k) for i in range(4)])]
    all_to_all x1, waiting for transfers between devices: 5.31 us -> 7.86 us  [local(): m_rows = lax.all_to_all(by_row, 'fsdp', 0, 0, tiled=True)]
    all_to_all x1, starting transfers between devices: 5.51 us -> 6.84 us  [local(): lax.all_to_all(cut, 'fsdp', 0, 0, axis_index_groups=groups, tiled=True)]
    all_to_all x1, waiting for transfers between devices: 3.61 us -> 2.52 us  [local(): lax.all_to_all(cut, 'fsdp', 0, 0, axis_index_groups=groups, tiled=True)]
  transfers between devices with their start and end apart: 14 -> 14, of which waited for: 5 -> 7; matrix products, arithmetic and copies ran while one was open for 0% -> 0% of each run, Pallas kernels for 19% -> 18%
where the time goes in v7:
time: 73.1 us; the launch traced here: 72.7 us
  starting transfers between devices  39.8 us (54%)
  Pallas kernels  16.2 us (22%)
  waiting for transfers between devices  15.9 us (22%)
  between operations  0.8 us (1%)
    pallas_call x10, Pallas kernels, call(): pl.pallas_call(lambda *refs: body(Place(), *refs), out_shape=outs, in_spe...  16.2 us
    ppermute x4, starting transfers between devices, across(): return lax.ppermute(x, ('replica', 'fsdp'), pairs)  14.4 us
    all_to_all x1, starting transfers between devices, local(): m_rows = lax.all_to_all(by_row, 'fsdp', 0, 0, tiled=True)  12.9 us
    all_to_all x1, waiting for transfers between devices, local(): m_rows = lax.all_to_all(by_row, 'fsdp', 0, 0, tiled=True)  7.86 us
    all_to_all x1, starting transfers between devices, local(): lax.all_to_all(cut, 'fsdp', 0, 0, axis_index_groups=groups, tiled=True)  6.84 us
    ppermute x7, starting transfers between devices, swap(): return lax.ppermute(x, 'replica', [(i, i ^ k) for i in range(4)])  3.98 us
    ppermute x4, waiting for transfers between devices, across(): return lax.ppermute(x, ('replica', 'fsdp'), pairs)  3.95 us
    all_to_all x1, waiting for transfers between devices, local(): lax.all_to_all(cut, 'fsdp', 0, 0, axis_index_groups=groups, tiled=True)  2.52 us
  transfers between devices with their start and end apart: 14, of which 7 were waited for; matrix products, arithmetic and copies ran while one was open for 0% of the time, Pallas kernels for 18%

profile of v7, /device:TPU:8, one launch (start us, length us, event | category | flops | bytes accessed | tf_op | source)
XLA Modules:
  0.0 72.7 jit_solution(1893150715182012020)
XLA Ops:
  0.6 1.6 %prologue.1 = (bf16[64,8192]{1,0:T(8,128)(2,1)S(1)}, bf16[16,32,128]{2,1,0:T(8,128)(2,1)S(1)}, bf16[16,32,128]{2,1,0:T(8,128)(2,1)S(1)}, bf16[16,32,128]{2,1,0:T(8,128)(2,1)S(1)}, bf16[16,32,128]{2,1,0:T(8,128)(2,1)S(1)}) custom-call(bf16[128,8192]{1,0:T(8,128)(2,1)} %bitcast.3, f32[2048,128]{1,0:T(8,128)} %refs_2_.3), custom_call_target="tpu_custom_call" | custom-call | flops 2097152 | bytes 2097152 | tf_op jit(solution)/shard_map/prologue/pallas_call | solution.py:69
  2.2 0.1 collective-permute-start
  2.3 1.7 %collective-permute-start.2 = (bf16[16,32,128]{2,1,0:T(8,128)(2,1)S(1)}, bf16[16,32,128]{2,1,0:T(8,128)(2,1)S(1)}, u32[]{:S(2)}, u32[]{:S(2)}) collective-permute-start(bf16[16,32,128]{2,1,0:T(8,128)(2,1)S(1)} %get-tuple-element.25), channel_id=1, source_target_pairs={{0,196},{1,197},{2,198},{3,199},{4,192},{5,193},{6,194},{7,195},{8... | collective-permute-start | bytes 393224 | tf_op jit(solution)/shard_map/ppermute | solution.py:89
  4.0 1.9 %collective-permute-start.3 = (bf16[16,32,128]{2,1,0:T(8,128)(2,1)S(1)}, bf16[16,32,128]{2,1,0:T(8,128)(2,1)S(1)}, u32[]{:S(2)}, u32[]{:S(2)}) collective-permute-start(bf16[16,32,128]{2,1,0:T(8,128)(2,1)S(1)} %get-tuple-element.26), channel_id=1, source_target_pairs={{0,128},{64,192},{128,0},{192,64},{1,129},{65,193},{129,1},{193,65... | collective-permute-start | bytes 393224 | tf_op jit(solution)/shard_map/ppermute | solution.py:84
  5.9 0.0 collective-permute-start.4
  5.9 0.0 collective-permute-done.refs_1_
  5.9 2.2 %partial_rows.1 = (bf16[32,8192]{1,0:T(8,128)(2,1)S(1)}, bf16[32,8192]{1,0:T(8,128)(2,1)S(1)}) custom-call(bf16[128,8192]{1,0:T(8,128)(2,1)} %bitcast.4, bf16[64,8192]{1,0:T(8,128)(2,1)S(1)} %collective-permute-done.refs_1_, bf16[128,8192]{1,0:T(8,128)(2,1)} %refs_1_.7), custom_call_target="tpu_custom_call" | custom-call | flops 2097152 | bytes 2097152 | tf_op jit(solution)/shard_map/partial_rows/pallas_call | solution.py:69
  8.1 1.3 %collective-permute-start.1 = (bf16[32,8192]{1,0:T(8,128)(2,1)S(1)}, bf16[32,8192]{1,0:T(8,128)(2,1)S(1)}, u32[]{:S(2)}, u32[]{:S(2)}) collective-permute-start(bf16[32,8192]{1,0:T(8,128)(2,1)S(1)} %get-tuple-element.23.refs_0_), channel_id=1, source_target_pairs={{0,128},{64,192},{128,0},{192,64},{1,129},{65,193},{129,1},{193,65... | collective-permute-start | bytes 1572872 | tf_op jit(solution)/shard_map/ppermute | solution.py:84
  9.5 0.0 collective-permute-done.2.refs_1_
  9.5 0.2 collective-permute-done.3.refs_2_
  9.7 0.0 collective-permute-done.4.refs_3_
  9.7 0.8 %in_order.1 = bf16[4,16,32,128]{3,2,1,0:T(8,128)(2,1)} custom-call(bf16[32,8192]{1,0:T(8,128)(2,1)S(1)} %get-tuple-element.23.refs_0_, bf16[16,32,128]{2,1,0:T(8,128)(2,1)S(1)} %collective-permute-done.2.refs_1_, bf16[16,32,128]{2,1,0:T(8,128)(2,1)S(1)} %collective-permute-done.3.refs_2_, bf16[16,32,128]{2,1,0:T(8,128)(2,1)S(1)} %collective-permute-done.4.refs_3_, ...), custom_call_target="tpu_custom_call" | custom-call | flops 17179869184 | bytes 17179869184 | tf_op jit(solution)/shard_map/in_order/pallas_call | solution.py:69
  10.5 12.9 %all-to-all-start = ((bf16[64,32,128]{2,1,0:T(8,128)(2,1)}), bf16[64,32,128]{2,1,0:T(8,128)(2,1)S(1)}, u32[]{:S(2)}, u32[]{:S(2)}) async-start(bf16[64,32,128]{2,1,0:T(8,128)(2,1)} %bitcast.1), calls=%async_computation | async-start | bytes 1048576 | tf_op jit(solution)/shard_map/all_to_all | solution.py:345
  23.4 0.0 collective-permute-done.1.refs_1_
  23.5 0.7 average_rows.1
  24.2 5.4 %collective-permute-start.10 = (bf16[16,32,128]{2,1,0:T(8,128)(2,1)S(1)}, bf16[16,32,128]{2,1,0:T(8,128)(2,1)S(1)}, u32[]{:S(2)}, u32[]{:S(2)}) collective-permute-start(bf16[16,32,128]{2,1,0:T(8,128)(2,1)S(1)} %get-tuple-element.36), channel_id=1, source_target_pairs={{0,16},{1,17},{2,18},{3,19},{4,20},{5,21},{6,22},{7,23},{8,24},{9,... | collective-permute-start | bytes 393224 | tf_op jit(solution)/shard_map/ppermute | solution.py:329
  29.6 3.6 %collective-permute-start.11 = (bf16[16,32,128]{2,1,0:T(8,128)(2,1)S(1)}, bf16[16,32,128]{2,1,0:T(8,128)(2,1)S(1)}, u32[]{:S(2)}, u32[]{:S(2)}) collective-permute-start(bf16[16,32,128]{2,1,0:T(8,128)(2,1)S(1)} %get-tuple-element.37), channel_id=1, source_target_pairs={{0,0},{1,1},{2,2},{3,3},{4,4},{5,5},{6,6},{7,7},{8,8},{9,9},{10,10... | collective-permute-start | bytes 393224 | tf_op jit(solution)/shard_map/ppermute | solution.py:329
  33.2 0.1 collective-permute-start.8
  33.3 5.3 %collective-permute-start.9 = (bf16[16,32,128]{2,1,0:T(8,128)(2,1)S(1)}, bf16[16,32,128]{2,1,0:T(8,128)(2,1)S(1)}, u32[]{:S(2)}, u32[]{:S(2)}) collective-permute-start(bf16[16,32,128]{2,1,0:T(8,128)(2,1)S(1)} %get-tuple-element.35), channel_id=1, source_target_pairs={{0,32},{1,33},{2,34},{3,35},{4,36},{5,37},{6,38},{7,39},{8,40},{9,... | collective-permute-start | bytes 393224 | tf_op jit(solution)/shard_map/ppermute | solution.py:329
  38.6 7.9 %all-to-all-done.refs_1_ = bf16[64,32,128]{2,1,0:T(8,128)(2,1)S(1)} async-done(((bf16[64,32,128]{2,1,0:T(8,128)(2,1)}), bf16[64,32,128]{2,1,0:T(8,128)(2,1)S(1)}, u32[]{:S(2)}, u32[]{:S(2)}) %all-to-all-start) | async-done | bytes 524320 | tf_op jit(solution)/shard_map/all_to_all | solution.py:345
  46.4 1.5 %change_rows.1.refs_2_ = bf16[32,8192]{1,0:T(8,128)(2,1)S(1)} custom-call(f32[32,8192]{1,0:T(8,128)S(1)} %get-tuple-element.24.refs_0_, bf16[64,32,128]{2,1,0:T(8,128)(2,1)S(1)} %all-to-all-done.refs_1_), custom_call_target="tpu_custom_call" | custom-call | flops 2097152 | bytes 2097152 | tf_op jit(solution)/shard_map/change_rows/pallas_call | solution.py:69
  47.9 0.1 collective-permute-start.5
  48.0 0.0 collective-permute-done.10.refs_2_
  48.0 1.4 %collective-permute-done.11.refs_3_ = bf16[16,32,128]{2,1,0:T(8,128)(2,1)S(1)} collective-permute-done((bf16[16,32,128]{2,1,0:T(8,128)(2,1)S(1)}, bf16[16,32,128]{2,1,0:T(8,128)(2,1)S(1)}, u32[]{:S(2)}, u32[]{:S(2)}) %collective-permute-start.11) | collective-permute-done | bytes 131104 | tf_op jit(solution)/shard_map/ppermute | solution.py:329
  49.4 1.7 %collective-permute-done.8.refs_0_ = bf16[16,32,128]{2,1,0:T(8,128)(2,1)S(1)} collective-permute-done((bf16[16,32,128]{2,1,0:T(8,128)(2,1)S(1)}, bf16[16,32,128]{2,1,0:T(8,128)(2,1)S(1)}, u32[]{:S(2)}, u32[]{:S(2)}) %collective-permute-start.8) | collective-permute-done | bytes 131104 | tf_op jit(solution)/shard_map/ppermute | solution.py:329
  51.1 0.8 %collective-permute-done.9.refs_1_ = bf16[16,32,128]{2,1,0:T(8,128)(2,1)S(1)} collective-permute-done((bf16[16,32,128]{2,1,0:T(8,128)(2,1)S(1)}, bf16[16,32,128]{2,1,0:T(8,128)(2,1)S(1)}, u32[]{:S(2)}, u32[]{:S(2)}) %collective-permute-start.9) | collective-permute-done | bytes 131104 | tf_op jit(solution)/shard_map/ppermute | solution.py:329
  51.9 0.8 %stack_pieces.1 = bf16[16,4,32,128]{3,2,1,0:T(8,128)(2,1)} custom-call(bf16[16,32,128]{2,1,0:T(8,128)(2,1)S(1)} %collective-permute-done.8.refs_0_, bf16[16,32,128]{2,1,0:T(8,128)(2,1)S(1)} %collective-permute-done.9.refs_1_, bf16[16,32,128]{2,1,0:T(8,128)(2,1)S(1)} %collective-permute-done.10.refs_2_, bf16[16,32,128]{2,1,0:T(8,128)(2,1)S(1)} %collective-permute-done.11.refs_3_), custom_call_target="tpu_custom_call" | custom-call | flops 2097152 | bytes 2097152 | tf_op jit(solution)/shard_map/stack_pieces/pallas_call | solution.py:69
  52.8 6.8 %all-to-all-start.1 = ((bf16[16,4,32,128]{3,2,1,0:T(8,128)(2,1)}), bf16[16,4,32,128]{3,2,1,0:T(8,128)(2,1)S(1)}, u32[]{:S(2)}, u32[]{:S(2)}) async-start(bf16[16,4,32,128]{3,2,1,0:T(8,128)(2,1)} %stack_pieces.1), calls=%async_computation.1 | async-start | bytes 1048576 | tf_op jit(solution)/shard_map/all_to_all | solution.py:350
  59.6 0.1 collective-permute-start.7
  59.7 0.0 collective-permute-done.5.refs_2_
  59.7 0.5 collective-permute-start.6
  60.2 1.4 %collective-permute-done.7.refs_3_ = bf16[32,8192]{1,0:T(8,128)(2,1)S(1)} collective-permute-done((bf16[32,8192]{1,0:T(8,128)(2,1)S(1)}, bf16[32,8192]{1,0:T(8,128)(2,1)S(1)}, u32[]{:S(2)}, u32[]{:S(2)}) %collective-permute-start.7) | collective-permute-done | bytes 524320 | tf_op jit(solution)/shard_map/ppermute | solution.py:84
  61.6 2.7 %outputs_of.3 = (bf16[128,8192]{1,0:T(8,128)(2,1)}, bf16[128,8192]{1,0:T(8,128)(2,1)}) custom-call(bf16[128,8192]{1,0:T(8,128)(2,1)} %bitcast.5, bf16[128,8192]{1,0:T(8,128)(2,1)} %refs_1_.7, bf16[32,8192]{1,0:T(8,128)(2,1)S(1)} %change_rows.1.refs_2_, bf16[32,8192]{1,0:T(8,128)(2,1)S(1)} %collective-permute-done.7.refs_3_), custom_call_target="tpu_custom_call" | custom-call | flops 2097152 | bytes 2097152 | tf_op jit(solution)/shard_map/outputs_of/pallas_call | solution.py:69
  64.4 2.2 %outputs_of.4 = (bf16[128,8192]{1,0:T(8,128)(2,1)}, bf16[128,8192]{1,0:T(8,128)(2,1)}) custom-call(bf16[128,8192]{1,0:T(8,128)(2,1)} %bitcast.6, bf16[128,8192]{1,0:T(8,128)(2,1)} %refs_1_.7, bf16[32,8192]{1,0:T(8,128)(2,1)S(1)} %collective-permute-done.5.refs_2_, ...), custom_call_target="tpu_custom_call", output_to_operand_aliasing={{0}: (3, {}), {1}: (4, {})} | custom-call | flops 2097152 | bytes 2097152 | tf_op jit(solution)/shard_map/outputs_of/pallas_call | solution.py:69
  66.6 0.0 collective-permute-done.6.refs_2_
  66.7 0.0 copy-start
  66.7 2.3 %outputs_of.5 = (bf16[128,8192]{1,0:T(8,128)(2,1)}, bf16[128,8192]{1,0:T(8,128)(2,1)}) custom-call(bf16[128,8192]{1,0:T(8,128)(2,1)} %bitcast.7, bf16[128,8192]{1,0:T(8,128)(2,1)} %refs_1_.7, bf16[32,8192]{1,0:T(8,128)(2,1)S(1)} %collective-permute-done.6.refs_2_, ...), custom_call_target="tpu_custom_call", output_to_operand_aliasing={{0}: (3, {}), {1}: (4, {})} | custom-call | flops 2097152 | bytes 2097152 | tf_op jit(solution)/shard_map/outputs_of/pallas_call | solution.py:69
  69.0 2.5 %all-to-all-done.1.refs_1_ = bf16[16,4,32,128]{3,2,1,0:T(8,128)(2,1)S(1)} async-done(((bf16[16,4,32,128]{3,2,1,0:T(8,128)(2,1)}), bf16[16,4,32,128]{3,2,1,0:T(8,128)(2,1)S(1)}, u32[]{:S(2)}, u32[]{:S(2)}) %all-to-all-start.1) | async-done | bytes 524320 | tf_op jit(solution)/shard_map/all_to_all | solution.py:350
  71.5 0.0 copy-done
  71.5 1.2 %new_momentum_of.1 = f32[2048,128]{1,0:T(8,128)} custom-call(bf16[128,8192]{1,0:T(8,128)(2,1)} %get-tuple-element.33.refs_0_, bf16[16,4,32,128]{3,2,1,0:T(8,128)(2,1)S(1)} %all-to-all-done.1.refs_1_, f32[2048,128]{1,0:T(8,128)S(1)} %copy-done), custom_call_target="tpu_custom_call" | custom-call | flops 2097152 | bytes 2097152 | tf_op jit(solution)/shard_map/new_momentum_of/pallas_call | solution.py:69
Async XLA Ops:
  2.2 3.7 %collective-permute-start = (bf16[64,8192]{1,0:T(8,128)(2,1)S(1)}, bf16[64,8192]{1,0:T(8,128)(2,1)S(1)}, u32[]{:S(2)}, u32[]{:S(2)}) collective-permute-start(bf16[64,8192]{1,0:T(8,128)(2,1)S(1)} %get-tuple-element.21), channel_id=1, source_target_pairs={{0,64},{64,0},{128,192},{192,128},{1,65},{65,1},{129,193},{193,129... | collective-permute-start | bytes 3145736 | tf_op jit(solution)/shard_map/ppermute | solution.py:84
  2.3 7.1 %collective-permute-start.2 = (bf16[16,32,128]{2,1,0:T(8,128)(2,1)S(1)}, bf16[16,32,128]{2,1,0:T(8,128)(2,1)S(1)}, u32[]{:S(2)}, u32[]{:S(2)}) collective-permute-start(bf16[16,32,128]{2,1,0:T(8,128)(2,1)S(1)} %get-tuple-element.25), channel_id=1, source_target_pairs={{0,196},{1,197},{2,198},{3,199},{4,192},{5,193},{6,194},{7,195},{8... | collective-permute-start | bytes 393224 | tf_op jit(solution)/shard_map/ppermute | solution.py:89
  4.0 5.6 %collective-permute-start.3 = (bf16[16,32,128]{2,1,0:T(8,128)(2,1)S(1)}, bf16[16,32,128]{2,1,0:T(8,128)(2,1)S(1)}, u32[]{:S(2)}, u32[]{:S(2)}) collective-permute-start(bf16[16,32,128]{2,1,0:T(8,128)(2,1)S(1)} %get-tuple-element.26), channel_id=1, source_target_pairs={{0,128},{64,192},{128,0},{192,64},{1,129},{65,193},{129,1},{193,65... | collective-permute-start | bytes 393224 | tf_op jit(solution)/shard_map/ppermute | solution.py:84
  5.9 3.7 %collective-permute-start.4 = (bf16[16,32,128]{2,1,0:T(8,128)(2,1)S(1)}, bf16[16,32,128]{2,1,0:T(8,128)(2,1)S(1)}, u32[]{:S(2)}, u32[]{:S(2)}) collective-permute-start(bf16[16,32,128]{2,1,0:T(8,128)(2,1)S(1)} %get-tuple-element.27), channel_id=1, source_target_pairs={{0,64},{64,0},{128,192},{192,128},{1,65},{65,1},{129,193},{193,129... | collective-permute-start | bytes 393224 | tf_op jit(solution)/shard_map/ppermute | solution.py:84
  8.1 15.3 %collective-permute-start.1 = (bf16[32,8192]{1,0:T(8,128)(2,1)S(1)}, bf16[32,8192]{1,0:T(8,128)(2,1)S(1)}, u32[]{:S(2)}, u32[]{:S(2)}) collective-permute-start(bf16[32,8192]{1,0:T(8,128)(2,1)S(1)} %get-tuple-element.23.refs_0_), channel_id=1, source_target_pairs={{0,128},{64,192},{128,0},{192,64},{1,129},{65,193},{129,1},{193,65... | collective-permute-start | bytes 1572872 | tf_op jit(solution)/shard_map/ppermute | solution.py:84
  10.5 35.9 %all-to-all-start = ((bf16[64,32,128]{2,1,0:T(8,128)(2,1)}), bf16[64,32,128]{2,1,0:T(8,128)(2,1)S(1)}, u32[]{:S(2)}, u32[]{:S(2)}) async-start(bf16[64,32,128]{2,1,0:T(8,128)(2,1)} %bitcast.1), calls=%async_computation | async-start | bytes 1048576 | tf_op jit(solution)/shard_map/all_to_all | solution.py:345
  24.2 23.8 %collective-permute-start.10 = (bf16[16,32,128]{2,1,0:T(8,128)(2,1)S(1)}, bf16[16,32,128]{2,1,0:T(8,128)(2,1)S(1)}, u32[]{:S(2)}, u32[]{:S(2)}) collective-permute-start(bf16[16,32,128]{2,1,0:T(8,128)(2,1)S(1)} %get-tuple-element.36), channel_id=1, source_target_pairs={{0,16},{1,17},{2,18},{3,19},{4,20},{5,21},{6,22},{7,23},{8,24},{9,... | collective-permute-start | bytes 393224 | tf_op jit(solution)/shard_map/ppermute | solution.py:329
  29.6 19.9 %collective-permute-start.11 = (bf16[16,32,128]{2,1,0:T(8,128)(2,1)S(1)}, bf16[16,32,128]{2,1,0:T(8,128)(2,1)S(1)}, u32[]{:S(2)}, u32[]{:S(2)}) collective-permute-start(bf16[16,32,128]{2,1,0:T(8,128)(2,1)S(1)} %get-tuple-element.37), channel_id=1, source_target_pairs={{0,0},{1,1},{2,2},{3,3},{4,4},{5,5},{6,6},{7,7},{8,8},{9,9},{10,10... | collective-permute-start | bytes 393224 | tf_op jit(solution)/shard_map/ppermute | solution.py:329
  33.2 17.9 %collective-permute-start.8 = (bf16[16,32,128]{2,1,0:T(8,128)(2,1)S(1)}, bf16[16,32,128]{2,1,0:T(8,128)(2,1)S(1)}, u32[]{:S(2)}, u32[]{:S(2)}) collective-permute-start(bf16[16,32,128]{2,1,0:T(8,128)(2,1)S(1)} %get-tuple-element.34), channel_id=1, source_target_pairs={{0,48},{1,49},{2,50},{3,51},{4,52},{5,53},{6,54},{7,55},{8,56},{9,... | collective-permute-start | bytes 393224 | tf_op jit(solution)/shard_map/ppermute | solution.py:329
  33.3 18.7 %collective-permute-start.9 = (bf16[16,32,128]{2,1,0:T(8,128)(2,1)S(1)}, bf16[16,32,128]{2,1,0:T(8,128)(2,1)S(1)}, u32[]{:S(2)}, u32[]{:S(2)}) collective-permute-start(bf16[16,32,128]{2,1,0:T(8,128)(2,1)S(1)} %get-tuple-element.35), channel_id=1, source_target_pairs={{0,32},{1,33},{2,34},{3,35},{4,36},{5,37},{6,38},{7,39},{8,40},{9,... | collective-permute-start | bytes 393224 | tf_op jit(solution)/shard_map/ppermute | solution.py:329
  47.9 11.9 %collective-permute-start.5 = (bf16[32,8192]{1,0:T(8,128)(2,1)S(1)}, bf16[32,8192]{1,0:T(8,128)(2,1)S(1)}, u32[]{:S(2)}, u32[]{:S(2)}) collective-permute-start(bf16[32,8192]{1,0:T(8,128)(2,1)S(1)} %change_rows.1.refs_2_), channel_id=1, source_target_pairs={{0,128},{64,192},{128,0},{192,64},{1,129},{65,193},{129,1},{193,65... | collective-permute-start | bytes 1572872 | tf_op jit(solution)/shard_map/ppermute | solution.py:84
  52.8 18.7 %all-to-all-start.1 = ((bf16[16,4,32,128]{3,2,1,0:T(8,128)(2,1)}), bf16[16,4,32,128]{3,2,1,0:T(8,128)(2,1)S(1)}, u32[]{:S(2)}, u32[]{:S(2)}) async-start(bf16[16,4,32,128]{3,2,1,0:T(8,128)(2,1)} %stack_pieces.1), calls=%async_computation.1 | async-start | bytes 1048576 | tf_op jit(solution)/shard_map/all_to_all | solution.py:350
  59.6 2.0 %collective-permute-start.7 = (bf16[32,8192]{1,0:T(8,128)(2,1)S(1)}, bf16[32,8192]{1,0:T(8,128)(2,1)S(1)}, u32[]{:S(2)}, u32[]{:S(2)}) collective-permute-start(bf16[32,8192]{1,0:T(8,128)(2,1)S(1)} %change_rows.1.refs_2_), channel_id=1, source_target_pairs={{0,64},{64,0},{128,192},{192,128},{1,65},{65,1},{129,193},{193,129... | collective-permute-start | bytes 1572872 | tf_op jit(solution)/shard_map/ppermute | solution.py:84
  59.7 6.9 %collective-permute-start.6 = (bf16[32,8192]{1,0:T(8,128)(2,1)S(1)}, bf16[32,8192]{1,0:T(8,128)(2,1)S(1)}, u32[]{:S(2)}, u32[]{:S(2)}) collective-permute-start(bf16[32,8192]{1,0:T(8,128)(2,1)S(1)} %collective-permute-done.5.refs_2_), channel_id=1, source_target_pairs={{0,64},{64,0},{128,192},{192,128},{1,65},{65,1},{129,193},{193,129... | collective-permute-start | bytes 1572872 | tf_op jit(solution)/shard_map/ppermute | solution.py:84
  66.7 4.9 %copy-start = (f32[2048,128]{1,0:T(8,128)S(1)}, f32[2048,128]{1,0:T(8,128)}, u32[]{:S(2)}) copy-start(f32[2048,128]{1,0:T(8,128)} %refs_2_.3) | copy-start | bytes 3145732

commit v8 on v7

--- a/solution.py
+++ b/solution.py
@@ -131,7 +131,7 @@
 
 
 def partial_rows(local, theirs, anchor):
-    def body(r_ref, l_ref, t_ref, a_ref, other_ref, own_ref, l, t, a, o, own, sems):
+    def body(r_ref, l_ref, t_ref, a_ref, own_ref, other_ref, l, t, a, own, sems):
         copies = Copies(sems)
         loads = []
         for k in (2, 0):
@@ -149,24 +149,29 @@
         for i, waits in enumerate(loads):
             for load in waits:
                 load.wait()
-            to, p = (o if i < PARTS else own), i % PARTS
-
-            def step(cols, i=i, p=p, to=to):
+            p = i % PARTS
+
+            def step(n, carry, i=i, p=p):
+                cols = at(n * INNER, INNER)
                 x = a[i, :, cols].astype(F32)
                 total = (x - l[i, :, cols].astype(F32)) + (x - t[i, :, cols].astype(F32))
-                to[p, :, cols] = total.astype(to.dtype)
-
-            inner(step)
-            to_ref = other_ref if i < PARTS else own_ref
-            copies.send(to.at[p], to_ref.at[:, pl.ds(p * WIDTH, WIDTH)])
+                if i < PARTS:
+                    other_ref[:, at(p * WIDTH + n * INNER, INNER)] = total.astype(BF)
+                else:
+                    own[p, :, cols] = total.astype(BF)
+                return carry
+
+            lax.fori_loop(0, WIDTH // INNER, step, 0, unroll=True)
+            if i >= PARTS:
+                copies.send(own.at[p], own_ref.at[:, pl.ds(p * WIDTH, WIDTH)])
         copies.finish()
 
     return call(
         body, "partial_rows", SHORT, [shape(32, 8192)] * 2,
         [local, theirs, anchor],
         [shape(2 * PARTS, 32, WIDTH)] * 3
-        + [shape(PARTS, 32, WIDTH)] * 2,
-        8 * PARTS,
+        + [shape(PARTS, 32, WIDTH)],
+        7 * PARTS, out_near=True, far=1,
     )
 
 
@@ -252,11 +257,11 @@
 def new_momentum_of(momentum, pieces, after):
     def body(rg_ref, after_ref, p_ref, m_ref, o_ref, q, o, sems):
         copies = Copies(sems)
-        copies.send(p_ref, q)
-        copies.finish()
-        copies.open = []
+        loads = [copies.start(p_ref.at[pl.ds(8 * i, 8)], q.at[pl.ds(8 * i, 8)]) for i in range(2)]
         r, g = rg_ref[0], rg_ref[1]
         for p in range(4):
+            if p % 2 == 0:
+                loads[p // 2].wait()
             for k in range(4):
                 other = peer(g, k)
                 flip = jnp.where(other // 2 == r // 2, 0, 4)
@@ -270,7 +275,7 @@
 
     return call(
         body, "new_momentum_of", SHORT, shape(2048, 128, dtype=F32),
-        [after, pieces, momentum], [shape(16, 4, 32, 128), shape(4, 512, 128, dtype=F32)], 5,
+        [after, pieces, momentum], [shape(16, 4, 32, 128), shape(4, 512, 128, dtype=F32)], 6,
         near=2,
     )
 
@@ -339,7 +344,7 @@
     half, *pieces = prologue(own, in_hbm(momentum))
     theirs = swap(half, 1)
     pieces = [pieces[0], swap(pieces[1], 1), swap(pieces[2], 2), swap_around(pieces[3])]
-    for_other, mine = partial_rows(own, theirs, anchor)
+    mine, for_other = partial_rows(own, theirs, anchor)
     partial = swap(for_other, 2)
     by_row = in_order(pieces, for_other).reshape(64, 32, 128)
     m_rows = lax.all_to_all(by_row, "fsdp", 0, 0, tiled=True)

time: 73.1 us -> 73.1 us (level)
  no operation moved by 1% of the time
where the time goes in v8:
time: 73.1 us; the launch traced here: 72.7 us
  starting transfers between devices  39.7 us (54%)
  waiting for transfers between devices  16.1 us (22%)
  Pallas kernels  16 us (22%)
  between operations  0.8 us (1%)
    pallas_call x10, Pallas kernels, call(): pl.pallas_call(lambda *refs: body(Place(), *refs), out_shape=outs, in_spe...  16 us
    ppermute x4, starting transfers between devices, across(): return lax.ppermute(x, ('replica', 'fsdp'), pairs)  14.3 us
    all_to_all x1, starting transfers between devices, local(): m_rows = lax.all_to_all(by_row, 'fsdp', 0, 0, tiled=True)  12.9 us
    all_to_all x1, waiting for transfers between devices, local(): m_rows = lax.all_to_all(by_row, 'fsdp', 0, 0, tiled=True)  7.95 us
    all_to_all x1, starting transfers between devices, local(): lax.all_to_all(cut, 'fsdp', 0, 0, axis_index_groups=groups, tiled=True)  6.84 us
    ppermute x7, starting transfers between devices, swap(): return lax.ppermute(x, 'replica', [(i, i ^ k) for i in range(4)])  3.98 us
    ppermute x4, waiting for transfers between devices, across(): return lax.ppermute(x, ('replica', 'fsdp'), pairs)  3.95 us
    all_to_all x1, waiting for transfers between devices, local(): lax.all_to_all(cut, 'fsdp', 0, 0, axis_index_groups=groups, tiled=True)  2.52 us
  transfers between devices with their start and end apart: 14, of which 7 were waited for; matrix products, arithmetic and copies ran while one was open for 0% of the time, Pallas kernels for 18%

profile of v8, /device:TPU:8, one launch (start us, length us, event | category | flops | bytes accessed | tf_op | source)
XLA Modules:
  0.0 72.7 jit_solution(3757975123495346602)
XLA Ops:
  0.6 1.6 %prologue.1 = (bf16[64,8192]{1,0:T(8,128)(2,1)S(1)}, bf16[16,32,128]{2,1,0:T(8,128)(2,1)S(1)}, bf16[16,32,128]{2,1,0:T(8,128)(2,1)S(1)}, bf16[16,32,128]{2,1,0:T(8,128)(2,1)S(1)}, bf16[16,32,128]{2,1,0:T(8,128)(2,1)S(1)}) custom-call(bf16[128,8192]{1,0:T(8,128)(2,1)} %bitcast.3, f32[2048,128]{1,0:T(8,128)} %refs_2_.3), custom_call_target="tpu_custom_call" | custom-call | flops 2097152 | bytes 2097152 | tf_op jit(solution)/shard_map/prologue/pallas_call | solution.py:69
  2.2 0.1 collective-permute-start
  2.3 1.7 %collective-permute-start.2 = (bf16[16,32,128]{2,1,0:T(8,128)(2,1)S(1)}, bf16[16,32,128]{2,1,0:T(8,128)(2,1)S(1)}, u32[]{:S(2)}, u32[]{:S(2)}) collective-permute-start(bf16[16,32,128]{2,1,0:T(8,128)(2,1)S(1)} %get-tuple-element.25), channel_id=1, source_target_pairs={{0,196},{1,197},{2,198},{3,199},{4,192},{5,193},{6,194},{7,195},{8... | collective-permute-start | bytes 393224 | tf_op jit(solution)/shard_map/ppermute | solution.py:89
  4.0 1.9 %collective-permute-start.3 = (bf16[16,32,128]{2,1,0:T(8,128)(2,1)S(1)}, bf16[16,32,128]{2,1,0:T(8,128)(2,1)S(1)}, u32[]{:S(2)}, u32[]{:S(2)}) collective-permute-start(bf16[16,32,128]{2,1,0:T(8,128)(2,1)S(1)} %get-tuple-element.26), channel_id=1, source_target_pairs={{0,128},{64,192},{128,0},{192,64},{1,129},{65,193},{129,1},{193,65... | collective-permute-start | bytes 393224 | tf_op jit(solution)/shard_map/ppermute | solution.py:84
  5.9 0.0 collective-permute-start.4
  5.9 0.0 collective-permute-done.refs_1_
  5.9 2.1 %partial_rows.1 = (bf16[32,8192]{1,0:T(8,128)(2,1)S(1)}, bf16[32,8192]{1,0:T(8,128)(2,1)S(1)}) custom-call(bf16[128,8192]{1,0:T(8,128)(2,1)} %bitcast.4, bf16[64,8192]{1,0:T(8,128)(2,1)S(1)} %collective-permute-done.refs_1_, bf16[128,8192]{1,0:T(8,128)(2,1)} %refs_1_.7), custom_call_target="tpu_custom_call" | custom-call | flops 2097152 | bytes 2097152 | tf_op jit(solution)/shard_map/partial_rows/pallas_call | solution.py:69
  8.1 1.3 %collective-permute-start.1 = (bf16[32,8192]{1,0:T(8,128)(2,1)S(1)}, bf16[32,8192]{1,0:T(8,128)(2,1)S(1)}, u32[]{:S(2)}, u32[]{:S(2)}) collective-permute-start(bf16[32,8192]{1,0:T(8,128)(2,1)S(1)} %get-tuple-element.23.refs_0_), channel_id=1, source_target_pairs={{0,128},{64,192},{128,0},{192,64},{1,129},{65,193},{129,1},{193,65... | collective-permute-start | bytes 1572872 | tf_op jit(solution)/shard_map/ppermute | solution.py:84
  9.4 0.0 collective-permute-done.2.refs_1_
  9.4 0.3 collective-permute-done.3.refs_2_
  9.7 0.0 collective-permute-done.4.refs_3_
  9.7 0.8 %in_order.1 = bf16[4,16,32,128]{3,2,1,0:T(8,128)(2,1)} custom-call(bf16[32,8192]{1,0:T(8,128)(2,1)S(1)} %get-tuple-element.23.refs_0_, bf16[16,32,128]{2,1,0:T(8,128)(2,1)S(1)} %collective-permute-done.2.refs_1_, bf16[16,32,128]{2,1,0:T(8,128)(2,1)S(1)} %collective-permute-done.3.refs_2_, bf16[16,32,128]{2,1,0:T(8,128)(2,1)S(1)} %collective-permute-done.4.refs_3_, ...), custom_call_target="tpu_custom_call" | custom-call | flops 17179869184 | bytes 17179869184 | tf_op jit(solution)/shard_map/in_order/pallas_call | solution.py:69
  10.5 12.9 %all-to-all-start = ((bf16[64,32,128]{2,1,0:T(8,128)(2,1)}), bf16[64,32,128]{2,1,0:T(8,128)(2,1)S(1)}, u32[]{:S(2)}, u32[]{:S(2)}) async-start(bf16[64,32,128]{2,1,0:T(8,128)(2,1)} %bitcast.1), calls=%async_computation | async-start | bytes 1048576 | tf_op jit(solution)/shard_map/all_to_all | solution.py:350
  23.4 0.0 collective-permute-done.1.refs_1_
  23.5 0.7 average_rows.1
  24.2 5.3 %collective-permute-start.10 = (bf16[16,32,128]{2,1,0:T(8,128)(2,1)S(1)}, bf16[16,32,128]{2,1,0:T(8,128)(2,1)S(1)}, u32[]{:S(2)}, u32[]{:S(2)}) collective-permute-start(bf16[16,32,128]{2,1,0:T(8,128)(2,1)S(1)} %get-tuple-element.36), channel_id=1, source_target_pairs={{0,16},{1,17},{2,18},{3,19},{4,20},{5,21},{6,22},{7,23},{8,24},{9,... | collective-permute-start | bytes 393224 | tf_op jit(solution)/shard_map/ppermute | solution.py:334
  29.5 3.7 %collective-permute-start.11 = (bf16[16,32,128]{2,1,0:T(8,128)(2,1)S(1)}, bf16[16,32,128]{2,1,0:T(8,128)(2,1)S(1)}, u32[]{:S(2)}, u32[]{:S(2)}) collective-permute-start(bf16[16,32,128]{2,1,0:T(8,128)(2,1)S(1)} %get-tuple-element.37), channel_id=1, source_target_pairs={{0,0},{1,1},{2,2},{3,3},{4,4},{5,5},{6,6},{7,7},{8,8},{9,9},{10,10... | collective-permute-start | bytes 393224 | tf_op jit(solution)/shard_map/ppermute | solution.py:334
  33.1 0.1 collective-permute-start.8
  33.2 5.2 %collective-permute-start.9 = (bf16[16,32,128]{2,1,0:T(8,128)(2,1)S(1)}, bf16[16,32,128]{2,1,0:T(8,128)(2,1)S(1)}, u32[]{:S(2)}, u32[]{:S(2)}) collective-permute-start(bf16[16,32,128]{2,1,0:T(8,128)(2,1)S(1)} %get-tuple-element.35), channel_id=1, source_target_pairs={{0,32},{1,33},{2,34},{3,35},{4,36},{5,37},{6,38},{7,39},{8,40},{9,... | collective-permute-start | bytes 393224 | tf_op jit(solution)/shard_map/ppermute | solution.py:334
  38.5 7.9 %all-to-all-done.refs_1_ = bf16[64,32,128]{2,1,0:T(8,128)(2,1)S(1)} async-done(((bf16[64,32,128]{2,1,0:T(8,128)(2,1)}), bf16[64,32,128]{2,1,0:T(8,128)(2,1)S(1)}, u32[]{:S(2)}, u32[]{:S(2)}) %all-to-all-start) | async-done | bytes 524320 | tf_op jit(solution)/shard_map/all_to_all | solution.py:350
  46.4 1.5 %change_rows.1.refs_2_ = bf16[32,8192]{1,0:T(8,128)(2,1)S(1)} custom-call(f32[32,8192]{1,0:T(8,128)S(1)} %get-tuple-element.24.refs_0_, bf16[64,32,128]{2,1,0:T(8,128)(2,1)S(1)} %all-to-all-done.refs_1_), custom_call_target="tpu_custom_call" | custom-call | flops 2097152 | bytes 2097152 | tf_op jit(solution)/shard_map/change_rows/pallas_call | solution.py:69
  47.9 0.1 collective-permute-start.5
  48.0 0.0 collective-permute-done.10.refs_2_
  48.0 1.3 %collective-permute-done.11.refs_3_ = bf16[16,32,128]{2,1,0:T(8,128)(2,1)S(1)} collective-permute-done((bf16[16,32,128]{2,1,0:T(8,128)(2,1)S(1)}, bf16[16,32,128]{2,1,0:T(8,128)(2,1)S(1)}, u32[]{:S(2)}, u32[]{:S(2)}) %collective-permute-start.11) | collective-permute-done | bytes 131104 | tf_op jit(solution)/shard_map/ppermute | solution.py:334
  49.3 1.8 %collective-permute-done.8.refs_0_ = bf16[16,32,128]{2,1,0:T(8,128)(2,1)S(1)} collective-permute-done((bf16[16,32,128]{2,1,0:T(8,128)(2,1)S(1)}, bf16[16,32,128]{2,1,0:T(8,128)(2,1)S(1)}, u32[]{:S(2)}, u32[]{:S(2)}) %collective-permute-start.8) | collective-permute-done | bytes 131104 | tf_op jit(solution)/shard_map/ppermute | solution.py:334
  51.2 0.8 %collective-permute-done.9.refs_1_ = bf16[16,32,128]{2,1,0:T(8,128)(2,1)S(1)} collective-permute-done((bf16[16,32,128]{2,1,0:T(8,128)(2,1)S(1)}, bf16[16,32,128]{2,1,0:T(8,128)(2,1)S(1)}, u32[]{:S(2)}, u32[]{:S(2)}) %collective-permute-start.9) | collective-permute-done | bytes 131104 | tf_op jit(solution)/shard_map/ppermute | solution.py:334
  51.9 0.8 %stack_pieces.1 = bf16[16,4,32,128]{3,2,1,0:T(8,128)(2,1)} custom-call(bf16[16,32,128]{2,1,0:T(8,128)(2,1)S(1)} %collective-permute-done.8.refs_0_, bf16[16,32,128]{2,1,0:T(8,128)(2,1)S(1)} %collective-permute-done.9.refs_1_, bf16[16,32,128]{2,1,0:T(8,128)(2,1)S(1)} %collective-permute-done.10.refs_2_, bf16[16,32,128]{2,1,0:T(8,128)(2,1)S(1)} %collective-permute-done.11.refs_3_), custom_call_target="tpu_custom_call" | custom-call | flops 2097152 | bytes 2097152 | tf_op jit(solution)/shard_map/stack_pieces/pallas_call | solution.py:69
  52.8 6.8 %all-to-all-start.1 = ((bf16[16,4,32,128]{3,2,1,0:T(8,128)(2,1)}), bf16[16,4,32,128]{3,2,1,0:T(8,128)(2,1)S(1)}, u32[]{:S(2)}, u32[]{:S(2)}) async-start(bf16[16,4,32,128]{3,2,1,0:T(8,128)(2,1)} %stack_pieces.1), calls=%async_computation.1 | async-start | bytes 1048576 | tf_op jit(solution)/shard_map/all_to_all | solution.py:355
  59.6 0.1 collective-permute-start.7
  59.7 0.0 collective-permute-done.5.refs_2_
  59.7 0.5 collective-permute-start.6
  60.2 1.4 %collective-permute-done.7.refs_3_ = bf16[32,8192]{1,0:T(8,128)(2,1)S(1)} collective-permute-done((bf16[32,8192]{1,0:T(8,128)(2,1)S(1)}, bf16[32,8192]{1,0:T(8,128)(2,1)S(1)}, u32[]{:S(2)}, u32[]{:S(2)}) %collective-permute-start.7) | collective-permute-done | bytes 524320 | tf_op jit(solution)/shard_map/ppermute | solution.py:84
  61.6 2.7 %outputs_of.3 = (bf16[128,8192]{1,0:T(8,128)(2,1)}, bf16[128,8192]{1,0:T(8,128)(2,1)}) custom-call(bf16[128,8192]{1,0:T(8,128)(2,1)} %bitcast.5, bf16[128,8192]{1,0:T(8,128)(2,1)} %refs_1_.7, bf16[32,8192]{1,0:T(8,128)(2,1)S(1)} %change_rows.1.refs_2_, bf16[32,8192]{1,0:T(8,128)(2,1)S(1)} %collective-permute-done.7.refs_3_), custom_call_target="tpu_custom_call" | custom-call | flops 2097152 | bytes 2097152 | tf_op jit(solution)/shard_map/outputs_of/pallas_call | solution.py:69
  64.4 2.2 %outputs_of.4 = (bf16[128,8192]{1,0:T(8,128)(2,1)}, bf16[128,8192]{1,0:T(8,128)(2,1)}) custom-call(bf16[128,8192]{1,0:T(8,128)(2,1)} %bitcast.6, bf16[128,8192]{1,0:T(8,128)(2,1)} %refs_1_.7, bf16[32,8192]{1,0:T(8,128)(2,1)S(1)} %collective-permute-done.5.refs_2_, ...), custom_call_target="tpu_custom_call", output_to_operand_aliasing={{0}: (3, {}), {1}: (4, {})} | custom-call | flops 2097152 | bytes 2097152 | tf_op jit(solution)/shard_map/outputs_of/pallas_call | solution.py:69
  66.6 0.0 collective-permute-done.6.refs_2_
  66.7 0.0 copy-start
  66.7 2.3 %outputs_of.5 = (bf16[128,8192]{1,0:T(8,128)(2,1)}, bf16[128,8192]{1,0:T(8,128)(2,1)}) custom-call(bf16[128,8192]{1,0:T(8,128)(2,1)} %bitcast.7, bf16[128,8192]{1,0:T(8,128)(2,1)} %refs_1_.7, bf16[32,8192]{1,0:T(8,128)(2,1)S(1)} %collective-permute-done.6.refs_2_, ...), custom_call_target="tpu_custom_call", output_to_operand_aliasing={{0}: (3, {}), {1}: (4, {})} | custom-call | flops 2097152 | bytes 2097152 | tf_op jit(solution)/shard_map/outputs_of/pallas_call | solution.py:69
  69.0 2.5 %all-to-all-done.1.refs_1_ = bf16[16,4,32,128]{3,2,1,0:T(8,128)(2,1)S(1)} async-done(((bf16[16,4,32,128]{3,2,1,0:T(8,128)(2,1)}), bf16[16,4,32,128]{3,2,1,0:T(8,128)(2,1)S(1)}, u32[]{:S(2)}, u32[]{:S(2)}) %all-to-all-start.1) | async-done | bytes 524320 | tf_op jit(solution)/shard_map/all_to_all | solution.py:355
  71.5 0.0 copy-done
  71.5 1.2 %new_momentum_of.1 = f32[2048,128]{1,0:T(8,128)} custom-call(bf16[128,8192]{1,0:T(8,128)(2,1)} %get-tuple-element.33.refs_0_, bf16[16,4,32,128]{3,2,1,0:T(8,128)(2,1)S(1)} %all-to-all-done.1.refs_1_, f32[2048,128]{1,0:T(8,128)S(1)} %copy-done), custom_call_target="tpu_custom_call" | custom-call | flops 2097152 | bytes 2097152 | tf_op jit(solution)/shard_map/new_momentum_of/pallas_call | solution.py:69
Async XLA Ops:
  2.2 3.7 %collective-permute-start = (bf16[64,8192]{1,0:T(8,128)(2,1)S(1)}, bf16[64,8192]{1,0:T(8,128)(2,1)S(1)}, u32[]{:S(2)}, u32[]{:S(2)}) collective-permute-start(bf16[64,8192]{1,0:T(8,128)(2,1)S(1)} %get-tuple-element.21), channel_id=1, source_target_pairs={{0,64},{64,0},{128,192},{192,128},{1,65},{65,1},{129,193},{193,129... | collective-permute-start | bytes 3145736 | tf_op jit(solution)/shard_map/ppermute | solution.py:84
  2.3 7.0 %collective-permute-start.2 = (bf16[16,32,128]{2,1,0:T(8,128)(2,1)S(1)}, bf16[16,32,128]{2,1,0:T(8,128)(2,1)S(1)}, u32[]{:S(2)}, u32[]{:S(2)}) collective-permute-start(bf16[16,32,128]{2,1,0:T(8,128)(2,1)S(1)} %get-tuple-element.25), channel_id=1, source_target_pairs={{0,196},{1,197},{2,198},{3,199},{4,192},{5,193},{6,194},{7,195},{8... | collective-permute-start | bytes 393224 | tf_op jit(solution)/shard_map/ppermute | solution.py:89
  4.0 5.6 %collective-permute-start.3 = (bf16[16,32,128]{2,1,0:T(8,128)(2,1)S(1)}, bf16[16,32,128]{2,1,0:T(8,128)(2,1)S(1)}, u32[]{:S(2)}, u32[]{:S(2)}) collective-permute-start(bf16[16,32,128]{2,1,0:T(8,128)(2,1)S(1)} %get-tuple-element.26), channel_id=1, source_target_pairs={{0,128},{64,192},{128,0},{192,64},{1,129},{65,193},{129,1},{193,65... | collective-permute-start | bytes 393224 | tf_op jit(solution)/shard_map/ppermute | solution.py:84
  5.9 3.7 %collective-permute-start.4 = (bf16[16,32,128]{2,1,0:T(8,128)(2,1)S(1)}, bf16[16,32,128]{2,1,0:T(8,128)(2,1)S(1)}, u32[]{:S(2)}, u32[]{:S(2)}) collective-permute-start(bf16[16,32,128]{2,1,0:T(8,128)(2,1)S(1)} %get-tuple-element.27), channel_id=1, source_target_pairs={{0,64},{64,0},{128,192},{192,128},{1,65},{65,1},{129,193},{193,129... | collective-permute-start | bytes 393224 | tf_op jit(solution)/shard_map/ppermute | solution.py:84
  8.1 15.4 %collective-permute-start.1 = (bf16[32,8192]{1,0:T(8,128)(2,1)S(1)}, bf16[32,8192]{1,0:T(8,128)(2,1)S(1)}, u32[]{:S(2)}, u32[]{:S(2)}) collective-permute-start(bf16[32,8192]{1,0:T(8,128)(2,1)S(1)} %get-tuple-element.23.refs_0_), channel_id=1, source_target_pairs={{0,128},{64,192},{128,0},{192,64},{1,129},{65,193},{129,1},{193,65... | collective-permute-start | bytes 1572872 | tf_op jit(solution)/shard_map/ppermute | solution.py:84
  10.5 35.9 %all-to-all-start = ((bf16[64,32,128]{2,1,0:T(8,128)(2,1)}), bf16[64,32,128]{2,1,0:T(8,128)(2,1)S(1)}, u32[]{:S(2)}, u32[]{:S(2)}) async-start(bf16[64,32,128]{2,1,0:T(8,128)(2,1)} %bitcast.1), calls=%async_computation | async-start | bytes 1048576 | tf_op jit(solution)/shard_map/all_to_all | solution.py:350
  24.2 23.8 %collective-permute-start.10 = (bf16[16,32,128]{2,1,0:T(8,128)(2,1)S(1)}, bf16[16,32,128]{2,1,0:T(8,128)(2,1)S(1)}, u32[]{:S(2)}, u32[]{:S(2)}) collective-permute-start(bf16[16,32,128]{2,1,0:T(8,128)(2,1)S(1)} %get-tuple-element.36), channel_id=1, source_target_pairs={{0,16},{1,17},{2,18},{3,19},{4,20},{5,21},{6,22},{7,23},{8,24},{9,... | collective-permute-start | bytes 393224 | tf_op jit(solution)/shard_map/ppermute | solution.py:334
  29.5 19.9 %collective-permute-start.11 = (bf16[16,32,128]{2,1,0:T(8,128)(2,1)S(1)}, bf16[16,32,128]{2,1,0:T(8,128)(2,1)S(1)}, u32[]{:S(2)}, u32[]{:S(2)}) collective-permute-start(bf16[16,32,128]{2,1,0:T(8,128)(2,1)S(1)} %get-tuple-element.37), channel_id=1, source_target_pairs={{0,0},{1,1},{2,2},{3,3},{4,4},{5,5},{6,6},{7,7},{8,8},{9,9},{10,10... | collective-permute-start | bytes 393224 | tf_op jit(solution)/shard_map/ppermute | solution.py:334
  33.1 18.0 %collective-permute-start.8 = (bf16[16,32,128]{2,1,0:T(8,128)(2,1)S(1)}, bf16[16,32,128]{2,1,0:T(8,128)(2,1)S(1)}, u32[]{:S(2)}, u32[]{:S(2)}) collective-permute-start(bf16[16,32,128]{2,1,0:T(8,128)(2,1)S(1)} %get-tuple-element.34), channel_id=1, source_target_pairs={{0,48},{1,49},{2,50},{3,51},{4,52},{5,53},{6,54},{7,55},{8,56},{9,... | collective-permute-start | bytes 393224 | tf_op jit(solution)/shard_map/ppermute | solution.py:334
  33.2 18.7 %collective-permute-start.9 = (bf16[16,32,128]{2,1,0:T(8,128)(2,1)S(1)}, bf16[16,32,128]{2,1,0:T(8,128)(2,1)S(1)}, u32[]{:S(2)}, u32[]{:S(2)}) collective-permute-start(bf16[16,32,128]{2,1,0:T(8,128)(2,1)S(1)} %get-tuple-element.35), channel_id=1, source_target_pairs={{0,32},{1,33},{2,34},{3,35},{4,36},{5,37},{6,38},{7,39},{8,40},{9,... | collective-permute-start | bytes 393224 | tf_op jit(solution)/shard_map/ppermute | solution.py:334
  47.9 11.9 %collective-permute-start.5 = (bf16[32,8192]{1,0:T(8,128)(2,1)S(1)}, bf16[32,8192]{1,0:T(8,128)(2,1)S(1)}, u32[]{:S(2)}, u32[]{:S(2)}) collective-permute-start(bf16[32,8192]{1,0:T(8,128)(2,1)S(1)} %change_rows.1.refs_2_), channel_id=1, source_target_pairs={{0,128},{64,192},{128,0},{192,64},{1,129},{65,193},{129,1},{193,65... | collective-permute-start | bytes 1572872 | tf_op jit(solution)/shard_map/ppermute | solution.py:84
  52.8 18.7 %all-to-all-start.1 = ((bf16[16,4,32,128]{3,2,1,0:T(8,128)(2,1)}), bf16[16,4,32,128]{3,2,1,0:T(8,128)(2,1)S(1)}, u32[]{:S(2)}, u32[]{:S(2)}) async-start(bf16[16,4,32,128]{3,2,1,0:T(8,128)(2,1)} %stack_pieces.1), calls=%async_computation.1 | async-start | bytes 1048576 | tf_op jit(solution)/shard_map/all_to_all | solution.py:355
  59.6 2.0 %collective-permute-start.7 = (bf16[32,8192]{1,0:T(8,128)(2,1)S(1)}, bf16[32,8192]{1,0:T(8,128)(2,1)S(1)}, u32[]{:S(2)}, u32[]{:S(2)}) collective-permute-start(bf16[32,8192]{1,0:T(8,128)(2,1)S(1)} %change_rows.1.refs_2_), channel_id=1, source_target_pairs={{0,64},{64,0},{128,192},{192,128},{1,65},{65,1},{129,193},{193,129... | collective-permute-start | bytes 1572872 | tf_op jit(solution)/shard_map/ppermute | solution.py:84
  59.7 6.9 %collective-permute-start.6 = (bf16[32,8192]{1,0:T(8,128)(2,1)S(1)}, bf16[32,8192]{1,0:T(8,128)(2,1)S(1)}, u32[]{:S(2)}, u32[]{:S(2)}) collective-permute-start(bf16[32,8192]{1,0:T(8,128)(2,1)S(1)} %collective-permute-done.5.refs_2_), channel_id=1, source_target_pairs={{0,64},{64,0},{128,192},{192,128},{1,65},{65,1},{129,193},{193,129... | collective-permute-start | bytes 1572872 | tf_op jit(solution)/shard_map/ppermute | solution.py:84
  66.7 4.9 %copy-start = (f32[2048,128]{1,0:T(8,128)S(1)}, f32[2048,128]{1,0:T(8,128)}, u32[]{:S(2)}) copy-start(f32[2048,128]{1,0:T(8,128)} %refs_2_.3) | copy-start | bytes 3145732

commit v9 on v8

--- a/solution.py
+++ b/solution.py
@@ -193,8 +193,8 @@
             def step(i, carry, k=k):
                 cols = at(i * INNER, INNER)
                 y = (x[k, :, cols].astype(F32) + q[k, :, cols].astype(F32)) * 0.25
-                avg[k, :, cols] = y
                 narrow = y.astype(BF)
+                avg[k, :, cols] = narrow
                 for n in range(INNER // 128):
                     outs[k][i * (INNER // 128) + n] = narrow[:, n * 128 : (n + 1) * 128]
                 return carry
@@ -204,9 +204,9 @@
         copies.finish()
 
     return call(
-        body, "average_rows", LONG, [shape(32, 8192, dtype=F32)] + [shape(16, 32, 128)] * 4,
+        body, "average_rows", LONG, [shape(32, 8192)] + [shape(16, 32, 128)] * 4,
         [own, partial],
-        [shape(4, 32, WIDTH)] * 2 + [shape(4, 32, WIDTH, dtype=F32)], 12, out_near=True, far=1,
+        [shape(4, 32, WIDTH)] * 3, 12, out_near=True, far=1,
     )
 
 
@@ -238,7 +238,7 @@
 
             def step(n, carry, p=p):
                 cols = at(n * 128, 128)
-                x = avg[p, :, cols]
+                x = avg[p, :, cols].astype(F32)
                 momentum = outer_beta * m[p, peer(n, flip)].astype(F32) + x
                 o[p, :, cols] = (outer_rate * (x + outer_beta * momentum)).astype(BF)
                 return carry
@@ -249,7 +249,7 @@
 
     return call(
         body, "change_rows", SHORT, shape(32, 8192), [average, m_rows],
-        [shape(PARTS, 32, WIDTH, dtype=F32), shape(4, 16, 32, 128), shape(PARTS, 32, WIDTH)],
+        [shape(PARTS, 32, WIDTH), shape(4, 16, 32, 128), shape(PARTS, 32, WIDTH)],
         3 * PARTS,
     )
 

time: 73.1 us -> 73.1 us (level)
  transfers between devices with their start and end apart: 14 -> 14, of which waited for: 7 -> 7; matrix products, arithmetic and copies ran while one was open for 0% -> 0% of each run, Pallas kernels for 18% -> 19%
where the time goes in v9:
time: 73.1 us; the launch traced here: 72.7 us
  starting transfers between devices  39.7 us (54%)
  Pallas kernels  16.3 us (22%)
  waiting for transfers between devices  15.9 us (22%)
  between operations  0.8 us (1%)
    pallas_call x10, Pallas kernels, call(): pl.pallas_call(lambda *refs: body(Place(), *refs), out_shape=outs, in_spe...  16.3 us
    ppermute x4, starting transfers between devices, across(): return lax.ppermute(x, ('replica', 'fsdp'), pairs)  14.3 us
    all_to_all x1, starting transfers between devices, local(): m_rows = lax.all_to_all(by_row, 'fsdp', 0, 0, tiled=True)  12.9 us
    all_to_all x1, waiting for transfers between devices, local(): m_rows = lax.all_to_all(by_row, 'fsdp', 0, 0, tiled=True)  7.81 us
    all_to_all x1, starting transfers between devices, local(): lax.all_to_all(cut, 'fsdp', 0, 0, axis_index_groups=groups, tiled=True)  6.84 us
    ppermute x7, starting transfers between devices, swap(): return lax.ppermute(x, 'replica', [(i, i ^ k) for i in range(4)])  3.98 us
    ppermute x4, waiting for transfers between devices, across(): return lax.ppermute(x, ('replica', 'fsdp'), pairs)  3.85 us
    all_to_all x1, waiting for transfers between devices, local(): lax.all_to_all(cut, 'fsdp', 0, 0, axis_index_groups=groups, tiled=True)  2.57 us
  transfers between devices with their start and end apart: 14, of which 7 were waited for; matrix products, arithmetic and copies ran while one was open for 0% of the time, Pallas kernels for 19%

profile of v9, /device:TPU:8, one launch (start us, length us, event | category | flops | bytes accessed | tf_op | source)
XLA Modules:
  0.0 72.7 jit_solution(3040956830246159410)
XLA Ops:
  0.6 1.6 %prologue.1 = (bf16[64,8192]{1,0:T(8,128)(2,1)S(1)}, bf16[16,32,128]{2,1,0:T(8,128)(2,1)S(1)}, bf16[16,32,128]{2,1,0:T(8,128)(2,1)S(1)}, bf16[16,32,128]{2,1,0:T(8,128)(2,1)S(1)}, bf16[16,32,128]{2,1,0:T(8,128)(2,1)S(1)}) custom-call(bf16[128,8192]{1,0:T(8,128)(2,1)} %bitcast.3, f32[2048,128]{1,0:T(8,128)} %refs_2_.3), custom_call_target="tpu_custom_call" | custom-call | flops 2097152 | bytes 2097152 | tf_op jit(solution)/shard_map/prologue/pallas_call | solution.py:69
  2.2 0.1 collective-permute-start
  2.3 1.7 %collective-permute-start.2 = (bf16[16,32,128]{2,1,0:T(8,128)(2,1)S(1)}, bf16[16,32,128]{2,1,0:T(8,128)(2,1)S(1)}, u32[]{:S(2)}, u32[]{:S(2)}) collective-permute-start(bf16[16,32,128]{2,1,0:T(8,128)(2,1)S(1)} %get-tuple-element.25), channel_id=1, source_target_pairs={{0,196},{1,197},{2,198},{3,199},{4,192},{5,193},{6,194},{7,195},{8... | collective-permute-start | bytes 393224 | tf_op jit(solution)/shard_map/ppermute | solution.py:89
  4.0 1.9 %collective-permute-start.3 = (bf16[16,32,128]{2,1,0:T(8,128)(2,1)S(1)}, bf16[16,32,128]{2,1,0:T(8,128)(2,1)S(1)}, u32[]{:S(2)}, u32[]{:S(2)}) collective-permute-start(bf16[16,32,128]{2,1,0:T(8,128)(2,1)S(1)} %get-tuple-element.26), channel_id=1, source_target_pairs={{0,128},{64,192},{128,0},{192,64},{1,129},{65,193},{129,1},{193,65... | collective-permute-start | bytes 393224 | tf_op jit(solution)/shard_map/ppermute | solution.py:84
  5.9 0.0 collective-permute-start.4
  5.9 0.0 collective-permute-done.refs_1_
  5.9 2.1 %partial_rows.1 = (bf16[32,8192]{1,0:T(8,128)(2,1)S(1)}, bf16[32,8192]{1,0:T(8,128)(2,1)S(1)}) custom-call(bf16[128,8192]{1,0:T(8,128)(2,1)} %bitcast.4, bf16[64,8192]{1,0:T(8,128)(2,1)S(1)} %collective-permute-done.refs_1_, bf16[128,8192]{1,0:T(8,128)(2,1)} %refs_1_.7), custom_call_target="tpu_custom_call" | custom-call | flops 2097152 | bytes 2097152 | tf_op jit(solution)/shard_map/partial_rows/pallas_call | solution.py:69
  8.1 1.3 %collective-permute-start.1 = (bf16[32,8192]{1,0:T(8,128)(2,1)S(1)}, bf16[32,8192]{1,0:T(8,128)(2,1)S(1)}, u32[]{:S(2)}, u32[]{:S(2)}) collective-permute-start(bf16[32,8192]{1,0:T(8,128)(2,1)S(1)} %get-tuple-element.23.refs_0_), channel_id=1, source_target_pairs={{0,128},{64,192},{128,0},{192,64},{1,129},{65,193},{129,1},{193,65... | collective-permute-start | bytes 1572872 | tf_op jit(solution)/shard_map/ppermute | solution.py:84
  9.4 0.0 collective-permute-done.2.refs_1_
  9.4 0.3 collective-permute-done.3.refs_2_
  9.7 0.0 collective-permute-done.4.refs_3_
  9.7 0.8 %in_order.1 = bf16[4,16,32,128]{3,2,1,0:T(8,128)(2,1)} custom-call(bf16[32,8192]{1,0:T(8,128)(2,1)S(1)} %get-tuple-element.23.refs_0_, bf16[16,32,128]{2,1,0:T(8,128)(2,1)S(1)} %collective-permute-done.2.refs_1_, bf16[16,32,128]{2,1,0:T(8,128)(2,1)S(1)} %collective-permute-done.3.refs_2_, bf16[16,32,128]{2,1,0:T(8,128)(2,1)S(1)} %collective-permute-done.4.refs_3_, ...), custom_call_target="tpu_custom_call" | custom-call | flops 17179869184 | bytes 17179869184 | tf_op jit(solution)/shard_map/in_order/pallas_call | solution.py:69
  10.5 12.9 %all-to-all-start = ((bf16[64,32,128]{2,1,0:T(8,128)(2,1)}), bf16[64,32,128]{2,1,0:T(8,128)(2,1)S(1)}, u32[]{:S(2)}, u32[]{:S(2)}) async-start(bf16[64,32,128]{2,1,0:T(8,128)(2,1)} %bitcast.1), calls=%async_computation | async-start | bytes 1048576 | tf_op jit(solution)/shard_map/all_to_all | solution.py:350
  23.4 0.0 collective-permute-done.1.refs_1_
  23.5 0.9 %average_rows.1 = (bf16[32,8192]{1,0:T(8,128)(2,1)S(1)}, bf16[16,32,128]{2,1,0:T(8,128)(2,1)S(1)}, bf16[16,32,128]{2,1,0:T(8,128)(2,1)S(1)}, bf16[16,32,128]{2,1,0:T(8,128)(2,1)S(1)}, bf16[16,32,128]{2,1,0:T(8,128)(2,1)S(1)}) custom-call(bf16[32,8192]{1,0:T(8,128)(2,1)S(1)} %get-tuple-element.22.refs_0_, bf16[32,8192]{1,0:T(8,128)(2,1)S(1)} %collective-permute-done.1.refs_1_), custom_call_target="tpu_custom_call" | custom-call | flops 17179869184 | bytes 17179869184 | tf_op jit(solution)/shard_map/average_rows/pallas_call | solution.py:69
  24.3 5.3 %collective-permute-start.10 = (bf16[16,32,128]{2,1,0:T(8,128)(2,1)S(1)}, bf16[16,32,128]{2,1,0:T(8,128)(2,1)S(1)}, u32[]{:S(2)}, u32[]{:S(2)}) collective-permute-start(bf16[16,32,128]{2,1,0:T(8,128)(2,1)S(1)} %get-tuple-element.36), channel_id=1, source_target_pairs={{0,16},{1,17},{2,18},{3,19},{4,20},{5,21},{6,22},{7,23},{8,24},{9,... | collective-permute-start | bytes 393224 | tf_op jit(solution)/shard_map/ppermute | solution.py:334
  29.6 3.7 %collective-permute-start.11 = (bf16[16,32,128]{2,1,0:T(8,128)(2,1)S(1)}, bf16[16,32,128]{2,1,0:T(8,128)(2,1)S(1)}, u32[]{:S(2)}, u32[]{:S(2)}) collective-permute-start(bf16[16,32,128]{2,1,0:T(8,128)(2,1)S(1)} %get-tuple-element.37), channel_id=1, source_target_pairs={{0,0},{1,1},{2,2},{3,3},{4,4},{5,5},{6,6},{7,7},{8,8},{9,9},{10,10... | collective-permute-start | bytes 393224 | tf_op jit(solution)/shard_map/ppermute | solution.py:334
  33.3 0.1 collective-permute-start.8
  33.4 5.2 %collective-permute-start.9 = (bf16[16,32,128]{2,1,0:T(8,128)(2,1)S(1)}, bf16[16,32,128]{2,1,0:T(8,128)(2,1)S(1)}, u32[]{:S(2)}, u32[]{:S(2)}) collective-permute-start(bf16[16,32,128]{2,1,0:T(8,128)(2,1)S(1)} %get-tuple-element.35), channel_id=1, source_target_pairs={{0,32},{1,33},{2,34},{3,35},{4,36},{5,37},{6,38},{7,39},{8,40},{9,... | collective-permute-start | bytes 393224 | tf_op jit(solution)/shard_map/ppermute | solution.py:334
  38.6 7.8 %all-to-all-done.refs_1_ = bf16[64,32,128]{2,1,0:T(8,128)(2,1)S(1)} async-done(((bf16[64,32,128]{2,1,0:T(8,128)(2,1)}), bf16[64,32,128]{2,1,0:T(8,128)(2,1)S(1)}, u32[]{:S(2)}, u32[]{:S(2)}) %all-to-all-start) | async-done | bytes 524320 | tf_op jit(solution)/shard_map/all_to_all | solution.py:350
  46.4 1.6 %change_rows.1.refs_2_ = bf16[32,8192]{1,0:T(8,128)(2,1)S(1)} custom-call(bf16[32,8192]{1,0:T(8,128)(2,1)S(1)} %get-tuple-element.24.refs_0_, bf16[64,32,128]{2,1,0:T(8,128)(2,1)S(1)} %all-to-all-done.refs_1_), custom_call_target="tpu_custom_call" | custom-call | flops 2097152 | bytes 2097152 | tf_op jit(solution)/shard_map/change_rows/pallas_call | solution.py:69
  48.0 0.1 collective-permute-start.5
  48.1 0.0 collective-permute-done.10.refs_2_
  48.1 1.0 %collective-permute-done.11.refs_3_ = bf16[16,32,128]{2,1,0:T(8,128)(2,1)S(1)} collective-permute-done((bf16[16,32,128]{2,1,0:T(8,128)(2,1)S(1)}, bf16[16,32,128]{2,1,0:T(8,128)(2,1)S(1)}, u32[]{:S(2)}, u32[]{:S(2)}) %collective-permute-start.11) | collective-permute-done | bytes 131104 | tf_op jit(solution)/shard_map/ppermute | solution.py:334
  49.1 1.9 %collective-permute-done.8.refs_0_ = bf16[16,32,128]{2,1,0:T(8,128)(2,1)S(1)} collective-permute-done((bf16[16,32,128]{2,1,0:T(8,128)(2,1)S(1)}, bf16[16,32,128]{2,1,0:T(8,128)(2,1)S(1)}, u32[]{:S(2)}, u32[]{:S(2)}) %collective-permute-start.8) | collective-permute-done | bytes 131104 | tf_op jit(solution)/shard_map/ppermute | solution.py:334
  51.0 1.0 %collective-permute-done.9.refs_1_ = bf16[16,32,128]{2,1,0:T(8,128)(2,1)S(1)} collective-permute-done((bf16[16,32,128]{2,1,0:T(8,128)(2,1)S(1)}, bf16[16,32,128]{2,1,0:T(8,128)(2,1)S(1)}, u32[]{:S(2)}, u32[]{:S(2)}) %collective-permute-start.9) | collective-permute-done | bytes 131104 | tf_op jit(solution)/shard_map/ppermute | solution.py:334
  51.9 0.8 %stack_pieces.1 = bf16[16,4,32,128]{3,2,1,0:T(8,128)(2,1)} custom-call(bf16[16,32,128]{2,1,0:T(8,128)(2,1)S(1)} %collective-permute-done.8.refs_0_, bf16[16,32,128]{2,1,0:T(8,128)(2,1)S(1)} %collective-permute-done.9.refs_1_, bf16[16,32,128]{2,1,0:T(8,128)(2,1)S(1)} %collective-permute-done.10.refs_2_, bf16[16,32,128]{2,1,0:T(8,128)(2,1)S(1)} %collective-permute-done.11.refs_3_), custom_call_target="tpu_custom_call" | custom-call | flops 2097152 | bytes 2097152 | tf_op jit(solution)/shard_map/stack_pieces/pallas_call | solution.py:69
  52.8 6.8 %all-to-all-start.1 = ((bf16[16,4,32,128]{3,2,1,0:T(8,128)(2,1)}), bf16[16,4,32,128]{3,2,1,0:T(8,128)(2,1)S(1)}, u32[]{:S(2)}, u32[]{:S(2)}) async-start(bf16[16,4,32,128]{3,2,1,0:T(8,128)(2,1)} %stack_pieces.1), calls=%async_computation.1 | async-start | bytes 1048576 | tf_op jit(solution)/shard_map/all_to_all | solution.py:355
  59.6 0.1 collective-permute-start.7
  59.7 0.0 collective-permute-done.5.refs_2_
  59.7 0.5 collective-permute-start.6
  60.2 1.4 %collective-permute-done.7.refs_3_ = bf16[32,8192]{1,0:T(8,128)(2,1)S(1)} collective-permute-done((bf16[32,8192]{1,0:T(8,128)(2,1)S(1)}, bf16[32,8192]{1,0:T(8,128)(2,1)S(1)}, u32[]{:S(2)}, u32[]{:S(2)}) %collective-permute-start.7) | collective-permute-done | bytes 524320 | tf_op jit(solution)/shard_map/ppermute | solution.py:84
  61.6 2.7 %outputs_of.3 = (bf16[128,8192]{1,0:T(8,128)(2,1)}, bf16[128,8192]{1,0:T(8,128)(2,1)}) custom-call(bf16[128,8192]{1,0:T(8,128)(2,1)} %bitcast.5, bf16[128,8192]{1,0:T(8,128)(2,1)} %refs_1_.7, bf16[32,8192]{1,0:T(8,128)(2,1)S(1)} %change_rows.1.refs_2_, bf16[32,8192]{1,0:T(8,128)(2,1)S(1)} %collective-permute-done.7.refs_3_), custom_call_target="tpu_custom_call" | custom-call | flops 2097152 | bytes 2097152 | tf_op jit(solution)/shard_map/outputs_of/pallas_call | solution.py:69
  64.4 2.2 %outputs_of.4 = (bf16[128,8192]{1,0:T(8,128)(2,1)}, bf16[128,8192]{1,0:T(8,128)(2,1)}) custom-call(bf16[128,8192]{1,0:T(8,128)(2,1)} %bitcast.6, bf16[128,8192]{1,0:T(8,128)(2,1)} %refs_1_.7, bf16[32,8192]{1,0:T(8,128)(2,1)S(1)} %collective-permute-done.5.refs_2_, ...), custom_call_target="tpu_custom_call", output_to_operand_aliasing={{0}: (3, {}), {1}: (4, {})} | custom-call | flops 2097152 | bytes 2097152 | tf_op jit(solution)/shard_map/outputs_of/pallas_call | solution.py:69
  66.6 0.0 collective-permute-done.6.refs_2_
  66.7 0.0 copy-start
  66.7 2.3 %outputs_of.5 = (bf16[128,8192]{1,0:T(8,128)(2,1)}, bf16[128,8192]{1,0:T(8,128)(2,1)}) custom-call(bf16[128,8192]{1,0:T(8,128)(2,1)} %bitcast.7, bf16[128,8192]{1,0:T(8,128)(2,1)} %refs_1_.7, bf16[32,8192]{1,0:T(8,128)(2,1)S(1)} %collective-permute-done.6.refs_2_, ...), custom_call_target="tpu_custom_call", output_to_operand_aliasing={{0}: (3, {}), {1}: (4, {})} | custom-call | flops 2097152 | bytes 2097152 | tf_op jit(solution)/shard_map/outputs_of/pallas_call | solution.py:69
  69.0 2.6 %all-to-all-done.1.refs_1_ = bf16[16,4,32,128]{3,2,1,0:T(8,128)(2,1)S(1)} async-done(((bf16[16,4,32,128]{3,2,1,0:T(8,128)(2,1)}), bf16[16,4,32,128]{3,2,1,0:T(8,128)(2,1)S(1)}, u32[]{:S(2)}, u32[]{:S(2)}) %all-to-all-start.1) | async-done | bytes 524320 | tf_op jit(solution)/shard_map/all_to_all | solution.py:355
  71.5 0.0 copy-done
  71.5 1.2 %new_momentum_of.1 = f32[2048,128]{1,0:T(8,128)} custom-call(bf16[128,8192]{1,0:T(8,128)(2,1)} %get-tuple-element.33.refs_0_, bf16[16,4,32,128]{3,2,1,0:T(8,128)(2,1)S(1)} %all-to-all-done.1.refs_1_, f32[2048,128]{1,0:T(8,128)S(1)} %copy-done), custom_call_target="tpu_custom_call" | custom-call | flops 2097152 | bytes 2097152 | tf_op jit(solution)/shard_map/new_momentum_of/pallas_call | solution.py:69
Async XLA Ops:
  2.2 3.7 %collective-permute-start = (bf16[64,8192]{1,0:T(8,128)(2,1)S(1)}, bf16[64,8192]{1,0:T(8,128)(2,1)S(1)}, u32[]{:S(2)}, u32[]{:S(2)}) collective-permute-start(bf16[64,8192]{1,0:T(8,128)(2,1)S(1)} %get-tuple-element.21), channel_id=1, source_target_pairs={{0,64},{64,0},{128,192},{192,128},{1,65},{65,1},{129,193},{193,129... | collective-permute-start | bytes 3145736 | tf_op jit(solution)/shard_map/ppermute | solution.py:84
  2.3 7.0 %collective-permute-start.2 = (bf16[16,32,128]{2,1,0:T(8,128)(2,1)S(1)}, bf16[16,32,128]{2,1,0:T(8,128)(2,1)S(1)}, u32[]{:S(2)}, u32[]{:S(2)}) collective-permute-start(bf16[16,32,128]{2,1,0:T(8,128)(2,1)S(1)} %get-tuple-element.25), channel_id=1, source_target_pairs={{0,196},{1,197},{2,198},{3,199},{4,192},{5,193},{6,194},{7,195},{8... | collective-permute-start | bytes 393224 | tf_op jit(solution)/shard_map/ppermute | solution.py:89
  4.0 5.6 %collective-permute-start.3 = (bf16[16,32,128]{2,1,0:T(8,128)(2,1)S(1)}, bf16[16,32,128]{2,1,0:T(8,128)(2,1)S(1)}, u32[]{:S(2)}, u32[]{:S(2)}) collective-permute-start(bf16[16,32,128]{2,1,0:T(8,128)(2,1)S(1)} %get-tuple-element.26), channel_id=1, source_target_pairs={{0,128},{64,192},{128,0},{192,64},{1,129},{65,193},{129,1},{193,65... | collective-permute-start | bytes 393224 | tf_op jit(solution)/shard_map/ppermute | solution.py:84
  5.9 3.7 %collective-permute-start.4 = (bf16[16,32,128]{2,1,0:T(8,128)(2,1)S(1)}, bf16[16,32,128]{2,1,0:T(8,128)(2,1)S(1)}, u32[]{:S(2)}, u32[]{:S(2)}) collective-permute-start(bf16[16,32,128]{2,1,0:T(8,128)(2,1)S(1)} %get-tuple-element.27), channel_id=1, source_target_pairs={{0,64},{64,0},{128,192},{192,128},{1,65},{65,1},{129,193},{193,129... | collective-permute-start | bytes 393224 | tf_op jit(solution)/shard_map/ppermute | solution.py:84
  8.1 15.4 %collective-permute-start.1 = (bf16[32,8192]{1,0:T(8,128)(2,1)S(1)}, bf16[32,8192]{1,0:T(8,128)(2,1)S(1)}, u32[]{:S(2)}, u32[]{:S(2)}) collective-permute-start(bf16[32,8192]{1,0:T(8,128)(2,1)S(1)} %get-tuple-element.23.refs_0_), channel_id=1, source_target_pairs={{0,128},{64,192},{128,0},{192,64},{1,129},{65,193},{129,1},{193,65... | collective-permute-start | bytes 1572872 | tf_op jit(solution)/shard_map/ppermute | solution.py:84
  10.5 35.9 %all-to-all-start = ((bf16[64,32,128]{2,1,0:T(8,128)(2,1)}), bf16[64,32,128]{2,1,0:T(8,128)(2,1)S(1)}, u32[]{:S(2)}, u32[]{:S(2)}) async-start(bf16[64,32,128]{2,1,0:T(8,128)(2,1)} %bitcast.1), calls=%async_computation | async-start | bytes 1048576 | tf_op jit(solution)/shard_map/all_to_all | solution.py:350
  24.3 23.8 %collective-permute-start.10 = (bf16[16,32,128]{2,1,0:T(8,128)(2,1)S(1)}, bf16[16,32,128]{2,1,0:T(8,128)(2,1)S(1)}, u32[]{:S(2)}, u32[]{:S(2)}) collective-permute-start(bf16[16,32,128]{2,1,0:T(8,128)(2,1)S(1)} %get-tuple-element.36), channel_id=1, source_target_pairs={{0,16},{1,17},{2,18},{3,19},{4,20},{5,21},{6,22},{7,23},{8,24},{9,... | collective-permute-start | bytes 393224 | tf_op jit(solution)/shard_map/ppermute | solution.py:334
  29.6 19.5 %collective-permute-start.11 = (bf16[16,32,128]{2,1,0:T(8,128)(2,1)S(1)}, bf16[16,32,128]{2,1,0:T(8,128)(2,1)S(1)}, u32[]{:S(2)}, u32[]{:S(2)}) collective-permute-start(bf16[16,32,128]{2,1,0:T(8,128)(2,1)S(1)} %get-tuple-element.37), channel_id=1, source_target_pairs={{0,0},{1,1},{2,2},{3,3},{4,4},{5,5},{6,6},{7,7},{8,8},{9,9},{10,10... | collective-permute-start | bytes 393224 | tf_op jit(solution)/shard_map/ppermute | solution.py:334
  33.3 17.7 %collective-permute-start.8 = (bf16[16,32,128]{2,1,0:T(8,128)(2,1)S(1)}, bf16[16,32,128]{2,1,0:T(8,128)(2,1)S(1)}, u32[]{:S(2)}, u32[]{:S(2)}) collective-permute-start(bf16[16,32,128]{2,1,0:T(8,128)(2,1)S(1)} %get-tuple-element.34), channel_id=1, source_target_pairs={{0,48},{1,49},{2,50},{3,51},{4,52},{5,53},{6,54},{7,55},{8,56},{9,... | collective-permute-start | bytes 393224 | tf_op jit(solution)/shard_map/ppermute | solution.py:334
  33.4 18.6 %collective-permute-start.9 = (bf16[16,32,128]{2,1,0:T(8,128)(2,1)S(1)}, bf16[16,32,128]{2,1,0:T(8,128)(2,1)S(1)}, u32[]{:S(2)}, u32[]{:S(2)}) collective-permute-start(bf16[16,32,128]{2,1,0:T(8,128)(2,1)S(1)} %get-tuple-element.35), channel_id=1, source_target_pairs={{0,32},{1,33},{2,34},{3,35},{4,36},{5,37},{6,38},{7,39},{8,40},{9,... | collective-permute-start | bytes 393224 | tf_op jit(solution)/shard_map/ppermute | solution.py:334
  48.0 11.8 %collective-permute-start.5 = (bf16[32,8192]{1,0:T(8,128)(2,1)S(1)}, bf16[32,8192]{1,0:T(8,128)(2,1)S(1)}, u32[]{:S(2)}, u32[]{:S(2)}) collective-permute-start(bf16[32,8192]{1,0:T(8,128)(2,1)S(1)} %change_rows.1.refs_2_), channel_id=1, source_target_pairs={{0,128},{64,192},{128,0},{192,64},{1,129},{65,193},{129,1},{193,65... | collective-permute-start | bytes 1572872 | tf_op jit(solution)/shard_map/ppermute | solution.py:84
  52.8 18.8 %all-to-all-start.1 = ((bf16[16,4,32,128]{3,2,1,0:T(8,128)(2,1)}), bf16[16,4,32,128]{3,2,1,0:T(8,128)(2,1)S(1)}, u32[]{:S(2)}, u32[]{:S(2)}) async-start(bf16[16,4,32,128]{3,2,1,0:T(8,128)(2,1)} %stack_pieces.1), calls=%async_computation.1 | async-start | bytes 1048576 | tf_op jit(solution)/shard_map/all_to_all | solution.py:355
  59.6 2.0 %collective-permute-start.7 = (bf16[32,8192]{1,0:T(8,128)(2,1)S(1)}, bf16[32,8192]{1,0:T(8,128)(2,1)S(1)}, u32[]{:S(2)}, u32[]{:S(2)}) collective-permute-start(bf16[32,8192]{1,0:T(8,128)(2,1)S(1)} %change_rows.1.refs_2_), channel_id=1, source_target_pairs={{0,64},{64,0},{128,192},{192,128},{1,65},{65,1},{129,193},{193,129... | collective-permute-start | bytes 1572872 | tf_op jit(solution)/shard_map/ppermute | solution.py:84
  59.7 6.9 %collective-permute-start.6 = (bf16[32,8192]{1,0:T(8,128)(2,1)S(1)}, bf16[32,8192]{1,0:T(8,128)(2,1)S(1)}, u32[]{:S(2)}, u32[]{:S(2)}) collective-permute-start(bf16[32,8192]{1,0:T(8,128)(2,1)S(1)} %collective-permute-done.5.refs_2_), channel_id=1, source_target_pairs={{0,64},{64,0},{128,192},{192,128},{1,65},{65,1},{129,193},{193,129... | collective-permute-start | bytes 1572872 | tf_op jit(solution)/shard_map/ppermute | solution.py:84
  66.7 4.9 %copy-start = (f32[2048,128]{1,0:T(8,128)S(1)}, f32[2048,128]{1,0:T(8,128)}, u32[]{:S(2)}) copy-start(f32[2048,128]{1,0:T(8,128)} %refs_2_.3) | copy-start | bytes 3145732
